TPU v7x, 32 devices: a whole 2x2x4 slice. The times are simulated.
32 devices in a mesh: gx: 4 (over y, core), gy: 8 (over z, x).
Axes of the slice: x: 2, y: 2, z: 4, core: 2. Of those that a mesh axis runs over, the one named last changes fastest.
Arguments:
- beta: float32 [16, 32, 1024], P(None, 'gx', 'gy'), may hold values from -6 to 6
- design: float32 [16, 16], replicated, may hold values from -1.5 to 1.5
- prior: float32 [16], replicated, may hold values from 0.25 to 4
- kept: int32 [16, 32, 1024], P(None, 'gx', 'gy'), may hold values from 1 to 40
- removed: int32 [16, 32, 1024], P(None, 'gx', 'gy'), may hold values from 0 to 8
- removed_labels: int32 [16, 32, 1024], P(None, 'gx', 'gy'), may hold values from 0 to 8, as said below
Outputs:
- newton_step: float32 [16, 32, 1024], P(None, 'gx', 'gy')
Inputs may be any that keep to these rules, and one draw needn't show every extreme that they name: `removed_labels`: each entry is at most the entry of removed at the same place.
All inputs are finite; a program needn't handle non-finite values.
Results may differ from a plain program's by a relative error of at most 0.00022.
Values sent between devices are 32-bit elements; how exact they have to be, the bound alone decides.
No kernel may reach another device: no remote copies, remote signals or barrier semaphores. Data moves between devices by JAX's collectives and lax.ppermute only.
A program may use at most 64 MiB of HBM per device.

v0:
```python
import jax
import jax.numpy as jnp
from jax import lax
from jax.sharding import PartitionSpec as P

ITERS = 4
SWEEPS = 2
LEVELS = 4
COARSE_SWEEPS = 4


damping = 0.7
highest = lax.Precision.HIGHEST


def extended(block, sides, width):
    for axis, dim in sides:
        count = lax.axis_size(axis)
        forward = [(i, i + 1) for i in range(count - 1)]
        backward = [(target, source) for source, target in forward]
        low = lax.ppermute(
            lax.slice_in_dim(block, block.shape[dim] - width, None, axis=dim), axis, forward
        )
        high = lax.ppermute(lax.slice_in_dim(block, 0, width, axis=dim), axis, backward)
        block = jnp.concatenate([low, block, high], axis=dim)
    return block


def gauss_jordan(blocks):
    size = blocks.shape[0]
    for pivot_at in range(size):
        pivots = blocks[pivot_at, pivot_at]
        scaled = blocks[pivot_at].at[pivot_at].set(1.0) / pivots[None]
        factors = blocks[:, pivot_at]
        blocks = blocks.at[:, pivot_at].set(0.0) - factors[:, None] * scaled[None]
        blocks = blocks.at[pivot_at].set(scaled)
    return blocks


def apply_inverse(inverse, vector):
    return jnp.einsum("klxy,lxy->kxy", inverse, vector, precision=highest)


def operate(field, padded, design, weights, prior, scale):
    inner = jnp.einsum("jk,kxy->jxy", design, field, precision=highest)
    data_term = jnp.einsum("jk,jxy->kxy", design, weights * inner, precision=highest)
    beside = padded[:, 2:, 1:-1] + padded[:, :-2, 1:-1] + padded[:, 1:-1, 2:] + padded[:, 1:-1, :-2]
    return data_term + scale * prior[:, None, None] * (4.0 * field - beside)


def restrict(field):
    chans, rows, cols = field.shape
    return field.reshape(chans, rows // 2, 2, cols // 2, 2).sum(axis=(2, 4))


def prolong(field):
    return jnp.repeat(jnp.repeat(field, 2, axis=1), 2, axis=2)


def build_inverse(design, weights, prior, scale):
    outer = design[:, :, None] * design[:, None, :]
    blocks = jnp.einsum("jkl,jxy->klxy", outer, weights, precision=highest)
    blocks = blocks + (4.0 * scale * jnp.diag(prior))[:, :, None, None]
    return gauss_jordan(blocks)


def fine_pad(field):
    return extended(field, (("gx", 1), ("gy", 2)), 1)


def coarse_pad(field):
    return extended(field, (("gx", 1), ("gy", 2)), 1)


def smooth(field, rhs, padder, design, weights, inverse, prior, scale):
    leftover = rhs - operate(field, padder(field), design, weights, prior, scale)
    return field + damping * apply_inverse(inverse, leftover)


def sweeps(rhs, count, padder, design, weights, inverse, prior, scale):
    field = damping * apply_inverse(inverse, rhs)
    for sweep in range(count - 1):
        field = smooth(field, rhs, padder, design, weights, inverse, prior, scale)
    return field


def multigrid(rhs, level, tables, design, prior):
    weights, inverse = tables[level]
    scale = 2.0**level
    if level == len(tables) - 1:
        return sweeps(rhs, COARSE_SWEEPS, coarse_pad, design, weights, inverse, prior, scale)
    field = sweeps(rhs, SWEEPS, fine_pad, design, weights, inverse, prior, scale)
    leftover = rhs - operate(field, fine_pad(field), design, weights, prior, scale)
    field = field + prolong(multigrid(restrict(leftover), level + 1, tables, design, prior))
    for sweep in range(SWEEPS):
        field = smooth(field, rhs, fine_pad, design, weights, inverse, prior, scale)
    return field


def residual_product(residual, precond):
    return lax.psum(jnp.sum(residual * precond), ("gx", "gy"))


def local(beta, design, prior, kept, removed, removed_labels):
    logits = jnp.einsum("jk,kxy->jxy", design, beta, precision=highest)
    prob = 1.0 / (1.0 + jnp.exp(-logits))
    weights = kept.astype(jnp.float32) * prob * (1.0 - prob)
    source = removed.astype(jnp.float32) * prob - removed_labels.astype(jnp.float32)
    rhs = jnp.einsum("jk,jxy->kxy", design, source, precision=highest)
    tables = []
    for level in range(LEVELS):
        if level > 0:
            weights = restrict(weights)
        tables.append((weights, build_inverse(design, weights, prior, 2.0**level)))
    fine_weights = tables[0][0]

    def precondition(residual):
        return multigrid(residual, 0, tables, design, prior)

    newton_step = jnp.zeros_like(rhs)
    residual = rhs
    precond = precondition(residual)
    direction = precond
    gamma = residual_product(residual, precond)
    for step in range(ITERS):
        image = operate(direction, fine_pad(direction), design, fine_weights, prior, 1.0)
        alpha = gamma / lax.psum(jnp.sum(direction * image), ("gx", "gy"))
        newton_step = newton_step + alpha * direction
        residual = residual - alpha * image
        if step + 1 < ITERS:
            precond = precondition(residual)
            gamma_next = residual_product(residual, precond)
            direction = precond + gamma_next / gamma * direction
            gamma = gamma_next
    return newton_step


def solution(mesh):
    placed = (
        P(None, "gx", "gy"),
        P(),
        P(),
        P(None, "gx", "gy"),
        P(None, "gx", "gy"),
        P(None, "gx", "gy"),
    )
    return jax.shard_map(
        local, mesh=mesh, in_specs=placed, out_specs=P(None, "gx", "gy"), check_vma=False
    )
```

profile of v0, /device:TPU:0, one launch (start us, length us, event | category | flops | bytes accessed | tf_op | source)
XLA Modules:
  0.0 1592.0 jit_solution(2845961422161020345)
XLA Ops:
  287.9 5.8 collective-permute-start.15
  304.3 5.8 collective-permute-start.19
  320.3 5.8 collective-permute-start.23
  448.3 5.8 collective-permute-start.55
  490.3 49.0 %all-reduce = (f32[]{:T(128)}, f32[]{:T(128)}) all-reduce(f32[]{:T(128)} %get-tuple-element.2310, f32[]{:T(128)} %get-tuple-element.2309), channel_id=1, replica_groups=mesh['gx'=4,'gy'=8] {'gx','gy'}, use_global_device_ids=true, to_apply=%region_11.12 | all-reduce | flops 2 | bytes 16 | tf_op jit(solution)/shard_map/psum | solution.py:101
  594.2 5.8 collective-permute-start.79
  610.6 5.8 collective-permute-start.83
  626.5 5.8 collective-permute-start.87
  754.5 5.8 collective-permute-start.119
  771.5 5.8 collective-permute-start.123
  780.1 49.0 %psum.58 = f32[]{:T(128)} all-reduce(f32[]{:T(128)} %multiply_reduce_fusion.52), channel_id=1, replica_groups=mesh['gx'=4,'gy'=8] {'gx','gy'}, use_global_device_ids=true, to_apply=%region_19.20 | all-reduce | flops 1 | bytes 8 | tf_op jit(solution)/shard_map/psum | solution.py:101
  846.0 43.2 %psum.59 = f32[]{:T(128)} all-reduce(f32[]{:T(128)} %get-tuple-element.2556), channel_id=1, replica_groups=mesh['gx'=4,'gy'=8] {'gx','gy'}, use_global_device_ids=true, to_apply=%region_21.22 | all-reduce | flops 1 | bytes 8 | tf_op jit(solution)/shard_map/psum | solution.py:127
  944.6 5.8 collective-permute-start.143
  961.1 5.8 collective-permute-start.147
  977.0 5.8 collective-permute-start.151
  1105.0 5.9 collective-permute-start.183
  1130.6 48.9 %psum.60 = f32[]{:T(128)} all-reduce(f32[]{:T(128)} %multiply_reduce_fusion.50), channel_id=1, replica_groups=mesh['gx'=4,'gy'=8] {'gx','gy'}, use_global_device_ids=true, to_apply=%region_27.28 | all-reduce | flops 1 | bytes 8 | tf_op jit(solution)/shard_map/psum | solution.py:101
  1196.2 43.2 %psum.61 = f32[]{:T(128)} all-reduce(f32[]{:T(128)} %get-tuple-element.2558), channel_id=1, replica_groups=mesh['gx'=4,'gy'=8] {'gx','gy'}, use_global_device_ids=true, to_apply=%region_29.30 | all-reduce | flops 1 | bytes 8 | tf_op jit(solution)/shard_map/psum | solution.py:127
  1294.8 5.8 collective-permute-start.207
  1327.2 5.8 collective-permute-start.215
  1438.6 6.0 collective-permute-start.243
  1455.2 5.8 collective-permute-start.247
  1480.8 49.0 %psum.62 = f32[]{:T(128)} all-reduce(f32[]{:T(128)} %multiply_reduce_fusion.48), channel_id=1, replica_groups=mesh['gx'=4,'gy'=8] {'gx','gy'}, use_global_device_ids=true, to_apply=%region_35.36 | all-reduce | flops 1 | bytes 8 | tf_op jit(solution)/shard_map/psum | solution.py:101
  1546.6 43.2 %psum.63 = f32[]{:T(128)} all-reduce(f32[]{:T(128)} %fusion.74), channel_id=1, replica_groups=mesh['gx'=4,'gy'=8] {'gx','gy'}, use_global_device_ids=true, to_apply=%region_37.38 | all-reduce | flops 1 | bytes 8 | tf_op jit(solution)/shard_map/psum | solution.py:127
  (1570 shorter events, 1151.8 us)
Async XLA Ops:
  85.0 154.9 %collective-permute-start = (f32[16,1,128]{2,0,1:T(8,128)S(1)}, f32[16,1,128]{2,0,1:T(8,128)S(1)}, u32[]{:S(2)}, u32[]{:S(2)}) collective-permute-start(f32[16,1,128]{2,0,1:T(8,128)S(1)} %get-tuple-element.2394), channel_id=1, source_target_pairs={{8,0},{16,8},{24,16},{9,1},{17,9},{25,17},{10,2},{18,10},{26,18},{... | collective-permute-start | bytes 24584 | tf_op jit(solution)/shard_map/ppermute | solution.py:24
  86.3 153.6 %collective-permute-start.1 = (f32[16,1,128]{2,0,1:T(8,128)S(1)}, f32[16,1,128]{2,0,1:T(8,128)S(1)}, u32[]{:S(2)}, u32[]{:S(2)}) collective-permute-start(f32[16,1,128]{2,0,1:T(8,128)S(1)} %get-tuple-element.2393), channel_id=1, source_target_pairs={{0,8},{8,16},{16,24},{1,9},{9,17},{17,25},{2,10},{10,18},{18,26},{... | collective-permute-start | bytes 24584 | tf_op jit(solution)/shard_map/ppermute | solution.py:21
  241.3 9.0 collective-permute-start.3
  257.3 8.6 collective-permute-start.7
  287.9 7.6 collective-permute-start.15
  447.0 7.6 collective-permute-start.54
  448.3 7.8 collective-permute-start.55
  547.5 8.2 collective-permute-start.67
  562.7 8.3 collective-permute-start.71
  594.2 7.6 collective-permute-start.79
  753.2 7.6 collective-permute-start.118
  754.5 7.8 collective-permute-start.119
  837.0 8.1 collective-permute-start.127
  897.3 8.3 collective-permute-start.131
  944.6 7.6 collective-permute-start.143
  1088.3 7.5 collective-permute-start.179
  1103.7 7.6 collective-permute-start.182
  1105.0 7.8 collective-permute-start.183
  1187.3 8.1 collective-permute-start.191
  1247.6 8.3 collective-permute-start.195
  1294.8 7.6 collective-permute-start.207
  1453.9 7.6 collective-permute-start.246
  1455.2 7.8 collective-permute-start.247
  1537.6 8.1 collective-permute-start.255
  (238 other events, 1467.7 us)
where the time goes:
time: 1620 us; the launch traced here: 1590 us
  starting transfers between devices  804 us (50%)
  blocking collectives  325 us (20%)
  waiting for transfers between devices  159 us (10%)
  local copies, waits for them, and re-layouts  149 us (9%)
  other arithmetic  104 us (6%)
  matrix products  33.5 us (2%)
    ppermute x128, starting transfers between devices, extended(): lax.ppermute(lax.slice_in_dim(block, block.shape[dim] - width, None, axis...  639 us
    psum x4, blocking collectives, residual_product(): return lax.psum(jnp.sum(residual * precond), ('gx', 'gy'))  196 us
    ppermute x128, starting transfers between devices, extended(): lax.ppermute(lax.slice_in_dim(block, 0, width, axis=dim), axis, backward)  165 us
    ppermute x128, waiting for transfers between devices, extended(): lax.ppermute(lax.slice_in_dim(block, block.shape[dim] - width, None, axis...  153 us
    psum x3, blocking collectives, local(): alpha = gamma / lax.psum(jnp.sum(direction * image), ('gx', 'gy'))  130 us
    scatter x64, local copies, waits for them, and re-layouts, gauss_jordan(): scaled = blocks[pivot_at].at[pivot_at].set(1.0) / pivots[None]  75.5 us
    scatter x64, other arithmetic, gauss_jordan(): blocks = blocks.at[pivot_at].set(scaled)  42.9 us
    squeeze x64, local copies, waits for them, and re-layouts, gauss_jordan(): scaled = blocks[pivot_at].at[pivot_at].set(1.0) / pivots[None]  34.6 us
  transfers between devices with their start and end apart: 256, of which 146 were waited for; matrix products, arithmetic and copies ran while one was open for 10% of the time, Pallas kernels for 0%

commit v1 on v0

v1 whole, which is shorter than its diff:
```python
import functools

import jax
import jax.numpy as jnp
from jax import lax
from jax.experimental import pallas as pl
from jax.experimental.pallas import tpu as pltpu
from jax.sharding import PartitionSpec as P

ITERS = 4
LEVELS = 4
COARSE_SWEEPS = 4
K = 16
BLOCK = 8
SEGMENT = 32
HALO = 8
OWN = 16
DAMPING = 0.7

highest = lax.Precision.HIGHEST
f32 = jnp.float32

SIDES = [BLOCK >> m for m in range(LEVELS)]
COUNTS = [n * n for n in SIDES]
OFFSETS = [sum(COUNTS[:m]) for m in range(LEVELS)]
SLOTS = -(-sum(COUNTS) // 8) * 8
SPLITS = ((0, 0), (0, 1), (0, 2), (1, 0), (1, 1), (2, 0))

VMEM = pl.BlockSpec(memory_space=pltpu.VMEM)
SMEM = pl.BlockSpec(memory_space=pltpu.SMEM)


def params(mib):
    return pltpu.CompilerParams(vmem_limit_bytes=mib << 20)


def lanes_of(shape):
    return lax.broadcasted_iota(jnp.int32, shape, len(shape) - 1)


def roll(x, shift):
    shift = shift % x.shape[-1]
    return x if shift == 0 else pltpu.roll(x, shift, x.ndim - 1)


def lane_order():
    row = lax.broadcasted_iota(jnp.int32, (128, 128), 0)
    lane = lax.broadcasted_iota(jnp.int32, (128, 128), 1)
    return (lane == (row % BLOCK) * OWN + row // BLOCK).astype(f32)


def prepare_kernel(place, design, beta, kept, removed, labels, own, edge_a, edge_b, tile):
    probs = []
    for j in range(K):
        logit = sum(design[j, k] * beta[k] for k in range(K))
        prob = 1.0 / (1.0 + jnp.exp(-logit))
        probs.append(removed[j].astype(f32) * prob - labels[j].astype(f32))
        tile[pl.ds(j * BLOCK, BLOCK), :] = kept[j].astype(f32) * prob * (1.0 - prob)
    for k in range(K):
        tile[pl.ds((K + k) * BLOCK, BLOCK), :] = sum(design[j, k] * probs[j] for j in range(K))
    tile[...] = jnp.dot(tile[...], lane_order(), precision=highest, preferred_element_type=f32)
    even = place[1] % 2 == 0
    low = lanes_of((K, 128)) % OWN < HALO
    for f in range(2):
        rows = [tile[pl.ds(f * K * BLOCK + t, K, stride=BLOCK), :] for t in range(BLOCK)]
        for t in range(BLOCK):
            own[f, t] = rows[t]
        for i in range(BLOCK // 2):
            left = jnp.where(low, rows[2 * i], roll(rows[2 * i + 1], HALO))
            right = jnp.where(low, roll(rows[2 * i], -HALO), rows[2 * i + 1])
            edge_a[f, i] = jnp.where(even, right, left)
            edge_b[f, i] = jnp.where(even, left, right)


def symmetric_inverse(a, n):
    a = dict(a)
    for p in range(n):
        d = 1.0 / a[p, p]
        col = {i: a[max(i, p), min(i, p)] for i in range(n) if i != p}
        fac = {i: col[i] * d for i in col}
        for i in col:
            for j in col:
                if j <= i:
                    a[i, j] = a[i, j] - fac[i] * col[j]
        for i in col:
            a[max(i, p), min(i, p)] = fac[i]
        a[p, p] = -d
    return {ij: -x for ij, x in a.items()}


def setup_kernel(place, prior, outer, g_own, g_edge, blocks, inverse, rhs, weights, pieces, coarse_blocks, work):
    width = rhs.shape[-1]
    groups = width // 128
    lane = lanes_of((K, 128))
    left_at = (place[1] + 1) % 2
    right_at = 1 - left_at
    for f, target in ((0, weights), (1, rhs)):
        for group in range(groups):
            for t in range(BLOCK):
                for s in range(BLOCK):
                    value = jnp.zeros((K, 128), f32)
                    for p in range(4):
                        at = group * 4 + p
                        base = p * SEGMENT
                        odd = (t % 2) * HALO
                        mid = roll(g_own[at, f, t], base + HALO - s * OWN)
                        low = roll(g_edge[at, left_at, f, t // 2], base - s * OWN - odd)
                        high = roll(g_edge[at, right_at, f, t // 2], base + SEGMENT - HALO - s * OWN - odd)
                        value = jnp.where((lane >= base) & (lane < base + HALO), low, value)
                        value = jnp.where((lane >= base + HALO) & (lane < base + HALO + OWN), mid, value)
                        value = jnp.where((lane >= base + HALO + OWN) & (lane < base + SEGMENT), high, value)
                    target[s * BLOCK + t, :, pl.ds(group * 128, 128)] = value
    for m in range(1, LEVELS):
        n, fine, coarse = SIDES[m], OFFSETS[m - 1], OFFSETS[m]
        for s in range(n):
            for t in range(n):
                corner = fine + (2 * s) * (2 * n) + 2 * t
                weights[coarse + s * n + t] = (
                    weights[corner] + weights[corner + 1] + weights[corner + 2 * n] + weights[corner + 2 * n + 1]
                )
    for slot in range(sum(COUNTS), SLOTS):
        weights[slot] = jnp.zeros((K, width), f32)

    def split(slot, carry):
        for group in range(groups):
            rest = weights[slot, :, pl.ds(group * 128, 128)]
            parts = []
            for _ in range(3):
                part = rest.astype(jnp.bfloat16)
                parts.append(part)
                rest = rest - part.astype(f32)
            for i, (_, b) in enumerate(SPLITS):
                pieces[group, slot, pl.ds(i * K, K), :] = parts[b]
        return carry

    lax.fori_loop(0, SLOTS, split, 0)

    tables = ((blocks, 0, COUNTS[0]), (coarse_blocks, COUNTS[0], SLOTS - COUNTS[0]))
    for table, first, count in tables:

        def multiply(step, carry, table=table, first=first):
            for group in range(groups):
                for i in range(4):
                    slot = step * 4 + i
                    table[group, slot] = jnp.dot(
                        outer[...], pieces[group, first + slot], preferred_element_type=f32
                    )
            return carry

        lax.fori_loop(0, count // 4, multiply, 0)

    flat_inverse = inverse.reshape(groups * SLOTS * K * K, 128)
    column = lanes_of((8, 128)) % SEGMENT
    inside = ((place[1] > 0) | (column >= HALO)) & ((place[1] < place[2] - 1) | (column < HALO + OWN))
    damped = jnp.where(inside, DAMPING, 0.0).astype(f32)
    half = K // 2

    for group, (table, offset, count) in ((x, y) for x in range(groups) for y in tables):
        flat_blocks = table.reshape(groups * count * K * K, 128)

        def invert(g, carry, group=group, flat_blocks=flat_blocks, offset=offset, count=count):
            slot = offset + g * 8 + lax.broadcasted_iota(jnp.int32, (8, 128), 0)
            scale = jnp.where(
                slot < OFFSETS[1], 4.0, jnp.where(slot < OFFSETS[2], 8.0, jnp.where(slot < OFFSETS[3], 16.0, 32.0))
            ).astype(f32)
            source = (group * count + g * 8) * (K * K)
            target = (group * SLOTS + offset + g * 8) * (K * K)

            def load(k, l):
                value = flat_blocks[pl.ds(source + l * K + k, 8, stride=K * K), :]
                return value + scale * prior[k] if k == l else value

            def store(k, l, value):
                value = value * damped
                flat_inverse[pl.ds(target + l * K + k, 8, stride=K * K), :] = value
                if k != l:
                    flat_inverse[pl.ds(target + k * K + l, 8, stride=K * K), :] = value

            first = symmetric_inverse({(i, j): load(i, j) for i in range(half) for j in range(i + 1)}, half)
            for i in range(half):
                for j in range(half):
                    work[0, i * half + j] = load(half + j, i)
            for j in range(half):
                b = [work[0, i * half + j] for i in range(half)]
                for i in range(half):
                    work[1, i * half + j] = sum(first[max(i, h), min(i, h)] * b[h] for h in range(half))
            schur = {(i, j): load(half + i, half + j) for i in range(half) for j in range(i + 1)}
            for h in range(half):
                b = [work[0, h * half + j] for j in range(half)]
                y = [work[1, h * half + j] for j in range(half)]
                for i in range(half):
                    for j in range(i + 1):
                        schur[i, j] = schur[i, j] - b[i] * y[j]
            second = symmetric_inverse(schur, half)
            for (i, j), value in second.items():
                store(half + i, half + j, value)
            for i in range(half):
                y = [work[1, i * half + j] for j in range(half)]
                for j in range(half):
                    z = sum(y[h] * second[max(h, j), min(h, j)] for h in range(half))
                    work[0, i * half + j] = z
                    store(half + j, i, -z)
            for h in range(half):
                z = [work[0, i * half + h] for i in range(half)]
                y = [work[1, i * half + h] for i in range(half)]
                for i in range(half):
                    for j in range(i + 1):
                        first[i, j] = first[i, j] + z[i] * y[j]
            for (i, j), value in first.items():
                store(i, j, value)
            return carry

        lax.fori_loop(0, count // 8, invert, 0)


def beside(read, m, s, t, above, below):
    n = SIDES[m]
    total = read(s - 1, t) if s > 0 else roll(read(n - 1, t), 1)
    total = total + (read(s + 1, t) if s < n - 1 else roll(read(0, t), -1))
    total = total + (read(s, t - 1) if t > 0 else jnp.where(above, roll(read(s, n - 1), SEGMENT), 0.0))
    return total + (read(s, t + 1) if t < n - 1 else jnp.where(below, roll(read(s, 0), -SEGMENT), 0.0))


def block_product(table, first, count, source, finish):
    def one(i, carry):
        for group in range(table.shape[0]):
            cols = pl.ds(group * 128, 128)
            total = None
            for l in range(K):
                term = table[group, first + i, pl.ds(l * K, K), :] * source[i, pl.ds(l, 1), cols]
                total = term if total is None else total + term
            finish(i, cols, total)
        return carry

    lax.fori_loop(0, count, one, 0, unroll=min(count, 8))


def v_cycle(inverse, prior, b, v, d, w):
    width = b[0].shape[-1]
    lane = lanes_of((K, width))
    above, below = lane >= SEGMENT, lane < width - SEGMENT
    weight = [jnp.broadcast_to(prior[...] * 2.0**m, (K, width)) for m in range(LEVELS)]

    def sweep(m, keep=None):
        n = SIDES[m]
        for s in range(n):
            for t in range(n):
                near = beside(lambda x, y: v[m][x * n + y], m, s, t, above, below)
                w[m][s * n + t] = b[m][s * n + t] + weight[m] * near

        def finish(i, cols, total):
            old = v[m][i, :, cols]
            v[m][i, :, cols] = 0.3 * old + total
            if keep is not None:
                keep[i, :, cols] = total - 0.4 * old

        block_product(inverse, OFFSETS[m], COUNTS[m], w[m], finish)

    def begin(m):
        def finish(i, cols, total):
            v[m][i, :, cols] = total

        block_product(inverse, OFFSETS[m], COUNTS[m], b[m], finish)

    for m in range(LEVELS - 1):
        n = SIDES[m]
        begin(m)
        sweep(m, d[m])
        for s in range(0, n, 2):
            for t in range(0, n, 2):
                near, own = None, None
                for x, y in ((s, t), (s, t + 1), (s + 1, t), (s + 1, t + 1)):
                    one = beside(lambda x, y: d[m][x * n + y], m, x, y, above, below)
                    near = one if near is None else near + one
                    one = b[m][x * n + y]
                    own = one if own is None else own + one
                b[m + 1][(s // 2) * (n // 2) + t // 2] = 0.09 * own + weight[m] * near
    begin(LEVELS - 1)
    for _ in range(COARSE_SWEEPS - 1):
        sweep(LEVELS - 1)
    for m in range(LEVELS - 2, -1, -1):
        n = SIDES[m]
        for s in range(n):
            for t in range(n):
                v[m][s * n + t] = v[m][s * n + t] + v[m + 1][(s // 2) * (n // 2) + t // 2]
        sweep(m)
        sweep(m)


def iterate_kernel(step, last, *refs):
    refs = list(refs)
    place, prior, blocks, inverse, residual_in = (refs.pop(0) for _ in range(5))
    if step > 0:
        sums, edge_a, edge_b, z_in, az_in = (refs.pop(0) for _ in range(5))
    if step > 1:
        old, x_in, p_in, ap_in = (refs.pop(0) for _ in range(4))
    z_out, az_out, parts = (refs.pop(0) for _ in range(3))
    if not last:
        send_a, send_b = (refs.pop(0) for _ in range(2))
    if step > 0:
        scalars, residual, x, p, ap = (refs.pop(0) for _ in range(5))
    b, v, d, w = (refs[i * LEVELS : (i + 1) * LEVELS] for i in range(4))
    width = z_out.shape[-1]
    lane = lanes_of((K, width))
    column = lane % SEGMENT
    mine = (column >= HALO) & (column < HALO + OWN)
    even = place[1] % 2 == 0
    count = COUNTS[0]
    if step > 0:
        gamma, alpha, beta, energy = coefficients(sums, old if step > 1 else None)
        scalars[...] = jnp.concatenate(
            [jnp.broadcast_to(gamma, (1, 128)), jnp.broadcast_to(energy, (1, 128)), jnp.zeros((6, 128), f32)], axis=0
        )
        left_side, right_side = column < HALO, column >= HALO + OWN
        for i in range(count // 4):
            left = jnp.where(even, edge_b[i], edge_a[i])
            right = jnp.where(even, edge_a[i], edge_b[i])
            for g in range(4):
                at = 4 * i + g
                image = jnp.where(left_side, roll(left, -HALO * g), az_in[at])
                image = jnp.where(right_side, roll(right, SEGMENT - HALO - HALO * g), image)
                direction = z_in[at]
                if step > 1:
                    direction = direction + beta * p_in[at]
                    image = image + beta * ap_in[at]
                p[at] = direction
                ap[at] = image
                x[at] = x_in[at] + alpha * direction if step > 1 else alpha * direction
                left_over = residual_in[at] - alpha * image
                residual[at] = left_over
                b[0][at] = left_over
    else:
        for at in range(count):
            b[0][at] = residual_in[at]

    v_cycle(inverse, prior, b, v, d, w)

    above, below = lane >= SEGMENT, lane < width - SEGMENT
    weight = jnp.broadcast_to(prior[...], (K, width))
    n = SIDES[0]
    for s in range(n):
        for t in range(n):
            near = beside(lambda x, y: v[0][x * n + y], 0, s, t, above, below)
            w[0][s * n + t] = weight * (4.0 * v[0][s * n + t] - near)

    def finish(i, cols, total):
        az_out[i, :, cols] = total + w[0][i, :, cols]
        z_out[i, :, cols] = v[0][i, :, cols]

    block_product(blocks, 0, count, v[0], finish)

    names = 3 if step > 0 else 2
    totals = [jnp.zeros((K, width), f32) for _ in range(names)]
    for at in range(count):
        z = z_out[at]
        totals[0] = totals[0] + z * b[0][at]
        totals[1] = totals[1] + z * az_out[at]
        if step > 0:
            totals[2] = totals[2] + z * ap[at]
    rows = []
    for total in totals:
        total = jnp.sum(jnp.where(mine, total, 0.0), axis=0, keepdims=True)
        rows.append(sum(total[:, g * 128 : (g + 1) * 128] for g in range(width // 128)))
    rows.append(jnp.zeros((8 - names, 128), f32))
    tile = jnp.concatenate(rows, axis=0)
    for i in range(parts.shape[0]):
        parts[i] = tile
    if not last:
        for i in range(count // 4):
            left, right = None, None
            for g in range(4):
                value = az_out[4 * i + g]
                low, high = roll(value, HALO * g - HALO), roll(value, HALO * g - OWN)
                here = (column >= HALO * g) & (column < HALO * g + HALO)
                left = low if left is None else jnp.where(here, low, left)
                right = high if right is None else jnp.where(here, high, right)
            send_a[i] = jnp.where(even, right, left)
            send_b[i] = jnp.where(even, left, right)


def coefficients(sums, old):
    total = sums[0]
    for i in range(1, sums.shape[0]):
        total = total + sums[i]
    total = jnp.sum(total, axis=1, keepdims=True)
    gamma, energy = total[0:1], total[1:2]
    beta = None
    if old is not None:
        beta = gamma / old[0:1, 0:1]
        energy = energy + beta * (2.0 * total[2:3] + beta * old[1:2, 0:1])
    return gamma, gamma / energy, beta, energy


def finish_kernel(place, sums, old, x, p, z, out, tile):
    _, alpha, beta, _ = coefficients(sums, old)
    group = pl.ds(pl.multiple_of((place[0] // 4) * 128, 128), 128)
    base = (place[0] % 4) * SEGMENT + HALO
    lane = lanes_of((K, 128))
    for t in range(BLOCK):
        packed = None
        for s in range(BLOCK):
            at = s * BLOCK + t
            value = x[at, :, group] + alpha * (z[at, :, group] + beta * p[at, :, group])
            value = pltpu.roll(value, (128 + s * OWN - base) % 128, 1)
            packed = value if packed is None else jnp.where(lane >= s * OWN, value, packed)
        tile[pl.ds(t, K, stride=BLOCK), :] = packed
    back = lax.dot_general(
        tile[...], lane_order(), (((1,), (1,)), ((), ())), precision=highest, preferred_element_type=f32
    )
    out[...] = back.reshape(K, BLOCK, 128)


def local(beta, design, prior, kept, removed, removed_labels):
    rows, cols = lax.axis_size("gx"), lax.axis_size("gy")
    width = rows * SEGMENT
    place = jnp.stack([lax.axis_index("gx"), lax.axis_index("gy"), jnp.int32(cols)]).astype(jnp.int32)
    pairs = [(i, i ^ 1) for i in range(cols)]
    others = [(0, 0)] + [(i, ((i + 1) ^ 1) - 1) for i in range(1, cols - 1)] + [(cols - 1, cols - 1)]
    others = others[1:-1]

    def shape(*dims, dtype=f32):
        return jax.ShapeDtypeStruct(dims, dtype)

    own, edge_a, edge_b = pl.pallas_call(
        prepare_kernel,
        out_shape=[shape(2, 8, K, 128), shape(2, 4, K, 128), shape(2, 4, K, 128)],
        in_specs=[SMEM, SMEM] + [VMEM] * 4,
        out_specs=[VMEM] * 3,
        scratch_shapes=[pltpu.VMEM((2 * K * BLOCK, 128), f32)],
        name="prepare",
    )(place, design, beta, kept, removed, removed_labels)
    edge_a = lax.ppermute(edge_a, "gy", pairs)
    edge_b = lax.ppermute(edge_b, "gy", others)
    g_own = lax.all_gather(own, "gx")
    g_edge = lax.all_gather(jnp.stack([edge_a, edge_b]), "gx")

    products = (design[:, :, None] * design[:, None, :]).reshape(K, K * K).T
    parts, rest = [], products
    for _ in range(3):
        part = lax.reduce_precision(rest, 8, 7)
        parts.append(part)
        rest = rest - part
    outer = jnp.concatenate([parts[a] for a, _ in SPLITS], axis=1).astype(jnp.bfloat16)
    prior_rows = prior[:, None]

    field = shape(COUNTS[0], K, width)
    blocks, inverse, residual = pl.pallas_call(
        setup_kernel,
        out_shape=[shape(width // 128, n, K * K, 128) for n in (COUNTS[0], SLOTS)] + [field],
        in_specs=[SMEM, SMEM] + [VMEM] * 3,
        out_specs=[VMEM] * 3,
        scratch_shapes=[
            pltpu.VMEM((SLOTS, K, width), f32),
            pltpu.VMEM((width // 128, SLOTS, len(SPLITS) * K, 128), jnp.bfloat16),
            pltpu.VMEM((width // 128, SLOTS - COUNTS[0], K * K, 128), f32),
            pltpu.VMEM((2, K * K // 4, 8, 128), f32),
        ],
        compiler_params=params(24 if width == 128 else 60),
        name="setup",
    )(place, prior, outer, g_own, g_edge)

    levels = [pltpu.VMEM((n, K, width), f32) for n in COUNTS]
    state = ()
    for step in range(ITERS):
        last = step == ITERS - 1
        operands = (place, prior_rows, blocks, inverse, residual) + state
        shapes = [field, field, shape(cols, 8, 128)]
        if not last:
            shapes += [shape(COUNTS[0] // 4, K, width)] * 2
        if step > 0:
            shapes += [shape(8, 128), field, field, field, field]
        outs = pl.pallas_call(
            functools.partial(iterate_kernel, step, last),
            out_shape=shapes,
            in_specs=[SMEM] + [VMEM] * (len(operands) - 1),
            out_specs=[VMEM] * len(shapes),
            scratch_shapes=levels * 4,
            compiler_params=params(24 if width == 128 else 60),
            name=f"iterate_{step}",
        )(*operands)
        z, az, sums = outs[:3]
        outs = outs[3:]
        sums = lax.all_to_all(sums, "gy", 0, 0, tiled=True)
        if not last:
            edge_a = lax.ppermute(outs[0], "gy", pairs)
            edge_b = lax.ppermute(outs[1], "gy", others)
            outs = outs[2:]
        history = ()
        if step > 0:
            scalars, residual, x, p, ap = outs
            history = (scalars, x, p, ap)
        if not last:
            state = (sums, edge_a, edge_b, z, az) + history
    return pl.pallas_call(
        finish_kernel,
        out_shape=shape(*beta.shape),
        in_specs=[SMEM] + [VMEM] * 5,
        out_specs=VMEM,
        scratch_shapes=[pltpu.VMEM((K * BLOCK, 128), f32)],
        name="finish",
    )(place, sums, scalars, x, p, z)


def solution(mesh):
    placed = (
        P(None, "gx", "gy"),
        P(),
        P(),
        P(None, "gx", "gy"),
        P(None, "gx", "gy"),
        P(None, "gx", "gy"),
    )
    return jax.shard_map(
        local, mesh=mesh, in_specs=placed, out_specs=P(None, "gx", "gy"), check_vma=False
    )
```

time: 1620 us -> 144 us (0.09); the launches traced: 1590 us -> 143 us
  starting transfers between devices: 804 us -> 11 us
  blocking collectives: 325 us -> 61.5 us
  waiting for transfers between devices: 159 us -> 0.02 us
  local copies, waits for them, and re-layouts: 149 us -> 5.36 us
  other arithmetic: 104 us -> 0.67 us
  Pallas kernels: 0 us -> 64.4 us
  matrix products: 33.5 us -> 0 us
    ppermute x256 -> x8, starting transfers between devices: 804 us -> 11 us  [the longest x3 5.43 us: local(): edge_a = lax.ppermute(outs[0], 'gy', pairs)]
    psum x7 -> x0, blocking collectives: 325 us -> none  [the longest x4 196 us: residual_product(): return lax.psum(jnp.sum(residual * precond), ('gx', 'gy'))]
    ppermute x256 -> x8, waiting for transfers between devices: 159 us -> 0.02 us  [the longest x3 0.01 us: local(): edge_b = lax.ppermute(outs[1], 'gy', others)]
    scatter x129 -> x0, local copies, waits for them, and re-layouts: 101 us -> none  [the longest x64 75.5 us: gauss_jordan(): scaled = blocks[pivot_at].at[pivot_at].set(1.0) / pivots[None]]
    pallas_call x0 -> x7, Pallas kernels: none -> 64.4 us  [the longest x4 35.3 us: local(): pl.pallas_call(functools.partial(iterate_kernel, step, last), out_shape=s...]
    all_to_all x0 -> x4, blocking collectives: none -> 46.8 us  [local(): sums = lax.all_to_all(sums, 'gy', 0, 0, tiled=True)]
    scatter x64 -> x0, other arithmetic: 42.9 us -> none  [gauss_jordan(): blocks = blocks.at[pivot_at].set(scaled)]
    squeeze x64 -> x0, local copies, waits for them, and re-layouts: 34.6 us -> none  [gauss_jordan(): scaled = blocks[pivot_at].at[pivot_at].set(1.0) / pivots[None]]
  transfers between devices with their start and end apart: 256 -> 8, of which waited for: 146 -> 0; matrix products, arithmetic and copies ran while one was open for 10% -> 1% of each run, Pallas kernels for 0% -> 0%
where the time goes in v1:
time: 144 us; the launch traced here: 143 us
  Pallas kernels  64.4 us (45%)
  blocking collectives  61.5 us (43%)
  starting transfers between devices  11 us (8%)
  local copies, waits for them, and re-layouts  5.36 us (4%)
    all_to_all x4, blocking collectives, local(): sums = lax.all_to_all(sums, 'gy', 0, 0, tiled=True)  46.8 us
    pallas_call x4, Pallas kernels, local(): pl.pallas_call(functools.partial(iterate_kernel, step, last), out_shape=s...  35.3 us
    pallas_call x1, Pallas kernels, local(): pl.pallas_call(setup_kernel, out_shape=[shape(width // 128, n, K * K, 128...  24.3 us
    all_gather x1, blocking collectives, local(): g_own = lax.all_gather(own, 'gx')  7.41 us
    all_gather x1, blocking collectives, local(): g_edge = lax.all_gather(jnp.stack([edge_a, edge_b]), 'gx')  7.29 us
    ppermute x3, starting transfers between devices, local(): edge_a = lax.ppermute(outs[0], 'gy', pairs)  5.43 us
    unnamed x13, local copies, waits for them, and re-layouts  4.44 us
    ppermute x1, starting transfers between devices, local(): edge_a = lax.ppermute(edge_a, 'gy', pairs)  2.94 us
  transfers between devices with their start and end apart: 8, of which 0 were waited for; matrix products, arithmetic and copies ran while one was open for 1% of the time, Pallas kernels for 0%

profile of v1, /device:TPU:0, one launch (start us, length us, event | category | flops | bytes accessed | tf_op | source)
XLA Modules:
  0.0 143.1 jit_solution(9190275860002866118)
XLA Ops:
  0.6 2.2 %prepare.1 = (f32[2,8,16,128]{3,2,1,0:T(8,128)}, f32[2,4,16,128]{3,2,1,0:T(8,128)}, f32[2,4,16,128]{3,2,1,0:T(8,128)}) custom-call(s32[3]{0:T(128)} %pad_add_fusion.place.refs_0_, f32[16,16]{1,0:T(8,128)} %design.1, f32[16,8,128]{2,1,0:T(8,128)} %beta.1, s32[16,8,128]{2,1,0:T(8,128)} %kept.1, s32[16,8,128]{2,1,0:T(8,128)} %removed.1, s32[16,8,128]{2,1,0:T(8,128)} %labels.1), custom_call_target="tpu_custom_call" | custom-call | tf_op jit(solution)/shard_map/prepare/pallas_call | solution.py:424
  2.8 2.9 %collective-permute-start = (f32[2,4,16,128]{3,2,1,0:T(8,128)}, f32[2,4,16,128]{3,2,1,0:T(8,128)S(1)}, u32[]{:S(2)}, u32[]{:S(2)}) collective-permute-start(f32[2,4,16,128]{3,2,1,0:T(8,128)} %get-tuple-element.42), channel_id=1, source_target_pairs={{0,1},{1,0},{2,3},{3,2},{4,5},{5,4},{6,7},{7,6},{8,9},{9,8},{10,11... | collective-permute-start | bytes 196616 | tf_op jit(solution)/shard_map/ppermute | solution.py:432
  6.4 0.8 copy.19
  7.2 7.4 %all-gather = f32[8,8,16,128]{3,2,1,0:T(8,128)S(1)} all-gather(f32[2,8,16,128]{3,2,1,0:T(8,128)} %get-tuple-element.41), channel_id=2, replica_groups=mesh['gx'=4,'gy'=8] {'gx'}, dimensions={0}, use_global_device_ids=true | all-gather | bytes 655360 | tf_op jit(solution)/shard_map/all_gather | solution.py:434
  14.6 0.7 copy.24.refs_1_
  15.6 7.3 %all-gather.1 = f32[8,2,4,16,128]{4,3,2,1,0:T(8,128)S(1)} all-gather(f32[2,2,4,16,128]{4,3,2,1,0:T(8,128)S(1)} %pad_maximum_fusion), channel_id=3, replica_groups=mesh['gx'=4,'gy'=8] {'gx'}, dimensions={0}, use_global_device_ids=true | all-gather | bytes 655360 | tf_op jit(solution)/shard_map/all_gather | solution.py:435
  23.5 0.7 copy-done.5
  24.2 24.3 %setup.1 = (f32[1,64,256,128]{3,2,1,0:T(8,128)S(1)}, f32[1,88,256,128]{3,2,1,0:T(8,128)S(1)}, f32[64,16,128]{2,1,0:T(8,128)S(1)}) custom-call(s32[3]{0:T(128)S(1)} %copy-done.3, f32[16]{0:T(128)S(1)} %copy-done.5, bf16[256,96]{1,0:T(8,128)(2,1)S(1)} %concatenate.4.outer, f32[4,2,8,16,128]{4,3,2,1,0:T(8,128)S(1)} %bitcast.16, ...), custom_call_target="tpu_custom_call" | custom-call | tf_op jit(solution)/shard_map/setup/pallas_call | solution.py:447
  48.5 8.3 %iterate_0.1 = (f32[64,16,128]{2,1,0:T(8,128)S(1)}, f32[64,16,128]{2,1,0:T(8,128)S(1)}, f32[8,8,128]{2,1,0:T(8,128)S(1)}, f32[16,16,128]{2,1,0:T(8,128)S(1)}, f32[16,16,128]{2,1,0:T(8,128)S(1)}) custom-call(s32[3]{0:T(128)S(1)} %copy-done.3, f32[16,1]{1,0:T(8,128)S(1)} %copy.24.refs_1_, f32[1,64,256,128]{3,2,1,0:T(8,128)S(1)} %get-tuple-element.44.refs_2_, ...), custom_call_target="tpu_custom_call" | custom-call | tf_op jit(solution)/shard_map/iterate_0/pallas_call | solution.py:472
  56.8 4.3 %collective-permute-start.2 = (f32[16,16,128]{2,1,0:T(8,128)S(1)}, f32[16,16,128]{2,1,0:T(8,128)S(1)}, u32[]{:S(2)}, u32[]{:S(2)}) collective-permute-start(f32[16,16,128]{2,1,0:T(8,128)S(1)} %get-tuple-element.48), channel_id=1, source_target_pairs={{0,1},{1,0},{2,3},{3,2},{4,5},{5,4},{6,7},{7,6},{8,9},{9,8},{10,11... | collective-permute-start | bytes 393224 | tf_op jit(solution)/shard_map/ppermute | solution.py:485
  61.2 0.7 collective-permute-start.3
  61.9 13.1 %all_to_all.20.refs_5_ = f32[8,8,128]{2,1,0:T(8,128)S(1)} all-to-all(f32[8,8,128]{2,1,0:T(8,128)S(1)} %get-tuple-element.47), channel_id=1, replica_groups=mesh['gx'=4,'gy'=8] {'gy'}, dimensions={0} | all-to-all | bytes 65536 | tf_op jit(solution)/shard_map/all_to_all | solution.py:483
  74.9 8.6 %iterate_1.1 = (f32[64,16,128]{2,1,0:T(8,128)S(1)}, f32[64,16,128]{2,1,0:T(8,128)S(1)}, f32[8,8,128]{2,1,0:T(8,128)S(1)}, f32[16,16,128]{2,1,0:T(8,128)S(1)}, f3...) custom-call(s32[3]{0:T(128)S(1)} %copy-done.3, ...), custom_call_target="tpu_custom_call" | custom-call | tf_op jit(solution)/shard_map/iterate_1/pallas_call | solution.py:472
  84.1 0.7 collective-permute-start.5
  84.7 12.0 %all_to_all.21.refs_5_ = f32[8,8,128]{2,1,0:T(8,128)S(1)} all-to-all(f32[8,8,128]{2,1,0:T(8,128)S(1)} %get-tuple-element.53), channel_id=1, replica_groups=mesh['gx'=4,'gy'=8] {'gy'}, dimensions={0} | all-to-all | bytes 65536 | tf_op jit(solution)/shard_map/all_to_all | solution.py:483
  96.8 8.8 %iterate_2.1 = (f32[64,16,128]{2,1,0:T(8,128)S(1)}, f32[64,16,128]{2,1,0:T(8,128)S(1)}, f32[8,8,128]{2,1,0:T(8,128)S(1)}, f32[16,16,128]{2,1,0:T(8,128)S(1)}, f3...) custom-call(s32[3]{0:T(128)S(1)} %copy-done.3, ...), custom_call_target="tpu_custom_call" | custom-call | tf_op jit(solution)/shard_map/iterate_2/pallas_call | solution.py:472
  106.1 0.7 collective-permute-start.7
  106.8 12.0 %all_to_all.22.refs_5_ = f32[8,8,128]{2,1,0:T(8,128)S(1)} all-to-all(f32[8,8,128]{2,1,0:T(8,128)S(1)} %get-tuple-element.63), channel_id=1, replica_groups=mesh['gx'=4,'gy'=8] {'gy'}, dimensions={0} | all-to-all | bytes 65536 | tf_op jit(solution)/shard_map/all_to_all | solution.py:483
  118.8 9.6 %iterate_3.1 = (f32[64,16,128]{2,1,0:T(8,128)S(1)}, f32[64,16,128]{2,1,0:T(8,128)}, f32[8,8,128]{2,1,0:T(8,128)S(1)}, f32[8,128]{1,0:T(8,128)S(1)}, f32[64,16,12...) custom-call(s32[3]{0:T(128)S(1)} %copy-done.3, ...), custom_call_target="tpu_custom_call" | custom-call | tf_op jit(solution)/shard_map/iterate_3/pallas_call | solution.py:472
  128.4 0.8 copy-done
  129.2 0.8 copy-done.1
  130.0 0.8 copy-done.2
  130.8 9.7 %all_to_all.23.sums = f32[8,8,128]{2,1,0:T(8,128)} all-to-all(f32[8,8,128]{2,1,0:T(8,128)S(1)} %get-tuple-element.72), channel_id=1, replica_groups=mesh['gx'=4,'gy'=8] {'gy'}, dimensions={0} | all-to-all | bytes 65536 | tf_op jit(solution)/shard_map/all_to_all | solution.py:483
  140.5 2.6 %finish.1 = f32[16,8,128]{2,1,0:T(8,128)} custom-call(s32[3]{0:T(128)} %pad_add_fusion.place.refs_0_, f32[8,8,128]{2,1,0:T(8,128)} %all_to_all.23.sums, f32[8,128]{1,0:T(8,128)} %copy-done.4, f32[64,16,128]{2,1,0:T(8,128)} %copy-done.1, f32[64,16,128]{2,1,0:T(8,128)} %copy-done.2, f32[64,16,128]{2,1,0:T(8,128)} %copy-done), custom_call_target="tpu_custom_call" | custom-call | tf_op jit(solution)/shard_map/finish/pallas_call | solution.py:494
  (24 shorter events, 3.2 us)
Async XLA Ops:
  2.8 12.8 %collective-permute-start = (f32[2,4,16,128]{3,2,1,0:T(8,128)}, f32[2,4,16,128]{3,2,1,0:T(8,128)S(1)}, u32[]{:S(2)}, u32[]{:S(2)}) collective-permute-start(f32[2,4,16,128]{3,2,1,0:T(8,128)} %get-tuple-element.42), channel_id=1, source_target_pairs={{0,1},{1,0},{2,3},{3,2},{4,5},{5,4},{6,7},{7,6},{8,9},{9,8},{10,11... | collective-permute-start | bytes 196616 | tf_op jit(solution)/shard_map/ppermute | solution.py:432
  5.7 9.8 %collective-permute-start.1 = (f32[2,4,16,128]{3,2,1,0:T(8,128)}, f32[2,4,16,128]{3,2,1,0:T(8,128)S(1)}, u32[]{:S(2)}, u32[]{:S(2)}) collective-permute-start(f32[2,4,16,128]{3,2,1,0:T(8,128)} %get-tuple-element.43), channel_id=1, source_target_pairs={{1,2},{2,1},{3,4},{4,3},{5,6},{6,5},{9,10},{10,9},{11,12},{12,11},... | collective-permute-start | bytes 196616 | tf_op jit(solution)/shard_map/ppermute | solution.py:433
  22.9 0.6 copy-start.3
  23.5 0.7 copy-start.5
  56.8 18.1 %collective-permute-start.2 = (f32[16,16,128]{2,1,0:T(8,128)S(1)}, f32[16,16,128]{2,1,0:T(8,128)S(1)}, u32[]{:S(2)}, u32[]{:S(2)}) collective-permute-start(f32[16,16,128]{2,1,0:T(8,128)S(1)} %get-tuple-element.48), channel_id=1, source_target_pairs={{0,1},{1,0},{2,3},{3,2},{4,5},{5,4},{6,7},{7,6},{8,9},{9,8},{10,11... | collective-permute-start | bytes 393224 | tf_op jit(solution)/shard_map/ppermute | solution.py:485
  61.2 13.7 %collective-permute-start.3 = (f32[16,16,128]{2,1,0:T(8,128)S(1)}, f32[16,16,128]{2,1,0:T(8,128)S(1)}, u32[]{:S(2)}, u32[]{:S(2)}) collective-permute-start(f32[16,16,128]{2,1,0:T(8,128)S(1)} %get-tuple-element.49), channel_id=1, source_target_pairs={{1,2},{2,1},{3,4},{4,3},{5,6},{6,5},{9,10},{10,9},{11,12},{12,11},... | collective-permute-start | bytes 393224 | tf_op jit(solution)/shard_map/ppermute | solution.py:486
  83.5 13.2 %collective-permute-start.4 = (f32[16,16,128]{2,1,0:T(8,128)S(1)}, f32[16,16,128]{2,1,0:T(8,128)S(1)}, u32[]{:S(2)}, u32[]{:S(2)}) collective-permute-start(f32[16,16,128]{2,1,0:T(8,128)S(1)} %get-tuple-element.54), channel_id=1, source_target_pairs={{0,1},{1,0},{2,3},{3,2},{4,5},{5,4},{6,7},{7,6},{8,9},{9,8},{10,11... | collective-permute-start | bytes 393224 | tf_op jit(solution)/shard_map/ppermute | solution.py:485
  84.1 12.7 %collective-permute-start.5 = (f32[16,16,128]{2,1,0:T(8,128)S(1)}, f32[16,16,128]{2,1,0:T(8,128)S(1)}, u32[]{:S(2)}, u32[]{:S(2)}) collective-permute-start(f32[16,16,128]{2,1,0:T(8,128)S(1)} %get-tuple-element.55), channel_id=1, source_target_pairs={{1,2},{2,1},{3,4},{4,3},{5,6},{6,5},{9,10},{10,9},{11,12},{12,11},... | collective-permute-start | bytes 393224 | tf_op jit(solution)/shard_map/ppermute | solution.py:486
  105.6 13.2 %collective-permute-start.6 = (f32[16,16,128]{2,1,0:T(8,128)S(1)}, f32[16,16,128]{2,1,0:T(8,128)S(1)}, u32[]{:S(2)}, u32[]{:S(2)}) collective-permute-start(f32[16,16,128]{2,1,0:T(8,128)S(1)} %get-tuple-element.64), channel_id=1, source_target_pairs={{0,1},{1,0},{2,3},{3,2},{4,5},{5,4},{6,7},{7,6},{8,9},{9,8},{10,11... | collective-permute-start | bytes 393224 | tf_op jit(solution)/shard_map/ppermute | solution.py:485
  106.1 12.7 %collective-permute-start.7 = (f32[16,16,128]{2,1,0:T(8,128)S(1)}, f32[16,16,128]{2,1,0:T(8,128)S(1)}, u32[]{:S(2)}, u32[]{:S(2)}) collective-permute-start(f32[16,16,128]{2,1,0:T(8,128)S(1)} %get-tuple-element.65), channel_id=1, source_target_pairs={{1,2},{2,1},{3,4},{4,3},{5,6},{6,5},{9,10},{10,9},{11,12},{12,11},... | collective-permute-start | bytes 393224 | tf_op jit(solution)/shard_map/ppermute | solution.py:486
  128.4 0.8 copy-start
  129.2 0.8 copy-start.1
  130.0 0.8 copy-start.2
  130.8 9.7 %copy-start.4 = (f32[8,128]{1,0:T(8,128)}, f32[8,128]{1,0:T(8,128)S(1)}, u32[]{:S(2)}) copy-start(f32[8,128]{1,0:T(8,128)S(1)} %get-tuple-element.73.old) | copy-start | bytes 12292

commit v2 on v1

--- a/solution.py
+++ b/solution.py
@@ -24,6 +24,7 @@
 COUNTS = [n * n for n in SIDES]
 OFFSETS = [sum(COUNTS[:m]) for m in range(LEVELS)]
 SLOTS = -(-sum(COUNTS) // 8) * 8
+ROWS = K * K + 8
 SPLITS = ((0, 0), (0, 1), (0, 2), (1, 0), (1, 1), (2, 0))
 
 VMEM = pl.BlockSpec(memory_space=pltpu.VMEM)
@@ -88,103 +89,116 @@
     return {ij: -x for ij, x in a.items()}
 
 
-def setup_kernel(place, prior, outer, g_own, g_edge, blocks, inverse, rhs, weights, pieces, coarse_blocks, work):
+def setup_kernel(place, prior, outer, *refs):
+    rows = (len(refs) - 7) // 3
+    g_own, g_left, g_right = (refs[i * rows : (i + 1) * rows] for i in range(3))
+    blocks, inverse, rhs, weights, pieces, coarse_blocks, work = refs[3 * rows :]
     width = rhs.shape[-1]
     groups = width // 128
     lane = lanes_of((K, 128))
-    left_at = (place[1] + 1) % 2
-    right_at = 1 - left_at
-    for f, target in ((0, weights), (1, rhs)):
-        for group in range(groups):
+    even = place[1] % 2 == 0
+
+    def store_pieces(slot, group, rest):
+        cols = pl.ds((slot % 2) * 128, 128)
+        parts = []
+        for _ in range(3):
+            part = rest.astype(jnp.bfloat16)
+            parts.append(part)
+            rest = rest - part.astype(f32)
+        for i, (_, b) in enumerate(SPLITS):
+            pieces[group, slot // 2, pl.ds(i * K, K), cols] = parts[b]
+
+    for group in range(groups):
+        bases = [(place[0] ^ o) * SEGMENT - group * 128 for o in range(rows)]
+        masks = []
+        for base in bases:
+            at = lane - base
+            masks.append(((at >= 0) & (at < HALO), (at >= HALO) & (at < HALO + OWN), (at >= HALO + OWN) & (at < SEGMENT)))
+        for f in range(2):
             for t in range(BLOCK):
+                own = [g_own[o][f, t] for o in range(rows)]
+                first = [g_left[o][f, t // 2] for o in range(rows)]
+                second = [g_right[o][f, t // 2] for o in range(rows)]
+                left = [jnp.where(even, second[o], first[o]) for o in range(rows)]
+                right = [jnp.where(even, first[o], second[o]) for o in range(rows)]
+                odd = (t % 2) * HALO
                 for s in range(BLOCK):
                     value = jnp.zeros((K, 128), f32)
-                    for p in range(4):
-                        at = group * 4 + p
-                        base = p * SEGMENT
-                        odd = (t % 2) * HALO
-                        mid = roll(g_own[at, f, t], base + HALO - s * OWN)
-                        low = roll(g_edge[at, left_at, f, t // 2], base - s * OWN - odd)
-                        high = roll(g_edge[at, right_at, f, t // 2], base + SEGMENT - HALO - s * OWN - odd)
-                        value = jnp.where((lane >= base) & (lane < base + HALO), low, value)
-                        value = jnp.where((lane >= base + HALO) & (lane < base + HALO + OWN), mid, value)
-                        value = jnp.where((lane >= base + HALO + OWN) & (lane < base + SEGMENT), high, value)
-                    target[s * BLOCK + t, :, pl.ds(group * 128, 128)] = value
-    for m in range(1, LEVELS):
-        n, fine, coarse = SIDES[m], OFFSETS[m - 1], OFFSETS[m]
-        for s in range(n):
-            for t in range(n):
-                corner = fine + (2 * s) * (2 * n) + 2 * t
-                weights[coarse + s * n + t] = (
-                    weights[corner] + weights[corner + 1] + weights[corner + 2 * n] + weights[corner + 2 * n + 1]
-                )
-    for slot in range(sum(COUNTS), SLOTS):
-        weights[slot] = jnp.zeros((K, width), f32)
-
-    def split(slot, carry):
-        for group in range(groups):
-            rest = weights[slot, :, pl.ds(group * 128, 128)]
-            parts = []
-            for _ in range(3):
-                part = rest.astype(jnp.bfloat16)
-                parts.append(part)
-                rest = rest - part.astype(f32)
-            for i, (_, b) in enumerate(SPLITS):
-                pieces[group, slot, pl.ds(i * K, K), :] = parts[b]
-        return carry
-
-    lax.fori_loop(0, SLOTS, split, 0)
-
-    tables = ((blocks, 0, COUNTS[0]), (coarse_blocks, COUNTS[0], SLOTS - COUNTS[0]))
-    for table, first, count in tables:
-
-        def multiply(step, carry, table=table, first=first):
-            for group in range(groups):
-                for i in range(4):
-                    slot = step * 4 + i
-                    table[group, slot] = jnp.dot(
-                        outer[...], pieces[group, first + slot], preferred_element_type=f32
-                    )
-            return carry
-
-        lax.fori_loop(0, count // 4, multiply, 0)
-
-    flat_inverse = inverse.reshape(groups * SLOTS * K * K, 128)
+                    for o in range(rows):
+                        shift = bases[o] + 128 * rows - s * OWN
+                        low, mid, high = masks[o]
+                        value = jnp.where(low, pltpu.roll(left[o], (shift - odd) % 128, 1), value)
+                        value = jnp.where(mid, pltpu.roll(own[o], (shift + HALO) % 128, 1), value)
+                        value = jnp.where(high, pltpu.roll(right[o], (shift + SEGMENT - HALO - odd) % 128, 1), value)
+                    if f == 0:
+                        weights[s * BLOCK + t, :, pl.ds(group * 128, 128)] = value
+                        store_pieces(s * BLOCK + t, group, value)
+                    else:
+                        rhs[s * BLOCK + t, :, pl.ds(group * 128, 128)] = value
+        cols = pl.ds(group * 128, 128)
+        for m in range(1, LEVELS):
+            n, fine, coarse = SIDES[m], OFFSETS[m - 1], OFFSETS[m]
+            for s in range(n):
+                for t in range(n):
+                    corner = fine + (2 * s) * (2 * n) + 2 * t
+                    value = weights[corner, :, cols] + weights[corner + 1, :, cols]
+                    value = value + (weights[corner + 2 * n, :, cols] + weights[corner + 2 * n + 1, :, cols])
+                    weights[coarse + s * n + t, :, cols] = value
+                    store_pieces(coarse + s * n + t, group, value)
+        for slot in range(sum(COUNTS), SLOTS):
+            store_pieces(slot, group, jnp.zeros((K, 128), f32))
+
+    flat_inverse = inverse.reshape(groups * SLOTS * ROWS, 128)
     column = lanes_of((8, 128)) % SEGMENT
     inside = ((place[1] > 0) | (column >= HALO)) & ((place[1] < place[2] - 1) | (column < HALO + OWN))
     damped = jnp.where(inside, DAMPING, 0.0).astype(f32)
     half = K // 2
+    tables = ((blocks, 0, COUNTS[0]), (coarse_blocks, COUNTS[0], SLOTS - COUNTS[0]))
 
     for group, (table, offset, count) in ((x, y) for x in range(groups) for y in tables):
-        flat_blocks = table.reshape(groups * count * K * K, 128)
-
-        def invert(g, carry, group=group, flat_blocks=flat_blocks, offset=offset, count=count):
+        flat_blocks = table.reshape(groups * count * ROWS, 128)
+
+        def multiply(g, group=group, table=table, offset=offset):
+            for i in range(4):
+                pair = jnp.dot(outer[...], pieces[group, offset // 2 + g * 4 + i], preferred_element_type=f32)
+                table[group, g * 8 + 2 * i, pl.ds(0, K * K), :] = pair[:, :128]
+                table[group, g * 8 + 2 * i + 1, pl.ds(0, K * K), :] = pair[:, 128:]
+
+        def invert(g, carry, group=group, flat_blocks=flat_blocks, offset=offset, count=count, multiply=multiply):
             slot = offset + g * 8 + lax.broadcasted_iota(jnp.int32, (8, 128), 0)
             scale = jnp.where(
                 slot < OFFSETS[1], 4.0, jnp.where(slot < OFFSETS[2], 8.0, jnp.where(slot < OFFSETS[3], 16.0, 32.0))
             ).astype(f32)
-            source = (group * count + g * 8) * (K * K)
-            target = (group * SLOTS + offset + g * 8) * (K * K)
+            source = (group * count + g * 8) * ROWS
+            target = (group * SLOTS + offset + g * 8) * ROWS
 
             def load(k, l):
-                value = flat_blocks[pl.ds(source + l * K + k, 8, stride=K * K), :]
+                value = flat_blocks[pl.ds(source + l * K + k, 8, stride=ROWS), :]
                 return value + scale * prior[k] if k == l else value
 
             def store(k, l, value):
                 value = value * damped
-                flat_inverse[pl.ds(target + l * K + k, 8, stride=K * K), :] = value
+                flat_inverse[pl.ds(target + l * K + k, 8, stride=ROWS), :] = value
                 if k != l:
-                    flat_inverse[pl.ds(target + k * K + l, 8, stride=K * K), :] = value
-
-            first = symmetric_inverse({(i, j): load(i, j) for i in range(half) for j in range(i + 1)}, half)
+                    flat_inverse[pl.ds(target + k * K + l, 8, stride=ROWS), :] = value
+
             for i in range(half):
                 for j in range(half):
                     work[0, i * half + j] = load(half + j, i)
+            for i in range(half):
+                for j in range(i + 1):
+                    work[2, i * half + j] = load(half + i, half + j)
+            first = {(i, j): load(i, j) for i in range(half) for j in range(i + 1)}
+            multiply(jnp.minimum(g + 1, count // 8 - 1))
+            first = symmetric_inverse(first, half)
             for j in range(half):
                 b = [work[0, i * half + j] for i in range(half)]
                 for i in range(half):
                     work[1, i * half + j] = sum(first[max(i, h), min(i, h)] * b[h] for h in range(half))
-            schur = {(i, j): load(half + i, half + j) for i in range(half) for j in range(i + 1)}
+            for i in range(half):
+                for j in range(i + 1):
+                    work[3, i * half + j] = first[i, j]
+            schur = {(i, j): work[2, i * half + j] for i in range(half) for j in range(i + 1)}
             for h in range(half):
                 b = [work[0, h * half + j] for j in range(half)]
                 y = [work[1, h * half + j] for j in range(half)]
@@ -200,6 +214,7 @@
                     z = sum(y[h] * second[max(h, j), min(h, j)] for h in range(half))
                     work[0, i * half + j] = z
                     store(half + j, i, -z)
+            first = {(i, j): work[3, i * half + j] for i in range(half) for j in range(i + 1)}
             for h in range(half):
                 z = [work[0, i * half + h] for i in range(half)]
                 y = [work[1, i * half + h] for i in range(half)]
@@ -210,6 +225,7 @@
                 store(i, j, value)
             return carry
 
+        multiply(0)
         lax.fori_loop(0, count // 8, invert, 0)
 
 
@@ -232,7 +248,7 @@
             finish(i, cols, total)
         return carry
 
-    lax.fori_loop(0, count, one, 0, unroll=min(count, 8))
+    lax.fori_loop(0, count, one, 0, unroll=min(count, 16))
 
 
 def v_cycle(inverse, prior, b, v, d, w):
@@ -294,11 +310,12 @@
         sums, edge_a, edge_b, z_in, az_in = (refs.pop(0) for _ in range(5))
     if step > 1:
         old, x_in, p_in, ap_in = (refs.pop(0) for _ in range(4))
-    z_out, az_out, parts = (refs.pop(0) for _ in range(3))
-    if not last:
-        send_a, send_b = (refs.pop(0) for _ in range(2))
-    if step > 0:
-        scalars, residual, x, p, ap = (refs.pop(0) for _ in range(5))
+    if last:
+        parts, scalars, packed, residual, x, p, ap, z_out, az_out = (refs.pop(0) for _ in range(9))
+    else:
+        parts, z_out, az_out, send_a, send_b = (refs.pop(0) for _ in range(5))
+        if step > 0:
+            scalars, residual, x, p, ap = (refs.pop(0) for _ in range(5))
     b, v, d, w = (refs[i * LEVELS : (i + 1) * LEVELS] for i in range(4))
     width = z_out.shape[-1]
     lane = lanes_of((K, width))
@@ -365,7 +382,15 @@
     tile = jnp.concatenate(rows, axis=0)
     for i in range(parts.shape[0]):
         parts[i] = tile
-    if not last:
+    if last:
+        tile = refs[-1]
+        for i, source in enumerate((x, z_out, p)):
+            pack(place, source, tile)
+            back = lax.dot_general(
+                tile[...], lane_order(), (((1,), (1,)), ((), ())), precision=highest, preferred_element_type=f32
+            )
+            packed[i] = back.reshape(K, BLOCK, 128)
+    else:
         for i in range(count // 4):
             left, right = None, None
             for g in range(4):
@@ -391,23 +416,35 @@
     return gamma, gamma / energy, beta, energy
 
 
-def finish_kernel(place, sums, old, x, p, z, out, tile):
-    _, alpha, beta, _ = coefficients(sums, old)
+def pack(place, source, tile):
     group = pl.ds(pl.multiple_of((place[0] // 4) * 128, 128), 128)
     base = (place[0] % 4) * SEGMENT + HALO
     lane = lanes_of((K, 128))
     for t in range(BLOCK):
         packed = None
         for s in range(BLOCK):
-            at = s * BLOCK + t
-            value = x[at, :, group] + alpha * (z[at, :, group] + beta * p[at, :, group])
-            value = pltpu.roll(value, (128 + s * OWN - base) % 128, 1)
+            value = pltpu.roll(source[s * BLOCK + t, :, group], (128 + s * OWN - base) % 128, 1)
             packed = value if packed is None else jnp.where(lane >= s * OWN, value, packed)
         tile[pl.ds(t, K, stride=BLOCK), :] = packed
-    back = lax.dot_general(
-        tile[...], lane_order(), (((1,), (1,)), ((), ())), precision=highest, preferred_element_type=f32
-    )
-    out[...] = back.reshape(K, BLOCK, 128)
+
+
+def finish_kernel(sums, old, packed, out):
+    _, alpha, beta, _ = coefficients(sums, old)
+    alpha, beta = jnp.broadcast_to(alpha, (BLOCK, 128)), jnp.broadcast_to(beta, (BLOCK, 128))
+    for k in range(K):
+        out[k] = packed[0, k] + alpha * (packed[1, k] + beta * packed[2, k])
+
+
+def gather(value):
+    rows = lax.axis_size("gx")
+    held = {0: value}
+    bit = rows // 2
+    while bit:
+        pairs = [(i, i ^ bit) for i in range(rows)]
+        for o in list(held):
+            held[o ^ bit] = lax.ppermute(held[o], "gx", pairs)
+        bit //= 2
+    return [held[o] for o in range(rows)]
 
 
 def local(beta, design, prior, kept, removed, removed_labels):
@@ -431,8 +468,7 @@
     )(place, design, beta, kept, removed, removed_labels)
     edge_a = lax.ppermute(edge_a, "gy", pairs)
     edge_b = lax.ppermute(edge_b, "gy", others)
-    g_own = lax.all_gather(own, "gx")
-    g_edge = lax.all_gather(jnp.stack([edge_a, edge_b]), "gx")
+    gathered = gather(own) + gather(edge_a) + gather(edge_b)
 
     products = (design[:, :, None] * design[:, None, :]).reshape(K, K * K).T
     parts, rest = [], products
@@ -446,59 +482,59 @@
     field = shape(COUNTS[0], K, width)
     blocks, inverse, residual = pl.pallas_call(
         setup_kernel,
-        out_shape=[shape(width // 128, n, K * K, 128) for n in (COUNTS[0], SLOTS)] + [field],
-        in_specs=[SMEM, SMEM] + [VMEM] * 3,
+        out_shape=[shape(width // 128, n, ROWS, 128) for n in (COUNTS[0], SLOTS)] + [field],
+        in_specs=[SMEM, SMEM] + [VMEM] * (1 + len(gathered)),
         out_specs=[VMEM] * 3,
         scratch_shapes=[
             pltpu.VMEM((SLOTS, K, width), f32),
-            pltpu.VMEM((width // 128, SLOTS, len(SPLITS) * K, 128), jnp.bfloat16),
-            pltpu.VMEM((width // 128, SLOTS - COUNTS[0], K * K, 128), f32),
-            pltpu.VMEM((2, K * K // 4, 8, 128), f32),
+            pltpu.VMEM((width // 128, SLOTS // 2, len(SPLITS) * K, 256), jnp.bfloat16),
+            pltpu.VMEM((width // 128, SLOTS - COUNTS[0], ROWS, 128), f32),
+            pltpu.VMEM((4, K * K // 4, 8, 128), f32),
         ],
         compiler_params=params(24 if width == 128 else 60),
         name="setup",
-    )(place, prior, outer, g_own, g_edge)
-
-    levels = [pltpu.VMEM((n, K, width), f32) for n in COUNTS]
+    )(place, prior, outer, *gathered)
+
+    levels = [pltpu.VMEM((n, K, width), f32) for n in COUNTS] * 4
+    whole = pltpu.VMEM((COUNTS[0], K, width), f32)
+    edge = shape(COUNTS[0] // 4, K, width)
+    parts = shape(cols, 8, 128)
     state = ()
     for step in range(ITERS):
         last = step == ITERS - 1
         operands = (place, prior_rows, blocks, inverse, residual) + state
-        shapes = [field, field, shape(cols, 8, 128)]
-        if not last:
-            shapes += [shape(COUNTS[0] // 4, K, width)] * 2
-        if step > 0:
-            shapes += [shape(8, 128), field, field, field, field]
+        if last:
+            shapes = [parts, shape(8, 128), shape(3, *beta.shape)]
+            scratch = [whole] * 6 + levels + [pltpu.VMEM((K * BLOCK, 128), f32)]
+        else:
+            shapes = [parts, field, field, edge, edge]
+            if step > 0:
+                shapes += [shape(8, 128), field, field, field, field]
+            scratch = levels
         outs = pl.pallas_call(
             functools.partial(iterate_kernel, step, last),
             out_shape=shapes,
             in_specs=[SMEM] + [VMEM] * (len(operands) - 1),
             out_specs=[VMEM] * len(shapes),
-            scratch_shapes=levels * 4,
+            scratch_shapes=scratch,
             compiler_params=params(24 if width == 128 else 60),
             name=f"iterate_{step}",
         )(*operands)
-        z, az, sums = outs[:3]
-        outs = outs[3:]
-        sums = lax.all_to_all(sums, "gy", 0, 0, tiled=True)
+        sums = lax.all_to_all(outs[0], "gy", 0, 0, tiled=True)
         if not last:
-            edge_a = lax.ppermute(outs[0], "gy", pairs)
-            edge_b = lax.ppermute(outs[1], "gy", others)
-            outs = outs[2:]
-        history = ()
-        if step > 0:
-            scalars, residual, x, p, ap = outs
-            history = (scalars, x, p, ap)
-        if not last:
-            state = (sums, edge_a, edge_b, z, az) + history
+            edge_a = lax.ppermute(outs[3], "gy", pairs)
+            edge_b = lax.ppermute(outs[4], "gy", others)
+            state = (sums, edge_a, edge_b, outs[1], outs[2])
+            if step > 0:
+                residual = outs[6]
+                state += (outs[5], outs[7], outs[8], outs[9])
     return pl.pallas_call(
         finish_kernel,
         out_shape=shape(*beta.shape),
-        in_specs=[SMEM] + [VMEM] * 5,
+        in_specs=[VMEM] * 3,
         out_specs=VMEM,
-        scratch_shapes=[pltpu.VMEM((K * BLOCK, 128), f32)],
         name="finish",
-    )(place, sums, scalars, x, p, z)
+    )(sums, outs[1], outs[2])
 
 
 def solution(mesh):

time: 144 us -> 123 us (0.85)
  blocking collectives: 61.5 us -> 46.8 us
  Pallas kernels: 64.4 us -> 51.6 us
  starting transfers between devices: 11 us -> 15.8 us
  waiting for transfers between devices: 0.02 us -> 3.25 us
    all_gather x2 -> x0, blocking collectives: 14.7 us -> none  [the longest x1 7.41 us: local(): g_own = lax.all_gather(own, 'gx')]
    pallas_call x2, Pallas kernels: 26.9 us -> 15.5 us  [the longest x1 13.8 us: local(): pl.pallas_call(setup_kernel, out_shape=[shape(width // 128, n, ROWS, 128)...]
    ppermute x6 -> x15, starting transfers between devices: 7.4 us -> 12.2 us  [the longest x3 5.34 us: local(): edge_a = lax.ppermute(outs[3], 'gy', pairs)]
    ppermute x6 -> x15, waiting for transfers between devices: 0.02 us -> 3.24 us  [the longest x9 3.23 us: gather(): held[o ^ bit] = lax.ppermute(held[o], 'gx', pairs)]
    unnamed x13 -> x11, local copies, waits for them, and re-layouts: 4.44 us -> 3.67 us
  transfers between devices with their start and end apart: 8 -> 17, of which waited for: 0 -> 2; matrix products, arithmetic and copies ran while one was open for 1% -> 1% of each run, Pallas kernels for 0% -> 0%
where the time goes in v2:
time: 123 us
  Pallas kernels  51.6 us (42%)
  blocking collectives  46.8 us (38%)
  starting transfers between devices  15.8 us (13%)
  local copies, waits for them, and re-layouts  4.58 us (4%)
  waiting for transfers between devices  3.25 us (3%)
    all_to_all x4, blocking collectives, local(): sums = lax.all_to_all(outs[0], 'gy', 0, 0, tiled=True)  46.8 us
    pallas_call x4, Pallas kernels, local(): pl.pallas_call(functools.partial(iterate_kernel, step, last), out_shape=s...  33.9 us
    pallas_call x1, Pallas kernels, local(): pl.pallas_call(setup_kernel, out_shape=[shape(width // 128, n, ROWS, 128)...  13.8 us
    ppermute x3, starting transfers between devices, local(): edge_a = lax.ppermute(outs[3], 'gy', pairs)  5.34 us
    ppermute x9, starting transfers between devices, gather(): held[o ^ bit] = lax.ppermute(held[o], 'gx', pairs)  4.86 us
    unnamed x11, local copies, waits for them, and re-layouts  3.67 us
    ppermute x9, waiting for transfers between devices, gather(): held[o ^ bit] = lax.ppermute(held[o], 'gx', pairs)  3.23 us
    ppermute x1, starting transfers between devices, local(): edge_a = lax.ppermute(edge_a, 'gy', pairs)  2.94 us
  transfers between devices with their start and end apart: 17, of which 2 were waited for; matrix products, arithmetic and copies ran while one was open for 1% of the time, Pallas kernels for 0%

profile of v2, /device:TPU:0, one launch (start us, length us, event | category | flops | bytes accessed | tf_op | source)
XLA Modules:
  0.0 122.8 jit_solution(10936021856601200971)
XLA Ops:
  0.6 2.2 %prepare.1 = (f32[2,8,16,128]{3,2,1,0:T(8,128)}, f32[2,4,16,128]{3,2,1,0:T(8,128)}, f32[2,4,16,128]{3,2,1,0:T(8,128)}) custom-call(s32[3]{0:T(128)} %pad_add_fusion.place.refs_0_, f32[16,16]{1,0:T(8,128)} %design.1, f32[16,8,128]{2,1,0:T(8,128)} %beta.1, s32[16,8,128]{2,1,0:T(8,128)} %kept.1, s32[16,8,128]{2,1,0:T(8,128)} %removed.1, s32[16,8,128]{2,1,0:T(8,128)} %labels.1), custom_call_target="tpu_custom_call" | custom-call | tf_op jit(solution)/shard_map/prepare/pallas_call | solution.py:461
  2.8 2.9 %collective-permute-start.3 = (f32[2,4,16,128]{3,2,1,0:T(8,128)}, f32[2,4,16,128]{3,2,1,0:T(8,128)S(1)}, u32[]{:S(2)}, u32[]{:S(2)}) collective-permute-start(f32[2,4,16,128]{3,2,1,0:T(8,128)} %get-tuple-element.40), channel_id=1, source_target_pairs={{0,1},{1,0},{2,3},{3,2},{4,5},{5,4},{6,7},{7,6},{8,9},{9,8},{10,11... | collective-permute-start | bytes 196616 | tf_op jit(solution)/shard_map/ppermute | solution.py:469
  6.4 1.6 %collective-permute-start.1 = (f32[2,8,16,128]{3,2,1,0:T(8,128)}, f32[2,8,16,128]{3,2,1,0:T(8,128)S(1)}, u32[]{:S(2)}, u32[]{:S(2)}) collective-permute-start(f32[2,8,16,128]{3,2,1,0:T(8,128)} %get-tuple-element.39.refs_0_), channel_id=1, source_target_pairs={{0,16},{8,24},{16,0},{24,8},{1,17},{9,25},{17,1},{25,9},{2,18},{10... | collective-permute-start | bytes 393224 | tf_op jit(solution)/shard_map/ppermute | solution.py:445
  8.0 0.8 copy.13
  8.8 1.5 %collective-permute-start.5 = (f32[2,4,16,128]{3,2,1,0:T(8,128)S(1)}, f32[2,4,16,128]{3,2,1,0:T(8,128)S(1)}, u32[]{:S(2)}, u32[]{:S(2)}) collective-permute-start(f32[2,4,16,128]{3,2,1,0:T(8,128)S(1)} %collective-permute-done.3.refs_4_), channel_id=1, source_target_pairs={{0,16},{8,24},{16,0},{24,8},{1,17},{9,25},{17,1},{25,9},{2,18},{10... | collective-permute-start | bytes 196616 | tf_op jit(solution)/shard_map/ppermute | solution.py:445
  10.3 0.8 collective-permute-start.9
  11.1 2.2 %collective-permute-done.5.refs_6_ = f32[2,4,16,128]{3,2,1,0:T(8,128)S(1)} collective-permute-done((f32[2,4,16,128]{3,2,1,0:T(8,128)S(1)}, f32[2,4,16,128]{3,2,1,0:T(8,128)S(1)}, u32[]{:S(2)}, u32[]{:S(2)}) %collective-permute-start.5) | collective-permute-done | bytes 65568 | tf_op jit(solution)/shard_map/ppermute | solution.py:445
  13.8 1.0 collective-permute-done.9.refs_10_
  15.3 0.7 copy.18.refs_1_
  16.3 0.9 copy-done.1
  18.5 13.8 %setup.1 = (f32[1,64,264,128]{3,2,1,0:T(8,128)S(1)}, f32[1,88,264,128]{3,2,1,0:T(8,128)S(1)}, f32[64,16,128]{2,1,0:T(8,128)S(1)}) custom-call(s32[3]{0:T(128)S(1)} %copy-done.2, f32[16]{0:T(128)S(1)} %copy-done.4, bf16[256,96]{1,0:T(8,128)(2,1)S(1)} %concatenate.4.outer, f32[2,8,16,128]{3,2,1,0:T(8,128)S(1)} %copy-done.1, ...), custom_call_target="tpu_custom_call" | custom-call | tf_op jit(solution)/shard_map/setup/pallas_call | solution.py:483
  32.3 8.0 %iterate_0.1 = (f32[8,8,128]{2,1,0:T(8,128)S(1)}, f32[64,16,128]{2,1,0:T(8,128)S(1)}, f32[64,16,128]{2,1,0:T(8,128)S(1)}, f32[16,16,128]{2,1,0:T(8,128)S(1)}, f32[16,16,128]{2,1,0:T(8,128)S(1)}) custom-call(s32[3]{0:T(128)S(1)} %copy-done.2, f32[16,1]{1,0:T(8,128)S(1)} %copy.18.refs_1_, f32[1,64,264,128]{3,2,1,0:T(8,128)S(1)} %get-tuple-element.42.refs_2_, ...), custom_call_target="tpu_custom_call" | custom-call | tf_op jit(solution)/shard_map/iterate_0/pallas_call | solution.py:514
  40.3 4.3 %collective-permute-start.11 = (f32[16,16,128]{2,1,0:T(8,128)S(1)}, f32[16,16,128]{2,1,0:T(8,128)S(1)}, u32[]{:S(2)}, u32[]{:S(2)}) collective-permute-start(f32[16,16,128]{2,1,0:T(8,128)S(1)} %get-tuple-element.46), channel_id=1, source_target_pairs={{0,1},{1,0},{2,3},{3,2},{4,5},{5,4},{6,7},{7,6},{8,9},{9,8},{10,11... | collective-permute-start | bytes 393224 | tf_op jit(solution)/shard_map/ppermute | solution.py:525
  44.6 0.7 collective-permute-start.12
  45.3 13.1 %all_to_all.20.refs_5_ = f32[8,8,128]{2,1,0:T(8,128)S(1)} all-to-all(f32[8,8,128]{2,1,0:T(8,128)S(1)} %get-tuple-element.45), channel_id=1, replica_groups=mesh['gx'=4,'gy'=8] {'gy'}, dimensions={0} | all-to-all | bytes 65536 | tf_op jit(solution)/shard_map/all_to_all | solution.py:523
  58.3 8.3 %iterate_1.1 = (f32[8,8,128]{2,1,0:T(8,128)S(1)}, f32[64,16,128]{2,1,0:T(8,128)S(1)}, f32[64,16,128]{2,1,0:T(8,128)S(1)}, f32[16,16,128]{2,1,0:T(8,128)S(1)}, f3...) custom-call(s32[3]{0:T(128)S(1)} %copy-done.2, ...), custom_call_target="tpu_custom_call" | custom-call | tf_op jit(solution)/shard_map/iterate_1/pallas_call | solution.py:514
  67.2 0.7 collective-permute-start.14
  67.9 12.0 %all_to_all.21.refs_5_ = f32[8,8,128]{2,1,0:T(8,128)S(1)} all-to-all(f32[8,8,128]{2,1,0:T(8,128)S(1)} %get-tuple-element.51), channel_id=1, replica_groups=mesh['gx'=4,'gy'=8] {'gy'}, dimensions={0} | all-to-all | bytes 65536 | tf_op jit(solution)/shard_map/all_to_all | solution.py:523
  79.9 8.5 %iterate_2.1 = (f32[8,8,128]{2,1,0:T(8,128)S(1)}, f32[64,16,128]{2,1,0:T(8,128)S(1)}, f32[64,16,128]{2,1,0:T(8,128)S(1)}, f32[16,16,128]{2,1,0:T(8,128)S(1)}, f3...) custom-call(s32[3]{0:T(128)S(1)} %copy-done.2, ...), custom_call_target="tpu_custom_call" | custom-call | tf_op jit(solution)/shard_map/iterate_2/pallas_call | solution.py:514
  89.6 12.0 %all_to_all.22.refs_5_ = f32[8,8,128]{2,1,0:T(8,128)S(1)} all-to-all(f32[8,8,128]{2,1,0:T(8,128)S(1)} %get-tuple-element.61), channel_id=1, replica_groups=mesh['gx'=4,'gy'=8] {'gy'}, dimensions={0} | all-to-all | bytes 65536 | tf_op jit(solution)/shard_map/all_to_all | solution.py:523
  101.6 9.0 %iterate_3.1 = (f32[8,8,128]{2,1,0:T(8,128)S(1)}, f32[8,128]{1,0:T(8,128)S(1)}, f32[3,16,8,128]{3,2,1,0:T(8,128)S(1)}) custom-call(s32[3]{0:T(128)S(1)} %copy-done.2, f32[16,1]{1,0:T(8,128)S(1)} %copy.18.refs_1_, f32[1,64,264,128]{3,2,1,0:T(8,128)S(1)} %get-tuple-element.42.refs_2_, f32[1,88,264,128]{3,2,1,0:T(8,128)S(1)} %get-tuple-element.43.refs_3_, ...), custom_call_target="tpu_custom_call" | custom-call | tf_op jit(solution)/shard_map/iterate_3/pallas_call | solution.py:514
  110.7 0.7 copy-done
  111.3 9.7 %all_to_all.23.sums = f32[8,8,128]{2,1,0:T(8,128)} all-to-all(f32[8,8,128]{2,1,0:T(8,128)S(1)} %get-tuple-element.70), channel_id=1, replica_groups=mesh['gx'=4,'gy'=8] {'gy'}, dimensions={0} | all-to-all | bytes 65536 | tf_op jit(solution)/shard_map/all_to_all | solution.py:523
  121.1 1.7 %finish.1 = f32[16,8,128]{2,1,0:T(8,128)} custom-call(f32[8,8,128]{2,1,0:T(8,128)} %all_to_all.23.sums, f32[8,128]{1,0:T(8,128)} %copy-done.3, f32[3,16,8,128]{3,2,1,0:T(8,128)} %copy-done), custom_call_target="tpu_custom_call" | custom-call | tf_op jit(solution)/shard_map/finish/pallas_call | solution.py:531
  (37 shorter events, 5.6 us)
Async XLA Ops:
  2.8 6.0 %collective-permute-start.3 = (f32[2,4,16,128]{3,2,1,0:T(8,128)}, f32[2,4,16,128]{3,2,1,0:T(8,128)S(1)}, u32[]{:S(2)}, u32[]{:S(2)}) collective-permute-start(f32[2,4,16,128]{3,2,1,0:T(8,128)} %get-tuple-element.40), channel_id=1, source_target_pairs={{0,1},{1,0},{2,3},{3,2},{4,5},{5,4},{6,7},{7,6},{8,9},{9,8},{10,11... | collective-permute-start | bytes 196616 | tf_op jit(solution)/shard_map/ppermute | solution.py:469
  5.8 4.5 %collective-permute-start.7 = (f32[2,4,16,128]{3,2,1,0:T(8,128)}, f32[2,4,16,128]{3,2,1,0:T(8,128)S(1)}, u32[]{:S(2)}, u32[]{:S(2)}) collective-permute-start(f32[2,4,16,128]{3,2,1,0:T(8,128)} %get-tuple-element.41), channel_id=1, source_target_pairs={{1,2},{2,1},{3,4},{4,3},{5,6},{6,5},{9,10},{10,9},{11,12},{12,11},... | collective-permute-start | bytes 196616 | tf_op jit(solution)/shard_map/ppermute | solution.py:470
  6.4 8.4 %collective-permute-start.1 = (f32[2,8,16,128]{3,2,1,0:T(8,128)}, f32[2,8,16,128]{3,2,1,0:T(8,128)S(1)}, u32[]{:S(2)}, u32[]{:S(2)}) collective-permute-start(f32[2,8,16,128]{3,2,1,0:T(8,128)} %get-tuple-element.39.refs_0_), channel_id=1, source_target_pairs={{0,16},{8,24},{16,0},{24,8},{1,17},{9,25},{17,1},{25,9},{2,18},{10... | collective-permute-start | bytes 393224 | tf_op jit(solution)/shard_map/ppermute | solution.py:445
  8.0 8.3 %collective-permute-start = (f32[2,8,16,128]{3,2,1,0:T(8,128)}, f32[2,8,16,128]{3,2,1,0:T(8,128)S(1)}, u32[]{:S(2)}, u32[]{:S(2)}) collective-permute-start(f32[2,8,16,128]{3,2,1,0:T(8,128)} %get-tuple-element.39.refs_0_), channel_id=1, source_target_pairs={{0,8},{8,0},{16,24},{24,16},{1,9},{9,1},{17,25},{25,17},{2,10},{10... | collective-permute-start | bytes 393224 | tf_op jit(solution)/shard_map/ppermute | solution.py:445
  8.8 4.5 %collective-permute-start.5 = (f32[2,4,16,128]{3,2,1,0:T(8,128)S(1)}, f32[2,4,16,128]{3,2,1,0:T(8,128)S(1)}, u32[]{:S(2)}, u32[]{:S(2)}) collective-permute-start(f32[2,4,16,128]{3,2,1,0:T(8,128)S(1)} %collective-permute-done.3.refs_4_), channel_id=1, source_target_pairs={{0,16},{8,24},{16,0},{24,8},{1,17},{9,25},{17,1},{25,9},{2,18},{10... | collective-permute-start | bytes 196616 | tf_op jit(solution)/shard_map/ppermute | solution.py:445
  10.3 3.0 %collective-permute-start.4 = (f32[2,4,16,128]{3,2,1,0:T(8,128)S(1)}, f32[2,4,16,128]{3,2,1,0:T(8,128)S(1)}, u32[]{:S(2)}, u32[]{:S(2)}) collective-permute-start(f32[2,4,16,128]{3,2,1,0:T(8,128)S(1)} %collective-permute-done.3.refs_4_), channel_id=1, source_target_pairs={{0,8},{8,0},{16,24},{24,16},{1,9},{9,1},{17,25},{25,17},{2,10},{10... | collective-permute-start | bytes 196616 | tf_op jit(solution)/shard_map/ppermute | solution.py:445
  10.3 4.5 %collective-permute-start.9 = (f32[2,4,16,128]{3,2,1,0:T(8,128)S(1)}, f32[2,4,16,128]{3,2,1,0:T(8,128)S(1)}, u32[]{:S(2)}, u32[]{:S(2)}) collective-permute-start(f32[2,4,16,128]{3,2,1,0:T(8,128)S(1)} %collective-permute-done.7.refs_8_), channel_id=1, source_target_pairs={{0,16},{8,24},{16,0},{24,8},{1,17},{9,25},{17,1},{25,9},{2,18},{10... | collective-permute-start | bytes 196616 | tf_op jit(solution)/shard_map/ppermute | solution.py:445
  13.3 3.0 %collective-permute-start.8 = (f32[2,4,16,128]{3,2,1,0:T(8,128)S(1)}, f32[2,4,16,128]{3,2,1,0:T(8,128)S(1)}, u32[]{:S(2)}, u32[]{:S(2)}) collective-permute-start(f32[2,4,16,128]{3,2,1,0:T(8,128)S(1)} %collective-permute-done.7.refs_8_), channel_id=1, source_target_pairs={{0,8},{8,0},{16,24},{24,16},{1,9},{9,1},{17,25},{25,17},{2,10},{10... | collective-permute-start | bytes 196616 | tf_op jit(solution)/shard_map/ppermute | solution.py:445
  13.3 3.0 %collective-permute-start.6 = (f32[2,4,16,128]{3,2,1,0:T(8,128)S(1)}, f32[2,4,16,128]{3,2,1,0:T(8,128)S(1)}, u32[]{:S(2)}, u32[]{:S(2)}) collective-permute-start(f32[2,4,16,128]{3,2,1,0:T(8,128)S(1)} %collective-permute-done.5.refs_6_), channel_id=1, source_target_pairs={{0,8},{8,0},{16,24},{24,16},{1,9},{9,1},{17,25},{25,17},{2,10},{10... | collective-permute-start | bytes 196616 | tf_op jit(solution)/shard_map/ppermute | solution.py:445
  14.8 1.5 %collective-permute-start.10 = (f32[2,4,16,128]{3,2,1,0:T(8,128)S(1)}, f32[2,4,16,128]{3,2,1,0:T(8,128)S(1)}, u32[]{:S(2)}, u32[]{:S(2)}) collective-permute-start(f32[2,4,16,128]{3,2,1,0:T(8,128)S(1)} %collective-permute-done.9.refs_10_), channel_id=1, source_target_pairs={{0,8},{8,0},{16,24},{24,16},{1,9},{9,1},{17,25},{25,17},{2,10},{10... | collective-permute-start | bytes 196616 | tf_op jit(solution)/shard_map/ppermute | solution.py:445
  14.8 1.5 %collective-permute-start.2 = (f32[2,8,16,128]{3,2,1,0:T(8,128)S(1)}, f32[2,8,16,128]{3,2,1,0:T(8,128)S(1)}, u32[]{:S(2)}, u32[]{:S(2)}) collective-permute-start(f32[2,8,16,128]{3,2,1,0:T(8,128)S(1)} %collective-permute-done.1.refs_2_), channel_id=1, source_target_pairs={{0,8},{8,0},{16,24},{24,16},{1,9},{9,1},{17,25},{25,17},{2,10},{10... | collective-permute-start | bytes 393224 | tf_op jit(solution)/shard_map/ppermute | solution.py:445
  16.3 0.9 copy-start.1
  17.2 0.7 copy-start.2
  17.9 0.7 copy-start.4
  40.3 18.0 %collective-permute-start.11 = (f32[16,16,128]{2,1,0:T(8,128)S(1)}, f32[16,16,128]{2,1,0:T(8,128)S(1)}, u32[]{:S(2)}, u32[]{:S(2)}) collective-permute-start(f32[16,16,128]{2,1,0:T(8,128)S(1)} %get-tuple-element.46), channel_id=1, source_target_pairs={{0,1},{1,0},{2,3},{3,2},{4,5},{5,4},{6,7},{7,6},{8,9},{9,8},{10,11... | collective-permute-start | bytes 393224 | tf_op jit(solution)/shard_map/ppermute | solution.py:525
  44.6 13.7 %collective-permute-start.12 = (f32[16,16,128]{2,1,0:T(8,128)S(1)}, f32[16,16,128]{2,1,0:T(8,128)S(1)}, u32[]{:S(2)}, u32[]{:S(2)}) collective-permute-start(f32[16,16,128]{2,1,0:T(8,128)S(1)} %get-tuple-element.47), channel_id=1, source_target_pairs={{1,2},{2,1},{3,4},{4,3},{5,6},{6,5},{9,10},{10,9},{11,12},{12,11},... | collective-permute-start | bytes 393224 | tf_op jit(solution)/shard_map/ppermute | solution.py:526
  66.7 13.2 %collective-permute-start.13 = (f32[16,16,128]{2,1,0:T(8,128)S(1)}, f32[16,16,128]{2,1,0:T(8,128)S(1)}, u32[]{:S(2)}, u32[]{:S(2)}) collective-permute-start(f32[16,16,128]{2,1,0:T(8,128)S(1)} %get-tuple-element.52), channel_id=1, source_target_pairs={{0,1},{1,0},{2,3},{3,2},{4,5},{5,4},{6,7},{7,6},{8,9},{9,8},{10,11... | collective-permute-start | bytes 393224 | tf_op jit(solution)/shard_map/ppermute | solution.py:525
  67.2 12.7 %collective-permute-start.14 = (f32[16,16,128]{2,1,0:T(8,128)S(1)}, f32[16,16,128]{2,1,0:T(8,128)S(1)}, u32[]{:S(2)}, u32[]{:S(2)}) collective-permute-start(f32[16,16,128]{2,1,0:T(8,128)S(1)} %get-tuple-element.53), channel_id=1, source_target_pairs={{1,2},{2,1},{3,4},{4,3},{5,6},{6,5},{9,10},{10,9},{11,12},{12,11},... | collective-permute-start | bytes 393224 | tf_op jit(solution)/shard_map/ppermute | solution.py:526
  88.4 13.2 %collective-permute-start.15 = (f32[16,16,128]{2,1,0:T(8,128)S(1)}, f32[16,16,128]{2,1,0:T(8,128)S(1)}, u32[]{:S(2)}, u32[]{:S(2)}) collective-permute-start(f32[16,16,128]{2,1,0:T(8,128)S(1)} %get-tuple-element.62), channel_id=1, source_target_pairs={{0,1},{1,0},{2,3},{3,2},{4,5},{5,4},{6,7},{7,6},{8,9},{9,8},{10,11... | collective-permute-start | bytes 393224 | tf_op jit(solution)/shard_map/ppermute | solution.py:525
  88.9 12.7 %collective-permute-start.16 = (f32[16,16,128]{2,1,0:T(8,128)S(1)}, f32[16,16,128]{2,1,0:T(8,128)S(1)}, u32[]{:S(2)}, u32[]{:S(2)}) collective-permute-start(f32[16,16,128]{2,1,0:T(8,128)S(1)} %get-tuple-element.63), channel_id=1, source_target_pairs={{1,2},{2,1},{3,4},{4,3},{5,6},{6,5},{9,10},{10,9},{11,12},{12,11},... | collective-permute-start | bytes 393224 | tf_op jit(solution)/shard_map/ppermute | solution.py:526
  110.6 0.7 copy-start
  111.3 9.7 %copy-start.3 = (f32[8,128]{1,0:T(8,128)}, f32[8,128]{1,0:T(8,128)S(1)}, u32[]{:S(2)}) copy-start(f32[8,128]{1,0:T(8,128)S(1)} %get-tuple-element.71.old) | copy-start | bytes 12292

commit v3 on v2

--- a/solution.py
+++ b/solution.py
@@ -7,7 +7,6 @@
 from jax.experimental.pallas import tpu as pltpu
 from jax.sharding import PartitionSpec as P
 
-ITERS = 4
 LEVELS = 4
 COARSE_SWEEPS = 4
 K = 16
@@ -90,13 +89,15 @@
 
 
 def setup_kernel(place, prior, outer, *refs):
-    rows = (len(refs) - 7) // 3
+    rows = (len(refs) - 8) // 3
     g_own, g_left, g_right = (refs[i * rows : (i + 1) * rows] for i in range(3))
-    blocks, inverse, rhs, weights, pieces, coarse_blocks, work = refs[3 * rows :]
+    blocks, inverse, rhs, prior_rows, weights, pieces, coarse_blocks, work = refs[3 * rows :]
     width = rhs.shape[-1]
     groups = width // 128
     lane = lanes_of((K, 128))
     even = place[1] % 2 == 0
+    channel = lax.broadcasted_iota(jnp.int32, (K, width), 0)
+    prior_rows[...] = sum(jnp.where(channel == k, prior[k], 0.0) for k in range(K))
 
     def store_pieces(slot, group, rest):
         cols = pl.ds((slot % 2) * 128, 128)
@@ -255,7 +256,7 @@
     width = b[0].shape[-1]
     lane = lanes_of((K, width))
     above, below = lane >= SEGMENT, lane < width - SEGMENT
-    weight = [jnp.broadcast_to(prior[...] * 2.0**m, (K, width)) for m in range(LEVELS)]
+    weight = [prior[...] * 2.0**m for m in range(LEVELS)]
 
     def sweep(m, keep=None):
         n = SIDES[m]
@@ -303,57 +304,116 @@
         sweep(m)
 
 
-def iterate_kernel(step, last, *refs):
+def dots(rows, width, mine):
+    totals = [jnp.zeros((K, width), f32) for _ in rows]
+    for at in range(COUNTS[0]):
+        for i, (one, other) in enumerate(rows):
+            totals[i] = totals[i] + one[at] * other[at]
+    lines = []
+    for total in totals:
+        total = jnp.sum(jnp.where(mine, total, 0.0), axis=0, keepdims=True)
+        lines.append(sum(total[:, g * 128 : (g + 1) * 128] for g in range(width // 128)))
+    if len(rows) % 8:
+        lines.append(jnp.zeros((-len(rows) % 8, 128), f32))
+    return jnp.concatenate(lines, axis=0)
+
+
+def summed(sums):
+    total = sums[0]
+    for i in range(1, sums.shape[0]):
+        total = total + sums[i]
+    total = jnp.sum(total, axis=1, keepdims=True)
+    return [total[i : i + 1] for i in range(total.shape[0])]
+
+
+def kept_apart(energy, whole):
+    return jnp.maximum(energy, 1e-7 * whole)
+
+
+def first_pair(sums):
+    g0, g1, e00, e01, e11 = summed(sums)[:5]
+    ratio = e01 / e00
+    energy = kept_apart(e11 - ratio * e01, e11)
+    return e00, energy, ratio, g0 / e00, (g1 - ratio * g0) / energy
+
+
+def second_pair(sums, e0, e1):
+    h0, h1, h2, h3, a20, a21, a22, a30, a31, a32, a33 = summed(sums)[:11]
+    l20, l21, l30, l31 = a20 / e0, a21 / e1, a30 / e0, a31 / e1
+    e2 = kept_apart(a22 - l20 * a20 - l21 * a21, a22)
+    cross = a32 - l20 * a30 - l21 * a31
+    l32 = cross / e2
+    e3 = kept_apart(a33 - l30 * a30 - l31 * a31 - l32 * cross, a33)
+    n2 = h2 - l20 * h0 - l21 * h1
+    n3 = h3 - l30 * h0 - l31 * h1 - l32 * n2
+    c3 = n3 / e3
+    c2 = n2 / e2 - l32 * c3
+    return h0 / e0 - l20 * c2 - l30 * c3, h1 / e1 - l21 * c2 - l31 * c3, c2, c3
+
+
+def iterate_kernel(step, *refs):
     refs = list(refs)
-    place, prior, blocks, inverse, residual_in = (refs.pop(0) for _ in range(5))
-    if step > 0:
-        sums, edge_a, edge_b, z_in, az_in = (refs.pop(0) for _ in range(5))
-    if step > 1:
-        old, x_in, p_in, ap_in = (refs.pop(0) for _ in range(4))
-    if last:
-        parts, scalars, packed, residual, x, p, ap, z_out, az_out = (refs.pop(0) for _ in range(9))
+    take = lambda n: [refs.pop(0) for _ in range(n)]
+    place, prior, blocks, inverse, rhs = take(5)
+    if step == 0:
+        z0, az0, send_a, send_b = take(4)
+        z, az = z0, az0
+    elif step == 1:
+        edge_a, edge_b, z0, az0, parts, full, w1, aw1, send_a, send_b = take(10)
+        z, az = w1, aw1
+    elif step == 2:
+        sums, edge_a, edge_b, z0, az0, w1, aw1 = take(7)
+        scalars, p1, ap1, left_over, z2, az2, send_a, send_b = take(8)
+        z, az = z2, az2
     else:
-        parts, z_out, az_out, send_a, send_b = (refs.pop(0) for _ in range(5))
-        if step > 0:
-            scalars, residual, x, p, ap = (refs.pop(0) for _ in range(5))
-    b, v, d, w = (refs[i * LEVELS : (i + 1) * LEVELS] for i in range(4))
-    width = z_out.shape[-1]
+        edge_a, edge_b, z0, az0, p1, ap1, z2, az2 = take(8)
+        parts, packed, w3, aw3 = take(4)
+        z, az = w3, aw3
+    b, v, d, w = (take(LEVELS) for _ in range(4))
+    width = z.shape[-1]
     lane = lanes_of((K, width))
     column = lane % SEGMENT
     mine = (column >= HALO) & (column < HALO + OWN)
     even = place[1] % 2 == 0
     count = COUNTS[0]
-    if step > 0:
-        gamma, alpha, beta, energy = coefficients(sums, old if step > 1 else None)
-        scalars[...] = jnp.concatenate(
-            [jnp.broadcast_to(gamma, (1, 128)), jnp.broadcast_to(energy, (1, 128)), jnp.zeros((6, 128), f32)], axis=0
-        )
+
+    def arrived(own):
         left_side, right_side = column < HALO, column >= HALO + OWN
         for i in range(count // 4):
             left = jnp.where(even, edge_b[i], edge_a[i])
             right = jnp.where(even, edge_a[i], edge_b[i])
             for g in range(4):
                 at = 4 * i + g
-                image = jnp.where(left_side, roll(left, -HALO * g), az_in[at])
-                image = jnp.where(right_side, roll(right, SEGMENT - HALO - HALO * g), image)
-                direction = z_in[at]
-                if step > 1:
-                    direction = direction + beta * p_in[at]
-                    image = image + beta * ap_in[at]
-                p[at] = direction
-                ap[at] = image
-                x[at] = x_in[at] + alpha * direction if step > 1 else alpha * direction
-                left_over = residual_in[at] - alpha * image
-                residual[at] = left_over
-                b[0][at] = left_over
+                value = jnp.where(left_side, roll(left, -HALO * g), own[at])
+                yield at, jnp.where(right_side, roll(right, SEGMENT - HALO - HALO * g), value)
+
+    if step == 0:
+        for at in range(count):
+            b[0][at] = rhs[at]
+    elif step == 1:
+        for at, image in arrived(az0):
+            full[at] = image
+            b[0][at] = rhs[at] - image
+    elif step == 2:
+        e0, e1, ratio, c0, c1 = first_pair(sums)
+        rows = [jnp.broadcast_to(x, (1, 128)) for x in (e0, e1, c0, c1)]
+        scalars[...] = jnp.concatenate(rows + [jnp.zeros((4, 128), f32)], axis=0)
+        for at, image in arrived(aw1):
+            first = az0[at]
+            image = image - ratio * first
+            ap1[at] = image
+            p1[at] = w1[at] - ratio * z0[at]
+            value = rhs[at] - c0 * first - c1 * image
+            left_over[at] = value
+            b[0][at] = value
     else:
-        for at in range(count):
-            b[0][at] = residual_in[at]
+        for at, image in arrived(az2):
+            b[0][at] = rhs[at] - image
 
     v_cycle(inverse, prior, b, v, d, w)
 
     above, below = lane >= SEGMENT, lane < width - SEGMENT
-    weight = jnp.broadcast_to(prior[...], (K, width))
+    weight = prior[...]
     n = SIDES[0]
     for s in range(n):
         for t in range(n):
@@ -361,30 +421,23 @@
             w[0][s * n + t] = weight * (4.0 * v[0][s * n + t] - near)
 
     def finish(i, cols, total):
-        az_out[i, :, cols] = total + w[0][i, :, cols]
-        z_out[i, :, cols] = v[0][i, :, cols]
+        az[i, :, cols] = total + w[0][i, :, cols]
+        z[i, :, cols] = v[0][i, :, cols]
 
     block_product(blocks, 0, count, v[0], finish)
 
-    names = 3 if step > 0 else 2
-    totals = [jnp.zeros((K, width), f32) for _ in range(names)]
-    for at in range(count):
-        z = z_out[at]
-        totals[0] = totals[0] + z * b[0][at]
-        totals[1] = totals[1] + z * az_out[at]
-        if step > 0:
-            totals[2] = totals[2] + z * ap[at]
-    rows = []
-    for total in totals:
-        total = jnp.sum(jnp.where(mine, total, 0.0), axis=0, keepdims=True)
-        rows.append(sum(total[:, g * 128 : (g + 1) * 128] for g in range(width // 128)))
-    rows.append(jnp.zeros((8 - names, 128), f32))
-    tile = jnp.concatenate(rows, axis=0)
-    for i in range(parts.shape[0]):
-        parts[i] = tile
-    if last:
+    if step == 1:
+        tile = dots([(z0, rhs), (w1, rhs), (z0, az0), (w1, az0), (w1, aw1)], width, mine)
+    elif step == 3:
+        pairs = [(z0, rhs), (p1, rhs), (z2, rhs), (w3, rhs)]
+        pairs += [(z2, az0), (z2, ap1), (z2, az2), (w3, az0), (w3, ap1), (w3, az2), (w3, aw3)]
+        tile = dots(pairs, width, mine)
+    if step % 2:
+        for i in range(parts.shape[0]):
+            parts[i] = tile
+    if step == 3:
         tile = refs[-1]
-        for i, source in enumerate((x, z_out, p)):
+        for i, source in enumerate((z0, p1, z2, w3)):
             pack(place, source, tile)
             back = lax.dot_general(
                 tile[...], lane_order(), (((1,), (1,)), ((), ())), precision=highest, preferred_element_type=f32
@@ -394,26 +447,13 @@
         for i in range(count // 4):
             left, right = None, None
             for g in range(4):
-                value = az_out[4 * i + g]
+                value = az[4 * i + g]
                 low, high = roll(value, HALO * g - HALO), roll(value, HALO * g - OWN)
                 here = (column >= HALO * g) & (column < HALO * g + HALO)
                 left = low if left is None else jnp.where(here, low, left)
                 right = high if right is None else jnp.where(here, high, right)
             send_a[i] = jnp.where(even, right, left)
             send_b[i] = jnp.where(even, left, right)
-
-
-def coefficients(sums, old):
-    total = sums[0]
-    for i in range(1, sums.shape[0]):
-        total = total + sums[i]
-    total = jnp.sum(total, axis=1, keepdims=True)
-    gamma, energy = total[0:1], total[1:2]
-    beta = None
-    if old is not None:
-        beta = gamma / old[0:1, 0:1]
-        energy = energy + beta * (2.0 * total[2:3] + beta * old[1:2, 0:1])
-    return gamma, gamma / energy, beta, energy
 
 
 def pack(place, source, tile):
@@ -428,11 +468,12 @@
         tile[pl.ds(t, K, stride=BLOCK), :] = packed
 
 
-def finish_kernel(sums, old, packed, out):
-    _, alpha, beta, _ = coefficients(sums, old)
-    alpha, beta = jnp.broadcast_to(alpha, (BLOCK, 128)), jnp.broadcast_to(beta, (BLOCK, 128))
+def finish_kernel(sums, scalars, packed, out):
+    e0, e1, c0, c1 = (scalars[i : i + 1, 0:1] for i in range(4))
+    d0, d1, d2, d3 = second_pair(sums, e0, e1)
+    factors = [jnp.broadcast_to(x, (BLOCK, 128)) for x in (c0 + d0, c1 + d1, d2, d3)]
     for k in range(K):
-        out[k] = packed[0, k] + alpha * (packed[1, k] + beta * packed[2, k])
+        out[k] = sum(factors[i] * packed[i, k] for i in range(4))
 
 
 def gather(value):
@@ -477,14 +518,13 @@
         parts.append(part)
         rest = rest - part
     outer = jnp.concatenate([parts[a] for a, _ in SPLITS], axis=1).astype(jnp.bfloat16)
-    prior_rows = prior[:, None]
 
     field = shape(COUNTS[0], K, width)
-    blocks, inverse, residual = pl.pallas_call(
+    blocks, inverse, rhs, prior_rows = pl.pallas_call(
         setup_kernel,
-        out_shape=[shape(width // 128, n, ROWS, 128) for n in (COUNTS[0], SLOTS)] + [field],
+        out_shape=[shape(width // 128, n, ROWS, 128) for n in (COUNTS[0], SLOTS)] + [field, shape(K, width)],
         in_specs=[SMEM, SMEM] + [VMEM] * (1 + len(gathered)),
-        out_specs=[VMEM] * 3,
+        out_specs=[VMEM] * 4,
         scratch_shapes=[
             pltpu.VMEM((SLOTS, K, width), f32),
             pltpu.VMEM((width // 128, SLOTS // 2, len(SPLITS) * K, 256), jnp.bfloat16),
@@ -498,43 +538,54 @@
     levels = [pltpu.VMEM((n, K, width), f32) for n in COUNTS] * 4
     whole = pltpu.VMEM((COUNTS[0], K, width), f32)
     edge = shape(COUNTS[0] // 4, K, width)
-    parts = shape(cols, 8, 128)
-    state = ()
-    for step in range(ITERS):
-        last = step == ITERS - 1
-        operands = (place, prior_rows, blocks, inverse, residual) + state
-        if last:
-            shapes = [parts, shape(8, 128), shape(3, *beta.shape)]
-            scratch = [whole] * 6 + levels + [pltpu.VMEM((K * BLOCK, 128), f32)]
-        else:
-            shapes = [parts, field, field, edge, edge]
-            if step > 0:
-                shapes += [shape(8, 128), field, field, field, field]
-            scratch = levels
-        outs = pl.pallas_call(
-            functools.partial(iterate_kernel, step, last),
+
+    def iterate(step, *operands, shapes, scratch=()):
+        return pl.pallas_call(
+            functools.partial(iterate_kernel, step),
             out_shape=shapes,
-            in_specs=[SMEM] + [VMEM] * (len(operands) - 1),
+            in_specs=[SMEM] + [VMEM] * (len(operands) + 3),
             out_specs=[VMEM] * len(shapes),
-            scratch_shapes=scratch,
+            scratch_shapes=list(scratch[:2]) + levels + list(scratch[2:]),
             compiler_params=params(24 if width == 128 else 60),
             name=f"iterate_{step}",
-        )(*operands)
-        sums = lax.all_to_all(outs[0], "gy", 0, 0, tiled=True)
-        if not last:
-            edge_a = lax.ppermute(outs[3], "gy", pairs)
-            edge_b = lax.ppermute(outs[4], "gy", others)
-            state = (sums, edge_a, edge_b, outs[1], outs[2])
-            if step > 0:
-                residual = outs[6]
-                state += (outs[5], outs[7], outs[8], outs[9])
+        )(place, prior_rows, blocks, inverse, *operands)
+
+    def exchange(edge_a, edge_b):
+        return lax.ppermute(edge_a, "gy", pairs), lax.ppermute(edge_b, "gy", others)
+
+    def total(parts):
+        return lax.all_to_all(parts, "gy", 0, 0, tiled=True)
+
+    z0, az0, *edges = iterate(0, rhs, shapes=[field, field, edge, edge])
+    edges = exchange(*edges)
+    parts, az0, w1, aw1, *edges = iterate(
+        1, rhs, *edges, z0, az0, shapes=[shape(cols, 8, 128), field, field, field, edge, edge]
+    )
+    sums, edges = total(parts), exchange(*edges)
+    scalars, p1, ap1, residual, z2, az2, *edges = iterate(
+        2, rhs, sums, *edges, z0, az0, w1, aw1, shapes=[shape(8, 128)] + [field] * 5 + [edge, edge]
+    )
+    edges = exchange(*edges)
+    parts, packed = iterate(
+        3,
+        residual,
+        *edges,
+        z0,
+        az0,
+        p1,
+        ap1,
+        z2,
+        az2,
+        shapes=[shape(cols, 16, 128), shape(4, *beta.shape)],
+        scratch=[whole, whole, pltpu.VMEM((K * BLOCK, 128), f32)],
+    )
     return pl.pallas_call(
         finish_kernel,
         out_shape=shape(*beta.shape),
         in_specs=[VMEM] * 3,
         out_specs=VMEM,
         name="finish",
-    )(sums, outs[1], outs[2])
+    )(total(parts), scalars, packed)
 
 
 def solution(mesh):

time: 123 us -> 112 us (0.911)
  blocking collectives: 46.8 us -> 27 us
  waiting for transfers between devices: 3.25 us -> 11 us
  starting transfers between devices: 15.8 us -> 20.1 us
  Pallas kernels: 51.6 us -> 48.7 us
    all_to_all x4 -> x2, blocking collectives: 46.8 us -> 27 us  [total(): return lax.all_to_all(parts, 'gy', 0, 0, tiled=True)]
    ppermute x6, waiting for transfers between devices: 0.02 us -> 7.01 us  [the longest x3 7.01 us: exchange(): lax.ppermute(edge_a, 'gy', pairs)]
    ppermute x6, starting transfers between devices: 7.31 us -> 11.7 us  [the longest x3 9.52 us: exchange(): lax.ppermute(edge_a, 'gy', pairs)]
    pallas_call x4, Pallas kernels: 33.9 us -> 31.1 us  [iterate(): pl.pallas_call(functools.partial(iterate_kernel, step), out_shape=shapes,...]
  transfers between devices with their start and end apart: 17 -> 17, of which waited for: 2 -> 6; matrix products, arithmetic and copies ran while one was open for 1% -> 1% of each run, Pallas kernels for 0% -> 0%
where the time goes in v3:
time: 112 us; the launch traced here: 111 us
  Pallas kernels  48.7 us (43%)
  blocking collectives  27 us (24%)
  starting transfers between devices  20.1 us (18%)
  waiting for transfers between devices  11 us (10%)
  local copies, waits for them, and re-layouts  3.88 us (3%)
    pallas_call x4, Pallas kernels, iterate(): pl.pallas_call(functools.partial(iterate_kernel, step), out_shape=shapes,...  31.1 us
    all_to_all x2, blocking collectives, total(): return lax.all_to_all(parts, 'gy', 0, 0, tiled=True)  27 us
    pallas_call x1, Pallas kernels, local(): pl.pallas_call(setup_kernel, out_shape=[shape(width // 128, n, ROWS, 128)...  13.6 us
    ppermute x3, starting transfers between devices, exchange(): lax.ppermute(edge_a, 'gy', pairs)  9.52 us
    ppermute x3, waiting for transfers between devices, exchange(): lax.ppermute(edge_a, 'gy', pairs)  7.01 us
    ppermute x9, starting transfers between devices, gather(): held[o ^ bit] = lax.ppermute(held[o], 'gx', pairs)  4.86 us
    ppermute x9, waiting for transfers between devices, gather(): held[o ^ bit] = lax.ppermute(held[o], 'gx', pairs)  3.95 us
    unnamed x11, local copies, waits for them, and re-layouts  3.69 us
  transfers between devices with their start and end apart: 17, of which 6 were waited for; matrix products, arithmetic and copies ran while one was open for 1% of the time, Pallas kernels for 0%

profile of v3, /device:TPU:0, one launch (start us, length us, event | category | flops | bytes accessed | tf_op | source)
XLA Modules:
  0.0 111.4 jit_solution(17509679998978324941)
XLA Ops:
  0.6 2.2 %prepare.1 = (f32[2,8,16,128]{3,2,1,0:T(8,128)}, f32[2,4,16,128]{3,2,1,0:T(8,128)}, f32[2,4,16,128]{3,2,1,0:T(8,128)}) custom-call(s32[3]{0:T(128)} %pad_add_fusion.place.refs_0_, f32[16,16]{1,0:T(8,128)} %design.1, f32[16,8,128]{2,1,0:T(8,128)} %beta.1, s32[16,8,128]{2,1,0:T(8,128)} %kept.1, s32[16,8,128]{2,1,0:T(8,128)} %removed.1, s32[16,8,128]{2,1,0:T(8,128)} %labels.1), custom_call_target="tpu_custom_call" | custom-call | tf_op jit(solution)/shard_map/prepare/pallas_call | solution.py:502
  2.8 2.9 %collective-permute-start.3 = (f32[2,4,16,128]{3,2,1,0:T(8,128)}, f32[2,4,16,128]{3,2,1,0:T(8,128)S(1)}, u32[]{:S(2)}, u32[]{:S(2)}) collective-permute-start(f32[2,4,16,128]{3,2,1,0:T(8,128)} %get-tuple-element.33), channel_id=1, source_target_pairs={{0,1},{1,0},{2,3},{3,2},{4,5},{5,4},{6,7},{7,6},{8,9},{9,8},{10,11... | collective-permute-start | bytes 196616 | tf_op jit(solution)/shard_map/ppermute | solution.py:510
  6.4 1.6 %collective-permute-start.1 = (f32[2,8,16,128]{3,2,1,0:T(8,128)}, f32[2,8,16,128]{3,2,1,0:T(8,128)S(1)}, u32[]{:S(2)}, u32[]{:S(2)}) collective-permute-start(f32[2,8,16,128]{3,2,1,0:T(8,128)} %get-tuple-element.32.refs_0_), channel_id=1, source_target_pairs={{0,16},{8,24},{16,0},{24,8},{1,17},{9,25},{17,1},{25,9},{2,18},{10... | collective-permute-start | bytes 393224 | tf_op jit(solution)/shard_map/ppermute | solution.py:486
  8.0 0.8 copy.9
  8.8 1.5 %collective-permute-start.5 = (f32[2,4,16,128]{3,2,1,0:T(8,128)S(1)}, f32[2,4,16,128]{3,2,1,0:T(8,128)S(1)}, u32[]{:S(2)}, u32[]{:S(2)}) collective-permute-start(f32[2,4,16,128]{3,2,1,0:T(8,128)S(1)} %collective-permute-done.3.refs_4_), channel_id=1, source_target_pairs={{0,16},{8,24},{16,0},{24,8},{1,17},{9,25},{17,1},{25,9},{2,18},{10... | collective-permute-start | bytes 196616 | tf_op jit(solution)/shard_map/ppermute | solution.py:486
  10.3 0.8 collective-permute-start.9
  11.1 2.2 %collective-permute-done.5.refs_6_ = f32[2,4,16,128]{3,2,1,0:T(8,128)S(1)} collective-permute-done((f32[2,4,16,128]{3,2,1,0:T(8,128)S(1)}, f32[2,4,16,128]{3,2,1,0:T(8,128)S(1)}, u32[]{:S(2)}, u32[]{:S(2)}) %collective-permute-start.5) | collective-permute-done | bytes 65568 | tf_op jit(solution)/shard_map/ppermute | solution.py:486
  13.8 1.0 collective-permute-done.9.refs_10_
  16.3 0.9 copy-done.1
  18.5 13.6 %setup.1 = (f32[1,64,264,128]{3,2,1,0:T(8,128)S(1)}, f32[1,88,264,128]{3,2,1,0:T(8,128)S(1)}, f32[64,16,128]{2,1,0:T(8,128)S(1)}, f32[16,128]{1,0:T(8,128)S(1)}) custom-call(s32[3]{0:T(128)S(1)} %copy-done.2, f32[16]{0:T(128)S(1)} %copy-done.4, bf16[256,96]{1,0:T(8,128)(2,1)S(1)} %concatenate.4.outer, f32[2,8,16,128]{3,2,1,0:T(8,128)S(1)} %copy-done.1, ...), custom_call_target="tpu_custom_call" | custom-call | tf_op jit(solution)/shard_map/setup/pallas_call | solution.py:523
  32.1 7.3 %iterate_0.1 = (f32[64,16,128]{2,1,0:T(8,128)S(1)}, f32[64,16,128]{2,1,0:T(8,128)S(1)}, f32[16,16,128]{2,1,0:T(8,128)S(1)}, f32[16,16,128]{2,1,0:T(8,128)S(1)}) custom-call(s32[3]{0:T(128)S(1)} %copy-done.2, f32[16,128]{1,0:T(8,128)S(1)} %get-tuple-element.35.refs_1_, f32[1,64,264,128]{3,2,1,0:T(8,128)S(1)} %get-tuple-element.36.refs_2_, ...), custom_call_target="tpu_custom_call" | custom-call | tf_op jit(solution)/shard_map/iterate_0/pallas_call | solution.py:543
  39.4 4.3 %collective-permute-start.11 = (f32[16,16,128]{2,1,0:T(8,128)S(1)}, f32[16,16,128]{2,1,0:T(8,128)S(1)}, u32[]{:S(2)}, u32[]{:S(2)}) collective-permute-start(f32[16,16,128]{2,1,0:T(8,128)S(1)} %get-tuple-element.39), channel_id=1, source_target_pairs={{0,1},{1,0},{2,3},{3,2},{4,5},{5,4},{6,7},{7,6},{8,9},{9,8},{10,11... | collective-permute-start | bytes 393224 | tf_op jit(solution)/shard_map/ppermute | solution.py:554
  43.7 0.8 collective-permute-start.12
  44.5 3.2 %collective-permute-done.11.refs_5_ = f32[16,16,128]{2,1,0:T(8,128)S(1)} collective-permute-done((f32[16,16,128]{2,1,0:T(8,128)S(1)}, f32[16,16,128]{2,1,0:T(8,128)S(1)}, u32[]{:S(2)}, u32[]{:S(2)}) %collective-permute-start.11) | collective-permute-done | bytes 131104 | tf_op jit(solution)/shard_map/ppermute | solution.py:554
  47.7 7.6 %iterate_1.1 = (f32[8,8,128]{2,1,0:T(8,128)S(1)}, f32[64,16,128]{2,1,0:T(8,128)S(1)}, f32[64,16,128]{2,1,0:T(8,128)S(1)}, f32[64,16,128]{2,1,0:T(8,128)S(1)}, f3...) custom-call(s32[3]{0:T(128)S(1)} %copy-done.2, f32[16,128]{1,0:T(8,128)S(1)} %get-tuple-element.35.refs_1_, ...), custom_call_target="tpu_custom_call" | custom-call | tf_op jit(solution)/shard_map/iterate_1/pallas_call | solution.py:543
  55.3 4.7 %collective-permute-start.13 = (f32[16,16,128]{2,1,0:T(8,128)S(1)}, f32[16,16,128]{2,1,0:T(8,128)S(1)}, u32[]{:S(2)}, u32[]{:S(2)}) collective-permute-start(f32[16,16,128]{2,1,0:T(8,128)S(1)} %get-tuple-element.44), channel_id=1, source_target_pairs={{0,1},{1,0},{2,3},{3,2},{4,5},{5,4},{6,7},{7,6},{8,9},{9,8},{10,11... | collective-permute-start | bytes 393224 | tf_op jit(solution)/shard_map/ppermute | solution.py:554
  60.0 0.7 collective-permute-start.14
  60.6 14.1 %all_to_all.10.refs_5_ = f32[8,8,128]{2,1,0:T(8,128)S(1)} all-to-all(f32[8,8,128]{2,1,0:T(8,128)S(1)} %get-tuple-element.43), channel_id=1, replica_groups=mesh['gx'=4,'gy'=8] {'gy'}, dimensions={0} | all-to-all | bytes 65536 | tf_op jit(solution)/shard_map/all_to_all | solution.py:557
  74.8 7.6 %iterate_2.1 = (f32[8,128]{1,0:T(8,128)S(1)}, f32[64,16,128]{2,1,0:T(8,128)S(1)}, f32[64,16,128]{2,1,0:T(8,128)S(1)}, f32[64,16,128]{2,1,0:T(8,128)S(1)}, f32[64...) custom-call(s32[3]{0:T(128)S(1)} %copy-done.2, ...), custom_call_target="tpu_custom_call" | custom-call | tf_op jit(solution)/shard_map/iterate_2/pallas_call | solution.py:543
  83.6 3.8 %collective-permute-done.15.refs_5_ = f32[16,16,128]{2,1,0:T(8,128)S(1)} collective-permute-done((f32[16,16,128]{2,1,0:T(8,128)S(1)}, f32[16,16,128]{2,1,0:T(8,128)S(1)}, u32[]{:S(2)}, u32[]{:S(2)}) %collective-permute-start.15) | collective-permute-done | bytes 131104 | tf_op jit(solution)/shard_map/ppermute | solution.py:554
  87.4 8.6 %iterate_3.1 = (f32[8,16,128]{2,1,0:T(8,128)S(1)}, f32[4,16,8,128]{3,2,1,0:T(8,128)S(1)}) custom-call(s32[3]{0:T(128)S(1)} %copy-done.2, f32[16,128]{1,0:T(8,128)S(1)} %get-tuple-element.35.refs_1_, f32[1,64,264,128]{3,2,1,0:T(8,128)S(1)} %get-tuple-element.36.refs_2_, f32[1,88,264,128]{3,2,1,0:T(8,128)S(1)} %get-tuple-element.37.refs_3_, ...), custom_call_target="tpu_custom_call" | custom-call | tf_op jit(solution)/shard_map/iterate_3/pallas_call | solution.py:543
  96.1 0.7 copy-done
  96.8 12.9 %all_to_all.11.sums = f32[8,16,128]{2,1,0:T(8,128)} all-to-all(f32[8,16,128]{2,1,0:T(8,128)S(1)} %get-tuple-element.56), channel_id=1, replica_groups=mesh['gx'=4,'gy'=8] {'gy'}, dimensions={0} | all-to-all | bytes 131072 | tf_op jit(solution)/shard_map/all_to_all | solution.py:557
  109.6 1.8 %finish.1 = f32[16,8,128]{2,1,0:T(8,128)} custom-call(f32[8,16,128]{2,1,0:T(8,128)} %all_to_all.11.sums, f32[8,128]{1,0:T(8,128)} %copy-done.3, f32[4,16,8,128]{3,2,1,0:T(8,128)} %copy-done), custom_call_target="tpu_custom_call" | custom-call | tf_op jit(solution)/shard_map/finish/pallas_call | solution.py:582
  (34 shorter events, 5.8 us)
Async XLA Ops:
  2.8 6.0 %collective-permute-start.3 = (f32[2,4,16,128]{3,2,1,0:T(8,128)}, f32[2,4,16,128]{3,2,1,0:T(8,128)S(1)}, u32[]{:S(2)}, u32[]{:S(2)}) collective-permute-start(f32[2,4,16,128]{3,2,1,0:T(8,128)} %get-tuple-element.33), channel_id=1, source_target_pairs={{0,1},{1,0},{2,3},{3,2},{4,5},{5,4},{6,7},{7,6},{8,9},{9,8},{10,11... | collective-permute-start | bytes 196616 | tf_op jit(solution)/shard_map/ppermute | solution.py:510
  5.8 4.5 %collective-permute-start.7 = (f32[2,4,16,128]{3,2,1,0:T(8,128)}, f32[2,4,16,128]{3,2,1,0:T(8,128)S(1)}, u32[]{:S(2)}, u32[]{:S(2)}) collective-permute-start(f32[2,4,16,128]{3,2,1,0:T(8,128)} %get-tuple-element.34), channel_id=1, source_target_pairs={{1,2},{2,1},{3,4},{4,3},{5,6},{6,5},{9,10},{10,9},{11,12},{12,11},... | collective-permute-start | bytes 196616 | tf_op jit(solution)/shard_map/ppermute | solution.py:511
  6.4 8.4 %collective-permute-start.1 = (f32[2,8,16,128]{3,2,1,0:T(8,128)}, f32[2,8,16,128]{3,2,1,0:T(8,128)S(1)}, u32[]{:S(2)}, u32[]{:S(2)}) collective-permute-start(f32[2,8,16,128]{3,2,1,0:T(8,128)} %get-tuple-element.32.refs_0_), channel_id=1, source_target_pairs={{0,16},{8,24},{16,0},{24,8},{1,17},{9,25},{17,1},{25,9},{2,18},{10... | collective-permute-start | bytes 393224 | tf_op jit(solution)/shard_map/ppermute | solution.py:486
  8.0 7.5 %collective-permute-start = (f32[2,8,16,128]{3,2,1,0:T(8,128)}, f32[2,8,16,128]{3,2,1,0:T(8,128)S(1)}, u32[]{:S(2)}, u32[]{:S(2)}) collective-permute-start(f32[2,8,16,128]{3,2,1,0:T(8,128)} %get-tuple-element.32.refs_0_), channel_id=1, source_target_pairs={{0,8},{8,0},{16,24},{24,16},{1,9},{9,1},{17,25},{25,17},{2,10},{10... | collective-permute-start | bytes 393224 | tf_op jit(solution)/shard_map/ppermute | solution.py:486
  8.8 4.5 %collective-permute-start.5 = (f32[2,4,16,128]{3,2,1,0:T(8,128)S(1)}, f32[2,4,16,128]{3,2,1,0:T(8,128)S(1)}, u32[]{:S(2)}, u32[]{:S(2)}) collective-permute-start(f32[2,4,16,128]{3,2,1,0:T(8,128)S(1)} %collective-permute-done.3.refs_4_), channel_id=1, source_target_pairs={{0,16},{8,24},{16,0},{24,8},{1,17},{9,25},{17,1},{25,9},{2,18},{10... | collective-permute-start | bytes 196616 | tf_op jit(solution)/shard_map/ppermute | solution.py:486
  10.3 3.0 %collective-permute-start.4 = (f32[2,4,16,128]{3,2,1,0:T(8,128)S(1)}, f32[2,4,16,128]{3,2,1,0:T(8,128)S(1)}, u32[]{:S(2)}, u32[]{:S(2)}) collective-permute-start(f32[2,4,16,128]{3,2,1,0:T(8,128)S(1)} %collective-permute-done.3.refs_4_), channel_id=1, source_target_pairs={{0,8},{8,0},{16,24},{24,16},{1,9},{9,1},{17,25},{25,17},{2,10},{10... | collective-permute-start | bytes 196616 | tf_op jit(solution)/shard_map/ppermute | solution.py:486
  10.3 4.5 %collective-permute-start.9 = (f32[2,4,16,128]{3,2,1,0:T(8,128)S(1)}, f32[2,4,16,128]{3,2,1,0:T(8,128)S(1)}, u32[]{:S(2)}, u32[]{:S(2)}) collective-permute-start(f32[2,4,16,128]{3,2,1,0:T(8,128)S(1)} %collective-permute-done.7.refs_8_), channel_id=1, source_target_pairs={{0,16},{8,24},{16,0},{24,8},{1,17},{9,25},{17,1},{25,9},{2,18},{10... | collective-permute-start | bytes 196616 | tf_op jit(solution)/shard_map/ppermute | solution.py:486
  13.3 2.2 %collective-permute-start.8 = (f32[2,4,16,128]{3,2,1,0:T(8,128)S(1)}, f32[2,4,16,128]{3,2,1,0:T(8,128)S(1)}, u32[]{:S(2)}, u32[]{:S(2)}) collective-permute-start(f32[2,4,16,128]{3,2,1,0:T(8,128)S(1)} %collective-permute-done.7.refs_8_), channel_id=1, source_target_pairs={{0,8},{8,0},{16,24},{24,16},{1,9},{9,1},{17,25},{25,17},{2,10},{10... | collective-permute-start | bytes 196616 | tf_op jit(solution)/shard_map/ppermute | solution.py:486
  13.3 2.3 %collective-permute-start.6 = (f32[2,4,16,128]{3,2,1,0:T(8,128)S(1)}, f32[2,4,16,128]{3,2,1,0:T(8,128)S(1)}, u32[]{:S(2)}, u32[]{:S(2)}) collective-permute-start(f32[2,4,16,128]{3,2,1,0:T(8,128)S(1)} %collective-permute-done.5.refs_6_), channel_id=1, source_target_pairs={{0,8},{8,0},{16,24},{24,16},{1,9},{9,1},{17,25},{25,17},{2,10},{10... | collective-permute-start | bytes 196616 | tf_op jit(solution)/shard_map/ppermute | solution.py:486
  14.8 1.3 %collective-permute-start.10 = (f32[2,4,16,128]{3,2,1,0:T(8,128)S(1)}, f32[2,4,16,128]{3,2,1,0:T(8,128)S(1)}, u32[]{:S(2)}, u32[]{:S(2)}) collective-permute-start(f32[2,4,16,128]{3,2,1,0:T(8,128)S(1)} %collective-permute-done.9.refs_10_), channel_id=1, source_target_pairs={{0,8},{8,0},{16,24},{24,16},{1,9},{9,1},{17,25},{25,17},{2,10},{10... | collective-permute-start | bytes 196616 | tf_op jit(solution)/shard_map/ppermute | solution.py:486
  14.8 1.5 %collective-permute-start.2 = (f32[2,8,16,128]{3,2,1,0:T(8,128)S(1)}, f32[2,8,16,128]{3,2,1,0:T(8,128)S(1)}, u32[]{:S(2)}, u32[]{:S(2)}) collective-permute-start(f32[2,8,16,128]{3,2,1,0:T(8,128)S(1)} %collective-permute-done.1.refs_2_), channel_id=1, source_target_pairs={{0,8},{8,0},{16,24},{24,16},{1,9},{9,1},{17,25},{25,17},{2,10},{10... | collective-permute-start | bytes 393224 | tf_op jit(solution)/shard_map/ppermute | solution.py:486
  16.3 0.9 copy-start.1
  17.2 0.7 copy-start.2
  17.8 0.7 copy-start.4
  39.4 8.3 %collective-permute-start.11 = (f32[16,16,128]{2,1,0:T(8,128)S(1)}, f32[16,16,128]{2,1,0:T(8,128)S(1)}, u32[]{:S(2)}, u32[]{:S(2)}) collective-permute-start(f32[16,16,128]{2,1,0:T(8,128)S(1)} %get-tuple-element.39), channel_id=1, source_target_pairs={{0,1},{1,0},{2,3},{3,2},{4,5},{5,4},{6,7},{7,6},{8,9},{9,8},{10,11... | collective-permute-start | bytes 393224 | tf_op jit(solution)/shard_map/ppermute | solution.py:554
  43.7 4.0 %collective-permute-start.12 = (f32[16,16,128]{2,1,0:T(8,128)S(1)}, f32[16,16,128]{2,1,0:T(8,128)S(1)}, u32[]{:S(2)}, u32[]{:S(2)}) collective-permute-start(f32[16,16,128]{2,1,0:T(8,128)S(1)} %get-tuple-element.40), channel_id=1, source_target_pairs={{1,2},{2,1},{3,4},{4,3},{5,6},{6,5},{9,10},{10,9},{11,12},{12,11},... | collective-permute-start | bytes 393224 | tf_op jit(solution)/shard_map/ppermute | solution.py:554
  55.3 19.5 %collective-permute-start.13 = (f32[16,16,128]{2,1,0:T(8,128)S(1)}, f32[16,16,128]{2,1,0:T(8,128)S(1)}, u32[]{:S(2)}, u32[]{:S(2)}) collective-permute-start(f32[16,16,128]{2,1,0:T(8,128)S(1)} %get-tuple-element.44), channel_id=1, source_target_pairs={{0,1},{1,0},{2,3},{3,2},{4,5},{5,4},{6,7},{7,6},{8,9},{9,8},{10,11... | collective-permute-start | bytes 393224 | tf_op jit(solution)/shard_map/ppermute | solution.py:554
  60.0 14.8 %collective-permute-start.14 = (f32[16,16,128]{2,1,0:T(8,128)S(1)}, f32[16,16,128]{2,1,0:T(8,128)S(1)}, u32[]{:S(2)}, u32[]{:S(2)}) collective-permute-start(f32[16,16,128]{2,1,0:T(8,128)S(1)} %get-tuple-element.45), channel_id=1, source_target_pairs={{1,2},{2,1},{3,4},{4,3},{5,6},{6,5},{9,10},{10,9},{11,12},{12,11},... | collective-permute-start | bytes 393224 | tf_op jit(solution)/shard_map/ppermute | solution.py:554
  82.4 13.7 %copy-start.3 = (f32[8,128]{1,0:T(8,128)}, f32[8,128]{1,0:T(8,128)S(1)}, u32[]{:S(2)}) copy-start(f32[8,128]{1,0:T(8,128)S(1)} %get-tuple-element.57.scalars) | copy-start | bytes 12292
  82.4 5.0 %collective-permute-start.15 = (f32[16,16,128]{2,1,0:T(8,128)S(1)}, f32[16,16,128]{2,1,0:T(8,128)S(1)}, u32[]{:S(2)}, u32[]{:S(2)}) collective-permute-start(f32[16,16,128]{2,1,0:T(8,128)S(1)} %get-tuple-element.50), channel_id=1, source_target_pairs={{0,1},{1,0},{2,3},{3,2},{4,5},{5,4},{6,7},{7,6},{8,9},{9,8},{10,11... | collective-permute-start | bytes 393224 | tf_op jit(solution)/shard_map/ppermute | solution.py:554
  82.9 4.5 %collective-permute-start.16 = (f32[16,16,128]{2,1,0:T(8,128)S(1)}, f32[16,16,128]{2,1,0:T(8,128)S(1)}, u32[]{:S(2)}, u32[]{:S(2)}) collective-permute-start(f32[16,16,128]{2,1,0:T(8,128)S(1)} %get-tuple-element.51), channel_id=1, source_target_pairs={{1,2},{2,1},{3,4},{4,3},{5,6},{6,5},{9,10},{10,9},{11,12},{12,11},... | collective-permute-start | bytes 393224 | tf_op jit(solution)/shard_map/ppermute | solution.py:554
  96.1 0.7 copy-start

commit v4 on v3

--- a/solution.py
+++ b/solution.py
@@ -7,6 +7,7 @@
 from jax.experimental.pallas import tpu as pltpu
 from jax.sharding import PartitionSpec as P
 
+ITERS = 4
 LEVELS = 4
 COARSE_SWEEPS = 4
 K = 16
@@ -24,6 +25,7 @@
 OFFSETS = [sum(COUNTS[:m]) for m in range(LEVELS)]
 SLOTS = -(-sum(COUNTS) // 8) * 8
 ROWS = K * K + 8
+GRAM = [(3, 0), (3, 1), (3, 2), (3, 3)] + [(i, -1) for i in range(ITERS)] + [(i, j) for i in range(3) for j in range(i + 1)]
 SPLITS = ((0, 0), (0, 1), (0, 2), (1, 0), (1, 1), (2, 0))
 
 VMEM = pl.BlockSpec(memory_space=pltpu.VMEM)
@@ -49,7 +51,7 @@
     return (lane == (row % BLOCK) * OWN + row // BLOCK).astype(f32)
 
 
-def prepare_kernel(place, design, beta, kept, removed, labels, own, edge_a, edge_b, tile):
+def prepare_kernel(design, prior, beta, kept, removed, labels, own, held, edge_a, edge_b, prior_rows, tile):
     probs = []
     for j in range(K):
         logit = sum(design[j, k] * beta[k] for k in range(K))
@@ -59,12 +61,15 @@
     for k in range(K):
         tile[pl.ds((K + k) * BLOCK, BLOCK), :] = sum(design[j, k] * probs[j] for j in range(K))
     tile[...] = jnp.dot(tile[...], lane_order(), precision=highest, preferred_element_type=f32)
-    even = place[1] % 2 == 0
+    channel = lax.broadcasted_iota(jnp.int32, prior_rows.shape, 0)
+    prior_rows[...] = sum(jnp.where(channel == k, prior[k], 0.0) for k in range(K))
+    even = lax.axis_index("gy") % 2 == 0
     low = lanes_of((K, 128)) % OWN < HALO
     for f in range(2):
         rows = [tile[pl.ds(f * K * BLOCK + t, K, stride=BLOCK), :] for t in range(BLOCK)]
         for t in range(BLOCK):
             own[f, t] = rows[t]
+            held[f, t] = rows[t]
         for i in range(BLOCK // 2):
             left = jnp.where(low, rows[2 * i], roll(rows[2 * i + 1], HALO))
             right = jnp.where(low, roll(rows[2 * i], -HALO), rows[2 * i + 1])
@@ -88,16 +93,15 @@
     return {ij: -x for ij, x in a.items()}
 
 
-def setup_kernel(place, prior, outer, *refs):
-    rows = (len(refs) - 8) // 3
+def setup_kernel(outer, prior_rows, *refs):
+    rows = (len(refs) - 7) // 3
     g_own, g_left, g_right = (refs[i * rows : (i + 1) * rows] for i in range(3))
-    blocks, inverse, rhs, prior_rows, weights, pieces, coarse_blocks, work = refs[3 * rows :]
+    blocks, inverse, rhs, weights, pieces, coarse_blocks, work = refs[3 * rows :]
+    gx, gy = lax.axis_index("gx"), lax.axis_index("gy")
     width = rhs.shape[-1]
     groups = width // 128
     lane = lanes_of((K, 128))
-    even = place[1] % 2 == 0
-    channel = lax.broadcasted_iota(jnp.int32, (K, width), 0)
-    prior_rows[...] = sum(jnp.where(channel == k, prior[k], 0.0) for k in range(K))
+    even = gy % 2 == 0
 
     def store_pieces(slot, group, rest):
         cols = pl.ds((slot % 2) * 128, 128)
@@ -110,7 +114,7 @@
             pieces[group, slot // 2, pl.ds(i * K, K), cols] = parts[b]
 
     for group in range(groups):
-        bases = [(place[0] ^ o) * SEGMENT - group * 128 for o in range(rows)]
+        bases = [(gx ^ o) * SEGMENT - group * 128 for o in range(rows)]
         masks = []
         for base in bases:
             at = lane - base
@@ -151,7 +155,7 @@
 
     flat_inverse = inverse.reshape(groups * SLOTS * ROWS, 128)
     column = lanes_of((8, 128)) % SEGMENT
-    inside = ((place[1] > 0) | (column >= HALO)) & ((place[1] < place[2] - 1) | (column < HALO + OWN))
+    inside = ((gy > 0) | (column >= HALO)) & ((gy < lax.axis_size("gy") - 1) | (column < HALO + OWN))
     damped = jnp.where(inside, DAMPING, 0.0).astype(f32)
     half = K // 2
     tables = ((blocks, 0, COUNTS[0]), (coarse_blocks, COUNTS[0], SLOTS - COUNTS[0]))
@@ -175,7 +179,7 @@
 
             def load(k, l):
                 value = flat_blocks[pl.ds(source + l * K + k, 8, stride=ROWS), :]
-                return value + scale * prior[k] if k == l else value
+                return value + scale * prior_rows[pl.ds(k, 1), pl.ds(0, 128)] if k == l else value
 
             def store(k, l, value):
                 value = value * damped
@@ -326,89 +330,66 @@
     return [total[i : i + 1] for i in range(total.shape[0])]
 
 
-def kept_apart(energy, whole):
-    return jnp.maximum(energy, 1e-7 * whole)
-
-
-def first_pair(sums):
-    g0, g1, e00, e01, e11 = summed(sums)[:5]
-    ratio = e01 / e00
-    energy = kept_apart(e11 - ratio * e01, e11)
-    return e00, energy, ratio, g0 / e00, (g1 - ratio * g0) / energy
-
-
-def second_pair(sums, e0, e1):
-    h0, h1, h2, h3, a20, a21, a22, a30, a31, a32, a33 = summed(sums)[:11]
-    l20, l21, l30, l31 = a20 / e0, a21 / e1, a30 / e0, a31 / e1
-    e2 = kept_apart(a22 - l20 * a20 - l21 * a21, a22)
-    cross = a32 - l20 * a30 - l21 * a31
-    l32 = cross / e2
-    e3 = kept_apart(a33 - l30 * a30 - l31 * a31 - l32 * cross, a33)
-    n2 = h2 - l20 * h0 - l21 * h1
-    n3 = h3 - l30 * h0 - l31 * h1 - l32 * n2
-    c3 = n3 / e3
-    c2 = n2 / e2 - l32 * c3
-    return h0 / e0 - l20 * c2 - l30 * c3, h1 / e1 - l21 * c2 - l31 * c3, c2, c3
+def best_factors(sums):
+    values = summed(sums)
+    lower, energy, row = {}, [], []
+    for i in range(ITERS):
+        cross = {}
+        for j in range(i):
+            cross[j] = values[GRAM.index((i, j))]
+            for k in range(j):
+                cross[j] = cross[j] - lower[j, k] * cross[k]
+            lower[i, j] = cross[j] / energy[j]
+        whole = values[GRAM.index((i, i))]
+        left = whole
+        for j in range(i):
+            left = left - lower[i, j] * cross[j]
+        energy.append(jnp.maximum(left, 1e-7 * whole))
+        value = values[GRAM.index((i, -1))]
+        for j in range(i):
+            value = value - lower[i, j] * row[j]
+        row.append(value)
+    factors = [row[i] / energy[i] for i in range(ITERS)]
+    for i in range(ITERS - 1, -1, -1):
+        for j in range(i + 1, ITERS):
+            factors[i] = factors[i] - lower[j, i] * factors[j]
+    return [1.0 + factor for factor in factors]
 
 
 def iterate_kernel(step, *refs):
     refs = list(refs)
     take = lambda n: [refs.pop(0) for _ in range(n)]
-    place, prior, blocks, inverse, rhs = take(5)
-    if step == 0:
-        z0, az0, send_a, send_b = take(4)
-        z, az = z0, az0
-    elif step == 1:
-        edge_a, edge_b, z0, az0, parts, full, w1, aw1, send_a, send_b = take(10)
-        z, az = w1, aw1
-    elif step == 2:
-        sums, edge_a, edge_b, z0, az0, w1, aw1 = take(7)
-        scalars, p1, ap1, left_over, z2, az2, send_a, send_b = take(8)
-        z, az = z2, az2
+    last = step == ITERS - 1
+    prior, blocks, inverse, residual = take(4)
+    if step > 0:
+        edge_a, edge_b, image = take(3)
+    if last:
+        earlier = [take(2) for _ in range(step)]
+        sides = take(2)
+        parts, packed, z, az, kept_residual, left_over = take(6)
     else:
-        edge_a, edge_b, z0, az0, p1, ap1, z2, az2 = take(8)
-        parts, packed, w3, aw3 = take(4)
-        z, az = w3, aw3
-    b, v, d, w = (take(LEVELS) for _ in range(4))
+        z, az, send_a, send_b = take(4)
+        if step > 0:
+            (left_over,) = take(1)
+    b, v = ([one] + take(LEVELS - 1) for one in (left_over if step > 0 else residual, z))
+    d, w = take(LEVELS - 1), take(LEVELS)
     width = z.shape[-1]
     lane = lanes_of((K, width))
     column = lane % SEGMENT
     mine = (column >= HALO) & (column < HALO + OWN)
-    even = place[1] % 2 == 0
+    even = lax.axis_index("gy") % 2 == 0
     count = COUNTS[0]
 
-    def arrived(own):
+    if step > 0:
         left_side, right_side = column < HALO, column >= HALO + OWN
         for i in range(count // 4):
             left = jnp.where(even, edge_b[i], edge_a[i])
             right = jnp.where(even, edge_a[i], edge_b[i])
             for g in range(4):
                 at = 4 * i + g
-                value = jnp.where(left_side, roll(left, -HALO * g), own[at])
-                yield at, jnp.where(right_side, roll(right, SEGMENT - HALO - HALO * g), value)
-
-    if step == 0:
-        for at in range(count):
-            b[0][at] = rhs[at]
-    elif step == 1:
-        for at, image in arrived(az0):
-            full[at] = image
-            b[0][at] = rhs[at] - image
-    elif step == 2:
-        e0, e1, ratio, c0, c1 = first_pair(sums)
-        rows = [jnp.broadcast_to(x, (1, 128)) for x in (e0, e1, c0, c1)]
-        scalars[...] = jnp.concatenate(rows + [jnp.zeros((4, 128), f32)], axis=0)
-        for at, image in arrived(aw1):
-            first = az0[at]
-            image = image - ratio * first
-            ap1[at] = image
-            p1[at] = w1[at] - ratio * z0[at]
-            value = rhs[at] - c0 * first - c1 * image
-            left_over[at] = value
-            b[0][at] = value
-    else:
-        for at, image in arrived(az2):
-            b[0][at] = rhs[at] - image
+                value = jnp.where(left_side, roll(left, -HALO * g), image[at])
+                value = jnp.where(right_side, roll(right, SEGMENT - HALO - HALO * g), value)
+                left_over[at] = residual[at] - value
 
     v_cycle(inverse, prior, b, v, d, w)
 
@@ -421,28 +402,25 @@
             w[0][s * n + t] = weight * (4.0 * v[0][s * n + t] - near)
 
     def finish(i, cols, total):
-        az[i, :, cols] = total + w[0][i, :, cols]
-        z[i, :, cols] = v[0][i, :, cols]
+        value = total + w[0][i, :, cols]
+        az[i, :, cols] = value
+        if last:
+            kept_residual[i, :, cols] = b[0][i, :, cols] - value
 
     block_product(blocks, 0, count, v[0], finish)
 
-    if step == 1:
-        tile = dots([(z0, rhs), (w1, rhs), (z0, az0), (w1, az0), (w1, aw1)], width, mine)
-    elif step == 3:
-        pairs = [(z0, rhs), (p1, rhs), (z2, rhs), (w3, rhs)]
-        pairs += [(z2, az0), (z2, ap1), (z2, az2), (w3, az0), (w3, ap1), (w3, az2), (w3, aw3)]
+    if last:
+        vectors = [one for one, _ in earlier] + [z]
+        images = [one for _, one in earlier] + [az]
+        pairs = [(z, one) for one in images] + [(one, kept_residual) for one in vectors]
         tile = dots(pairs, width, mine)
-    if step % 2:
+        first, second = sides[0][...], sides[1][...]
+        row = lax.broadcasted_iota(jnp.int32, (8, 128), 0)
+        other = jnp.where(row < 3, first, pltpu.roll(second, 3, 0))
         for i in range(parts.shape[0]):
-            parts[i] = tile
-    if step == 3:
-        tile = refs[-1]
-        for i, source in enumerate((z0, p1, z2, w3)):
-            pack(place, source, tile)
-            back = lax.dot_general(
-                tile[...], lane_order(), (((1,), (1,)), ((), ())), precision=highest, preferred_element_type=f32
-            )
-            packed[i] = back.reshape(K, BLOCK, 128)
+            parts[i, pl.ds(0, 8), :] = tile
+            parts[i, pl.ds(8, 8), :] = other
+        pack(z, refs[-1], packed)
     else:
         for i in range(count // 4):
             left, right = None, None
@@ -456,24 +434,39 @@
             send_b[i] = jnp.where(even, left, right)
 
 
-def pack(place, source, tile):
-    group = pl.ds(pl.multiple_of((place[0] // 4) * 128, 128), 128)
-    base = (place[0] % 4) * SEGMENT + HALO
+def pack(source, tile, packed):
+    gx = lax.axis_index("gx")
+    group = pl.ds(pl.multiple_of((gx // 4) * 128, 128), 128)
+    base = (gx % 4) * SEGMENT + HALO
     lane = lanes_of((K, 128))
     for t in range(BLOCK):
-        packed = None
+        row = None
         for s in range(BLOCK):
             value = pltpu.roll(source[s * BLOCK + t, :, group], (128 + s * OWN - base) % 128, 1)
-            packed = value if packed is None else jnp.where(lane >= s * OWN, value, packed)
-        tile[pl.ds(t, K, stride=BLOCK), :] = packed
-
-
-def finish_kernel(sums, scalars, packed, out):
-    e0, e1, c0, c1 = (scalars[i : i + 1, 0:1] for i in range(4))
-    d0, d1, d2, d3 = second_pair(sums, e0, e1)
-    factors = [jnp.broadcast_to(x, (BLOCK, 128)) for x in (c0 + d0, c1 + d1, d2, d3)]
+            row = value if row is None else jnp.where(lane >= s * OWN, value, row)
+        tile[pl.ds(t, K, stride=BLOCK), :] = row
+    back = lax.dot_general(
+        tile[...], lane_order(), (((1,), (1,)), ((), ())), precision=highest, preferred_element_type=f32
+    )
+    packed[...] = back.reshape(K, BLOCK, 128)
+
+
+def side_kernel(step, *refs):
+    fields, (out, *packed), tile = refs[: 2 * step + 2], refs[2 * step + 2 : -1], refs[-1]
+    column = lanes_of(fields[0].shape[1:]) % SEGMENT
+    mine = (column >= HALO) & (column < HALO + OWN)
+    first = 0 if step == 1 else step
+    pairs = [(fields[2 * i], fields[2 * j + 1]) for i in range(first, step + 1) for j in range(i + 1)]
+    out[...] = dots(pairs, fields[0].shape[-1], mine)
+    for i, target in enumerate(packed):
+        pack(fields[2 * (first + i)], tile, target)
+
+
+def finish_kernel(sums, *refs):
+    packed, out = refs[:ITERS], refs[ITERS]
+    factors = [jnp.broadcast_to(x, (BLOCK, 128)) for x in best_factors(sums)]
     for k in range(K):
-        out[k] = sum(factors[i] * packed[i, k] for i in range(4))
+        out[k] = sum(factors[i] * packed[i][k] for i in range(ITERS))
 
 
 def gather(value):
@@ -491,7 +484,6 @@
 def local(beta, design, prior, kept, removed, removed_labels):
     rows, cols = lax.axis_size("gx"), lax.axis_size("gy")
     width = rows * SEGMENT
-    place = jnp.stack([lax.axis_index("gx"), lax.axis_index("gy"), jnp.int32(cols)]).astype(jnp.int32)
     pairs = [(i, i ^ 1) for i in range(cols)]
     others = [(0, 0)] + [(i, ((i + 1) ^ 1) - 1) for i in range(1, cols - 1)] + [(cols - 1, cols - 1)]
     others = others[1:-1]
@@ -499,17 +491,17 @@
     def shape(*dims, dtype=f32):
         return jax.ShapeDtypeStruct(dims, dtype)
 
-    own, edge_a, edge_b = pl.pallas_call(
+    own, held, edge_a, edge_b, prior_rows = pl.pallas_call(
         prepare_kernel,
-        out_shape=[shape(2, 8, K, 128), shape(2, 4, K, 128), shape(2, 4, K, 128)],
+        out_shape=[shape(2, 8, K, 128)] * 2 + [shape(2, 4, K, 128)] * 2 + [shape(K, width)],
         in_specs=[SMEM, SMEM] + [VMEM] * 4,
-        out_specs=[VMEM] * 3,
+        out_specs=[VMEM] * 5,
         scratch_shapes=[pltpu.VMEM((2 * K * BLOCK, 128), f32)],
         name="prepare",
-    )(place, design, beta, kept, removed, removed_labels)
+    )(design, prior, beta, kept, removed, removed_labels)
     edge_a = lax.ppermute(edge_a, "gy", pairs)
     edge_b = lax.ppermute(edge_b, "gy", others)
-    gathered = gather(own) + gather(edge_a) + gather(edge_b)
+    gathered = [held] + gather(own)[1:] + gather(edge_a) + gather(edge_b)
 
     products = (design[:, :, None] * design[:, None, :]).reshape(K, K * K).T
     parts, rest = [], products
@@ -520,11 +512,11 @@
     outer = jnp.concatenate([parts[a] for a, _ in SPLITS], axis=1).astype(jnp.bfloat16)
 
     field = shape(COUNTS[0], K, width)
-    blocks, inverse, rhs, prior_rows = pl.pallas_call(
+    blocks, inverse, rhs = pl.pallas_call(
         setup_kernel,
-        out_shape=[shape(width // 128, n, ROWS, 128) for n in (COUNTS[0], SLOTS)] + [field, shape(K, width)],
-        in_specs=[SMEM, SMEM] + [VMEM] * (1 + len(gathered)),
-        out_specs=[VMEM] * 4,
+        out_shape=[shape(width // 128, n, ROWS, 128) for n in (COUNTS[0], SLOTS)] + [field],
+        in_specs=[VMEM] * (2 + len(gathered)),
+        out_specs=[VMEM] * 3,
         scratch_shapes=[
             pltpu.VMEM((SLOTS, K, width), f32),
             pltpu.VMEM((width // 128, SLOTS // 2, len(SPLITS) * K, 256), jnp.bfloat16),
@@ -533,9 +525,11 @@
         ],
         compiler_params=params(24 if width == 128 else 60),
         name="setup",
-    )(place, prior, outer, *gathered)
-
-    levels = [pltpu.VMEM((n, K, width), f32) for n in COUNTS] * 4
+    )(outer, prior_rows, *gathered)
+
+    levels = [pltpu.VMEM((n, K, width), f32) for n in COUNTS[1:] * 2 + COUNTS[:-1] + COUNTS]
+    tile = pltpu.VMEM((K * BLOCK, 128), f32)
+    own_tile = shape(*beta.shape)
     whole = pltpu.VMEM((COUNTS[0], K, width), f32)
     edge = shape(COUNTS[0] // 4, K, width)
 
@@ -543,12 +537,12 @@
         return pl.pallas_call(
             functools.partial(iterate_kernel, step),
             out_shape=shapes,
-            in_specs=[SMEM] + [VMEM] * (len(operands) + 3),
+            in_specs=[VMEM] * (len(operands) + 3),
             out_specs=[VMEM] * len(shapes),
-            scratch_shapes=list(scratch[:2]) + levels + list(scratch[2:]),
+            scratch_shapes=list(scratch[:4]) + levels + list(scratch[4:]),
             compiler_params=params(24 if width == 128 else 60),
             name=f"iterate_{step}",
-        )(place, prior_rows, blocks, inverse, *operands)
+        )(prior_rows, blocks, inverse, *operands)
 
     def exchange(edge_a, edge_b):
         return lax.ppermute(edge_a, "gy", pairs), lax.ppermute(edge_b, "gy", others)
@@ -556,36 +550,42 @@
     def total(parts):
         return lax.all_to_all(parts, "gy", 0, 0, tiled=True)
 
-    z0, az0, *edges = iterate(0, rhs, shapes=[field, field, edge, edge])
-    edges = exchange(*edges)
-    parts, az0, w1, aw1, *edges = iterate(
-        1, rhs, *edges, z0, az0, shapes=[shape(cols, 8, 128), field, field, field, edge, edge]
-    )
-    sums, edges = total(parts), exchange(*edges)
-    scalars, p1, ap1, residual, z2, az2, *edges = iterate(
-        2, rhs, sums, *edges, z0, az0, w1, aw1, shapes=[shape(8, 128)] + [field] * 5 + [edge, edge]
-    )
-    edges = exchange(*edges)
-    parts, packed = iterate(
-        3,
+    residual, edges, image, earlier, sides, packed = rhs, (), (), (), (), ()
+    for step in range(ITERS - 1):
+        shapes = [field, field, edge, edge] + ([field] if step > 0 else [])
+        z, az, *sent = iterate(step, residual, *edges, *image, shapes=shapes)
+        edges, image, earlier = exchange(*sent[:2]), (az,), earlier + (z, az)
+        if step > 0:
+            residual = sent[2]
+            fresh = [own_tile] * (2 if step == 1 else 1)
+            side, *tiles = pl.pallas_call(
+                functools.partial(side_kernel, step),
+                out_shape=[shape(8, 128)] + fresh,
+                in_specs=[VMEM] * len(earlier),
+                out_specs=[VMEM] * (1 + len(fresh)),
+                scratch_shapes=[tile],
+                cost_estimate=pl.CostEstimate(flops=4_000_000, bytes_accessed=1_000_000, transcendentals=0),
+                compiler_params=params(24 if width == 128 else 60),
+                name=f"side_{step}",
+            )(*earlier)
+            sides, packed = sides + (side,), packed + tuple(tiles)
+    parts, last_tile = iterate(
+        ITERS - 1,
         residual,
         *edges,
-        z0,
-        az0,
-        p1,
-        ap1,
-        z2,
-        az2,
-        shapes=[shape(cols, 16, 128), shape(4, *beta.shape)],
-        scratch=[whole, whole, pltpu.VMEM((K * BLOCK, 128), f32)],
+        *image,
+        *earlier,
+        *sides,
+        shapes=[shape(cols, 16, 128), own_tile],
+        scratch=[whole] * 4 + [tile],
     )
     return pl.pallas_call(
         finish_kernel,
-        out_shape=shape(*beta.shape),
-        in_specs=[VMEM] * 3,
+        out_shape=own_tile,
+        in_specs=[VMEM] * (1 + ITERS),
         out_specs=VMEM,
         name="finish",
-    )(total(parts), scalars, packed)
+    )(total(parts), *packed, last_tile)
 
 
 def solution(mesh):

time: 112 us -> 102 us (0.911)
  blocking collectives: 27 us -> 17 us
  starting transfers between devices: 20.1 us -> 24.3 us
  Pallas kernels: 48.7 us -> 46.5 us
  local copies, waits for them, and re-layouts: 3.88 us -> 2.57 us
    all_to_all x2 -> x1, blocking collectives: 27 us -> 17 us  [total(): return lax.all_to_all(parts, 'gy', 0, 0, tiled=True)]
    ppermute x3, starting transfers between devices: 9.52 us -> 13.7 us  [exchange(): lax.ppermute(edge_a, 'gy', pairs)]
    pallas_call x4, Pallas kernels: 31.1 us -> 28.1 us  [iterate(): pl.pallas_call(functools.partial(iterate_kernel, step), out_shape=shapes,...]
    unnamed x11 -> x13, local copies, waits for them, and re-layouts: 3.69 us -> 2.38 us
    pallas_call x2 -> x4, Pallas kernels: 3.98 us -> 5.23 us  [the longest x1 2.19 us: local(): pl.pallas_call(prepare_kernel, out_shape=[shape(2, 8, K, 128)] * 2 + [sha...]
  transfers between devices with their start and end apart: 17 -> 17, of which waited for: 6 -> 7; matrix products, arithmetic and copies ran while one was open for 1% -> 1% of each run, Pallas kernels for 0% -> 1%
where the time goes in v4:
time: 102 us
  Pallas kernels  46.5 us (46%)
  starting transfers between devices  24.3 us (24%)
  blocking collectives  17 us (17%)
  waiting for transfers between devices  11.2 us (11%)
  local copies, waits for them, and re-layouts  2.57 us (3%)
    pallas_call x4, Pallas kernels, iterate(): pl.pallas_call(functools.partial(iterate_kernel, step), out_shape=shapes,...  28.1 us
    all_to_all x1, blocking collectives, total(): return lax.all_to_all(parts, 'gy', 0, 0, tiled=True)  17 us
    ppermute x3, starting transfers between devices, exchange(): lax.ppermute(edge_a, 'gy', pairs)  13.7 us
    pallas_call x1, Pallas kernels, local(): pl.pallas_call(setup_kernel, out_shape=[shape(width // 128, n, ROWS, 128)...  13.1 us
    ppermute x3, waiting for transfers between devices, exchange(): lax.ppermute(edge_a, 'gy', pairs)  6.69 us
    ppermute x9, starting transfers between devices, gather(): held[o ^ bit] = lax.ppermute(held[o], 'gx', pairs)  4.86 us
    ppermute x9, waiting for transfers between devices, gather(): held[o ^ bit] = lax.ppermute(held[o], 'gx', pairs)  4.47 us
    ppermute x1, starting transfers between devices, local(): edge_a = lax.ppermute(edge_a, 'gy', pairs)  2.94 us
  transfers between devices with their start and end apart: 17, of which 7 were waited for; matrix products, arithmetic and copies ran while one was open for 1% of the time, Pallas kernels for 1%

profile of v4, /device:TPU:0, one launch (start us, length us, event | category | flops | bytes accessed | tf_op | source)
XLA Modules:
  0.0 101.7 jit_solution(461365919175784058)
XLA Ops:
  0.0 2.2 %prepare.1 = (f32[2,8,16,128]{3,2,1,0:T(8,128)}, f32[2,8,16,128]{3,2,1,0:T(8,128)}, f32[2,4,16,128]{3,2,1,0:T(8,128)}, f32[2,4,16,128]{3,2,1,0:T(8,128)}, f32[16,128]{1,0:T(8,128)}) custom-call(f32[16,16]{1,0:T(8,128)} %design.1, f32[16]{0:T(128)} %prior.1, f32[16,8,128]{2,1,0:T(8,128)} %beta.1, s32[16,8,128]{2,1,0:T(8,128)} %kept.1, s32[16,8,128]{2,1,0:T(8,128)} %removed.1, ...), custom_call_target="tpu_custom_call" | custom-call | tf_op jit(solution)/shard_map/prepare/pallas_call | solution.py:494
  2.2 2.9 %collective-permute-start.3 = (f32[2,4,16,128]{3,2,1,0:T(8,128)}, f32[2,4,16,128]{3,2,1,0:T(8,128)S(1)}, u32[]{:S(2)}, u32[]{:S(2)}) collective-permute-start(f32[2,4,16,128]{3,2,1,0:T(8,128)} %get-tuple-element.37), channel_id=1, source_target_pairs={{0,1},{1,0},{2,3},{3,2},{4,5},{5,4},{6,7},{7,6},{8,9},{9,8},{10,11... | collective-permute-start | bytes 196616 | tf_op jit(solution)/shard_map/ppermute | solution.py:502
  5.8 1.6 %collective-permute-start.1 = (f32[2,8,16,128]{3,2,1,0:T(8,128)}, f32[2,8,16,128]{3,2,1,0:T(8,128)S(1)}, u32[]{:S(2)}, u32[]{:S(2)}) collective-permute-start(f32[2,8,16,128]{3,2,1,0:T(8,128)} %get-tuple-element.36), channel_id=1, source_target_pairs={{0,16},{8,24},{16,0},{24,8},{1,17},{9,25},{17,1},{25,9},{2,18},{10... | collective-permute-start | bytes 393224 | tf_op jit(solution)/shard_map/ppermute | solution.py:479
  7.4 0.8 copy.9
  8.1 1.5 %collective-permute-start.5 = (f32[2,4,16,128]{3,2,1,0:T(8,128)S(1)}, f32[2,4,16,128]{3,2,1,0:T(8,128)S(1)}, u32[]{:S(2)}, u32[]{:S(2)}) collective-permute-start(f32[2,4,16,128]{3,2,1,0:T(8,128)S(1)} %collective-permute-done.3.refs_4_), channel_id=1, source_target_pairs={{0,16},{8,24},{16,0},{24,8},{1,17},{9,25},{17,1},{25,9},{2,18},{10... | collective-permute-start | bytes 196616 | tf_op jit(solution)/shard_map/ppermute | solution.py:479
  9.6 0.8 collective-permute-start.9
  10.4 3.7 %collective-permute-done.9.refs_10_ = f32[2,4,16,128]{3,2,1,0:T(8,128)S(1)} collective-permute-done((f32[2,4,16,128]{3,2,1,0:T(8,128)S(1)}, f32[2,4,16,128]{3,2,1,0:T(8,128)S(1)}, u32[]{:S(2)}, u32[]{:S(2)}) %collective-permute-start.9) | collective-permute-done | bytes 65568 | tf_op jit(solution)/shard_map/ppermute | solution.py:479
  16.2 0.7 copy-done
  16.9 0.9 copy-done.1
  17.8 13.1 %setup.1 = (f32[1,64,264,128]{3,2,1,0:T(8,128)S(1)}, f32[1,88,264,128]{3,2,1,0:T(8,128)S(1)}, f32[64,16,128]{2,1,0:T(8,128)S(1)}) custom-call(bf16[256,96]{1,0:T(8,128)(2,1)S(1)} %concatenate.4.outer, f32[16,128]{1,0:T(8,128)S(1)} %copy-done, f32[2,8,16,128]{3,2,1,0:T(8,128)S(1)} %copy-done.1, f32[2,8,16,128]{3,2,1,0:T(8,128)S(1)} %collective-permute-done.refs_1_, ...), custom_call_target="tpu_custom_call" | custom-call | tf_op jit(solution)/shard_map/setup/pallas_call | solution.py:515
  30.9 6.8 %iterate_0.1 = (f32[64,16,128]{2,1,0:T(8,128)S(1)}, f32[64,16,128]{2,1,0:T(8,128)S(1)}, f32[16,16,128]{2,1,0:T(8,128)S(1)}, f32[16,16,128]{2,1,0:T(8,128)S(1)}) custom-call(f32[16,128]{1,0:T(8,128)S(1)} %copy-done, f32[1,64,264,128]{3,2,1,0:T(8,128)S(1)} %get-tuple-element.39.refs_1_, f32[1,88,264,128]{3,2,1,0:T(8,128)S(1)} %get-tuple-element.40.refs_2_, ...), custom_call_target="tpu_custom_call" | custom-call | tf_op jit(solution)/shard_map/iterate_0/pallas_call | solution.py:537
  37.7 4.3 %collective-permute-start.11 = (f32[16,16,128]{2,1,0:T(8,128)S(1)}, f32[16,16,128]{2,1,0:T(8,128)S(1)}, u32[]{:S(2)}, u32[]{:S(2)}) collective-permute-start(f32[16,16,128]{2,1,0:T(8,128)S(1)} %get-tuple-element.42), channel_id=1, source_target_pairs={{0,1},{1,0},{2,3},{3,2},{4,5},{5,4},{6,7},{7,6},{8,9},{9,8},{10,11... | collective-permute-start | bytes 393224 | tf_op jit(solution)/shard_map/ppermute | solution.py:548
  42.0 0.8 collective-permute-start.12
  42.9 3.2 %collective-permute-done.11.refs_4_ = f32[16,16,128]{2,1,0:T(8,128)S(1)} collective-permute-done((f32[16,16,128]{2,1,0:T(8,128)S(1)}, f32[16,16,128]{2,1,0:T(8,128)S(1)}, u32[]{:S(2)}, u32[]{:S(2)}) %collective-permute-start.11) | collective-permute-done | bytes 131104 | tf_op jit(solution)/shard_map/ppermute | solution.py:548
  46.0 6.8 %iterate_1.1 = (f32[64,16,128]{2,1,0:T(8,128)S(1)}, f32[64,16,128]{2,1,0:T(8,128)S(1)}, f32[16,16,128]{2,1,0:T(8,128)S(1)}, f32[16,16,128]{2,1,0:T(8,128)S(1)}, f32[64,16,128]{2,1,0:T(8,128)S(1)}) custom-call(f32[16,128]{1,0:T(8,128)S(1)} %copy-done, f32[1,64,264,128]{3,2,1,0:T(8,128)S(1)} %get-tuple-element.39.refs_1_, ...), custom_call_target="tpu_custom_call" | custom-call | tf_op jit(solution)/shard_map/iterate_1/pallas_call | solution.py:537
  52.9 4.7 %collective-permute-start.13 = (f32[16,16,128]{2,1,0:T(8,128)S(1)}, f32[16,16,128]{2,1,0:T(8,128)S(1)}, u32[]{:S(2)}, u32[]{:S(2)}) collective-permute-start(f32[16,16,128]{2,1,0:T(8,128)S(1)} %get-tuple-element.46), channel_id=1, source_target_pairs={{0,1},{1,0},{2,3},{3,2},{4,5},{5,4},{6,7},{7,6},{8,9},{9,8},{10,11... | collective-permute-start | bytes 393224 | tf_op jit(solution)/shard_map/ppermute | solution.py:548
  58.2 2.5 %collective-permute-done.13.refs_4_ = f32[16,16,128]{2,1,0:T(8,128)S(1)} collective-permute-done((f32[16,16,128]{2,1,0:T(8,128)S(1)}, f32[16,16,128]{2,1,0:T(8,128)S(1)}, u32[]{:S(2)}, u32[]{:S(2)}) %collective-permute-start.13) | collective-permute-done | bytes 131104 | tf_op jit(solution)/shard_map/ppermute | solution.py:548
  60.8 7.1 %iterate_2.1 = (f32[64,16,128]{2,1,0:T(8,128)S(1)}, f32[64,16,128]{2,1,0:T(8,128)S(1)}, f32[16,16,128]{2,1,0:T(8,128)S(1)}, f32[16,16,128]{2,1,0:T(8,128)S(1)}, f32[64,16,128]{2,1,0:T(8,128)S(1)}) custom-call(f32[16,128]{1,0:T(8,128)S(1)} %copy-done, f32[1,64,264,128]{3,2,1,0:T(8,128)S(1)} %get-tuple-element.39.refs_1_, ...), custom_call_target="tpu_custom_call" | custom-call | tf_op jit(solution)/shard_map/iterate_2/pallas_call | solution.py:537
  67.9 4.7 %collective-permute-start.15 = (f32[16,16,128]{2,1,0:T(8,128)S(1)}, f32[16,16,128]{2,1,0:T(8,128)S(1)}, u32[]{:S(2)}, u32[]{:S(2)}) collective-permute-start(f32[16,16,128]{2,1,0:T(8,128)S(1)} %get-tuple-element.50), channel_id=1, source_target_pairs={{0,1},{1,0},{2,3},{3,2},{4,5},{5,4},{6,7},{7,6},{8,9},{9,8},{10,11... | collective-permute-start | bytes 393224 | tf_op jit(solution)/shard_map/ppermute | solution.py:548
  73.3 0.7 side_1.1
  74.6 1.0 collective-permute-done.15.refs_4_
  75.6 7.4 %iterate_3.1 = (f32[8,16,128]{2,1,0:T(8,128)S(1)}, f32[16,8,128]{2,1,0:T(8,128)S(1)}) custom-call(f32[16,128]{1,0:T(8,128)S(1)} %copy-done, f32[1,64,264,128]{3,2,1,0:T(8,128)S(1)} %get-tuple-element.39.refs_1_, f32[1,88,264,128]{3,2,1,0:T(8,128)S(1)} %get-tuple-element.40.refs_2_, f32[64,16,128]{2,1,0:T(8,128)S(1)} %get-tuple-element.49.refs_3_, ...), custom_call_target="tpu_custom_call" | custom-call | tf_op jit(solution)/shard_map/iterate_3/pallas_call | solution.py:537
  83.0 17.0 %all_to_all.5.sums = f32[8,16,128]{2,1,0:T(8,128)} all-to-all(f32[8,16,128]{2,1,0:T(8,128)S(1)} %get-tuple-element.58), channel_id=1, replica_groups=mesh['gx'=4,'gy'=8] {'gy'}, dimensions={0} | all-to-all | bytes 131072 | tf_op jit(solution)/shard_map/all_to_all | solution.py:551
  100.0 1.8 %finish.1 = f32[16,8,128]{2,1,0:T(8,128)} custom-call(f32[8,16,128]{2,1,0:T(8,128)} %all_to_all.5.sums, f32[16,8,128]{2,1,0:T(8,128)} %copy-done.2, f32[16,8,128]{2,1,0:T(8,128)} %copy-done.3, f32[16,8,128]{2,1,0:T(8,128)} %copy-done.4, f32[16,8,128]{2,1,0:T(8,128)} %copy-done.5), custom_call_target="tpu_custom_call" | custom-call | tf_op jit(solution)/shard_map/finish/pallas_call | solution.py:582
  (36 shorter events, 4.5 us)
Async XLA Ops:
  2.2 6.0 %collective-permute-start.3 = (f32[2,4,16,128]{3,2,1,0:T(8,128)}, f32[2,4,16,128]{3,2,1,0:T(8,128)S(1)}, u32[]{:S(2)}, u32[]{:S(2)}) collective-permute-start(f32[2,4,16,128]{3,2,1,0:T(8,128)} %get-tuple-element.37), channel_id=1, source_target_pairs={{0,1},{1,0},{2,3},{3,2},{4,5},{5,4},{6,7},{7,6},{8,9},{9,8},{10,11... | collective-permute-start | bytes 196616 | tf_op jit(solution)/shard_map/ppermute | solution.py:502
  5.1 4.5 %collective-permute-start.7 = (f32[2,4,16,128]{3,2,1,0:T(8,128)}, f32[2,4,16,128]{3,2,1,0:T(8,128)S(1)}, u32[]{:S(2)}, u32[]{:S(2)}) collective-permute-start(f32[2,4,16,128]{3,2,1,0:T(8,128)} %get-tuple-element.38), channel_id=1, source_target_pairs={{1,2},{2,1},{3,4},{4,3},{5,6},{6,5},{9,10},{10,9},{11,12},{12,11},... | collective-permute-start | bytes 196616 | tf_op jit(solution)/shard_map/ppermute | solution.py:503
  5.8 8.9 %collective-permute-start.1 = (f32[2,8,16,128]{3,2,1,0:T(8,128)}, f32[2,8,16,128]{3,2,1,0:T(8,128)S(1)}, u32[]{:S(2)}, u32[]{:S(2)}) collective-permute-start(f32[2,8,16,128]{3,2,1,0:T(8,128)} %get-tuple-element.36), channel_id=1, source_target_pairs={{0,16},{8,24},{16,0},{24,8},{1,17},{9,25},{17,1},{25,9},{2,18},{10... | collective-permute-start | bytes 393224 | tf_op jit(solution)/shard_map/ppermute | solution.py:479
  7.4 8.0 %collective-permute-start = (f32[2,8,16,128]{3,2,1,0:T(8,128)}, f32[2,8,16,128]{3,2,1,0:T(8,128)S(1)}, u32[]{:S(2)}, u32[]{:S(2)}) collective-permute-start(f32[2,8,16,128]{3,2,1,0:T(8,128)} %get-tuple-element.36), channel_id=1, source_target_pairs={{0,8},{8,0},{16,24},{24,16},{1,9},{9,1},{17,25},{25,17},{2,10},{10... | collective-permute-start | bytes 393224 | tf_op jit(solution)/shard_map/ppermute | solution.py:479
  8.1 6.0 %collective-permute-start.5 = (f32[2,4,16,128]{3,2,1,0:T(8,128)S(1)}, f32[2,4,16,128]{3,2,1,0:T(8,128)S(1)}, u32[]{:S(2)}, u32[]{:S(2)}) collective-permute-start(f32[2,4,16,128]{3,2,1,0:T(8,128)S(1)} %collective-permute-done.3.refs_4_), channel_id=1, source_target_pairs={{0,16},{8,24},{16,0},{24,8},{1,17},{9,25},{17,1},{25,9},{2,18},{10... | collective-permute-start | bytes 196616 | tf_op jit(solution)/shard_map/ppermute | solution.py:479
  9.6 5.1 %collective-permute-start.4 = (f32[2,4,16,128]{3,2,1,0:T(8,128)S(1)}, f32[2,4,16,128]{3,2,1,0:T(8,128)S(1)}, u32[]{:S(2)}, u32[]{:S(2)}) collective-permute-start(f32[2,4,16,128]{3,2,1,0:T(8,128)S(1)} %collective-permute-done.3.refs_4_), channel_id=1, source_target_pairs={{0,8},{8,0},{16,24},{24,16},{1,9},{9,1},{17,25},{25,17},{2,10},{10... | collective-permute-start | bytes 196616 | tf_op jit(solution)/shard_map/ppermute | solution.py:479
  9.6 4.5 %collective-permute-start.9 = (f32[2,4,16,128]{3,2,1,0:T(8,128)S(1)}, f32[2,4,16,128]{3,2,1,0:T(8,128)S(1)}, u32[]{:S(2)}, u32[]{:S(2)}) collective-permute-start(f32[2,4,16,128]{3,2,1,0:T(8,128)S(1)} %collective-permute-done.7.refs_8_), channel_id=1, source_target_pairs={{0,16},{8,24},{16,0},{24,8},{1,17},{9,25},{17,1},{25,9},{2,18},{10... | collective-permute-start | bytes 196616 | tf_op jit(solution)/shard_map/ppermute | solution.py:479
  14.1 1.3 %collective-permute-start.8 = (f32[2,4,16,128]{3,2,1,0:T(8,128)S(1)}, f32[2,4,16,128]{3,2,1,0:T(8,128)S(1)}, u32[]{:S(2)}, u32[]{:S(2)}) collective-permute-start(f32[2,4,16,128]{3,2,1,0:T(8,128)S(1)} %collective-permute-done.7.refs_8_), channel_id=1, source_target_pairs={{0,8},{8,0},{16,24},{24,16},{1,9},{9,1},{17,25},{25,17},{2,10},{10... | collective-permute-start | bytes 196616 | tf_op jit(solution)/shard_map/ppermute | solution.py:479
  14.2 1.4 %collective-permute-start.10 = (f32[2,4,16,128]{3,2,1,0:T(8,128)S(1)}, f32[2,4,16,128]{3,2,1,0:T(8,128)S(1)}, u32[]{:S(2)}, u32[]{:S(2)}) collective-permute-start(f32[2,4,16,128]{3,2,1,0:T(8,128)S(1)} %collective-permute-done.9.refs_10_), channel_id=1, source_target_pairs={{0,8},{8,0},{16,24},{24,16},{1,9},{9,1},{17,25},{25,17},{2,10},{10... | collective-permute-start | bytes 196616 | tf_op jit(solution)/shard_map/ppermute | solution.py:479
  14.7 1.3 %collective-permute-start.6 = (f32[2,4,16,128]{3,2,1,0:T(8,128)S(1)}, f32[2,4,16,128]{3,2,1,0:T(8,128)S(1)}, u32[]{:S(2)}, u32[]{:S(2)}) collective-permute-start(f32[2,4,16,128]{3,2,1,0:T(8,128)S(1)} %collective-permute-done.5.refs_6_), channel_id=1, source_target_pairs={{0,8},{8,0},{16,24},{24,16},{1,9},{9,1},{17,25},{25,17},{2,10},{10... | collective-permute-start | bytes 196616 | tf_op jit(solution)/shard_map/ppermute | solution.py:479
  14.7 1.4 %collective-permute-start.2 = (f32[2,8,16,128]{3,2,1,0:T(8,128)S(1)}, f32[2,8,16,128]{3,2,1,0:T(8,128)S(1)}, u32[]{:S(2)}, u32[]{:S(2)}) collective-permute-start(f32[2,8,16,128]{3,2,1,0:T(8,128)S(1)} %collective-permute-done.1.refs_2_), channel_id=1, source_target_pairs={{0,8},{8,0},{16,24},{24,16},{1,9},{9,1},{17,25},{25,17},{2,10},{10... | collective-permute-start | bytes 393224 | tf_op jit(solution)/shard_map/ppermute | solution.py:479
  16.2 0.7 copy-start
  16.9 0.9 copy-start.1
  37.7 8.3 %collective-permute-start.11 = (f32[16,16,128]{2,1,0:T(8,128)S(1)}, f32[16,16,128]{2,1,0:T(8,128)S(1)}, u32[]{:S(2)}, u32[]{:S(2)}) collective-permute-start(f32[16,16,128]{2,1,0:T(8,128)S(1)} %get-tuple-element.42), channel_id=1, source_target_pairs={{0,1},{1,0},{2,3},{3,2},{4,5},{5,4},{6,7},{7,6},{8,9},{9,8},{10,11... | collective-permute-start | bytes 393224 | tf_op jit(solution)/shard_map/ppermute | solution.py:548
  42.0 4.0 %collective-permute-start.12 = (f32[16,16,128]{2,1,0:T(8,128)S(1)}, f32[16,16,128]{2,1,0:T(8,128)S(1)}, u32[]{:S(2)}, u32[]{:S(2)}) collective-permute-start(f32[16,16,128]{2,1,0:T(8,128)S(1)} %get-tuple-element.43), channel_id=1, source_target_pairs={{1,2},{2,1},{3,4},{4,3},{5,6},{6,5},{9,10},{10,9},{11,12},{12,11},... | collective-permute-start | bytes 393224 | tf_op jit(solution)/shard_map/ppermute | solution.py:548
  52.9 7.9 %collective-permute-start.13 = (f32[16,16,128]{2,1,0:T(8,128)S(1)}, f32[16,16,128]{2,1,0:T(8,128)S(1)}, u32[]{:S(2)}, u32[]{:S(2)}) collective-permute-start(f32[16,16,128]{2,1,0:T(8,128)S(1)} %get-tuple-element.46), channel_id=1, source_target_pairs={{0,1},{1,0},{2,3},{3,2},{4,5},{5,4},{6,7},{7,6},{8,9},{9,8},{10,11... | collective-permute-start | bytes 393224 | tf_op jit(solution)/shard_map/ppermute | solution.py:548
  57.6 3.2 %collective-permute-start.14 = (f32[16,16,128]{2,1,0:T(8,128)S(1)}, f32[16,16,128]{2,1,0:T(8,128)S(1)}, u32[]{:S(2)}, u32[]{:S(2)}) collective-permute-start(f32[16,16,128]{2,1,0:T(8,128)S(1)} %get-tuple-element.47), channel_id=1, source_target_pairs={{1,2},{2,1},{3,4},{4,3},{5,6},{6,5},{9,10},{10,9},{11,12},{12,11},... | collective-permute-start | bytes 393224 | tf_op jit(solution)/shard_map/ppermute | solution.py:548
  67.9 7.7 %collective-permute-start.15 = (f32[16,16,128]{2,1,0:T(8,128)S(1)}, f32[16,16,128]{2,1,0:T(8,128)S(1)}, u32[]{:S(2)}, u32[]{:S(2)}) collective-permute-start(f32[16,16,128]{2,1,0:T(8,128)S(1)} %get-tuple-element.50), channel_id=1, source_target_pairs={{0,1},{1,0},{2,3},{3,2},{4,5},{5,4},{6,7},{7,6},{8,9},{9,8},{10,11... | collective-permute-start | bytes 393224 | tf_op jit(solution)/shard_map/ppermute | solution.py:548
  72.6 3.0 %collective-permute-start.16 = (f32[16,16,128]{2,1,0:T(8,128)S(1)}, f32[16,16,128]{2,1,0:T(8,128)S(1)}, u32[]{:S(2)}, u32[]{:S(2)}) collective-permute-start(f32[16,16,128]{2,1,0:T(8,128)S(1)} %get-tuple-element.51), channel_id=1, source_target_pairs={{1,2},{2,1},{3,4},{4,3},{5,6},{6,5},{9,10},{10,9},{11,12},{12,11},... | collective-permute-start | bytes 393224 | tf_op jit(solution)/shard_map/ppermute | solution.py:548
  74.0 1.5 %copy-start.3 = (f32[16,8,128]{2,1,0:T(8,128)}, f32[16,8,128]{2,1,0:T(8,128)S(1)}, u32[]{:S(2)}) copy-start(f32[16,8,128]{2,1,0:T(8,128)S(1)} %get-tuple-element.60.refs_1_) | copy-start | bytes 196612
  74.0 8.9 %copy-start.2 = (f32[16,8,128]{2,1,0:T(8,128)}, f32[16,8,128]{2,1,0:T(8,128)S(1)}, u32[]{:S(2)}) copy-start(f32[16,8,128]{2,1,0:T(8,128)S(1)} %get-tuple-element.59.refs_0_) | copy-start | bytes 196612
  74.6 8.4 %copy-start.4 = (f32[16,8,128]{2,1,0:T(8,128)}, f32[16,8,128]{2,1,0:T(8,128)S(1)}, u32[]{:S(2)}) copy-start(f32[16,8,128]{2,1,0:T(8,128)S(1)} %get-tuple-element.61.refs_2_) | copy-start | bytes 196612
  83.0 17.0 %copy-start.5 = (f32[16,8,128]{2,1,0:T(8,128)}, f32[16,8,128]{2,1,0:T(8,128)S(1)}, u32[]{:S(2)}) copy-start(f32[16,8,128]{2,1,0:T(8,128)S(1)} %get-tuple-element.62.refs_3_) | copy-start | bytes 196612

commit v5 on v4

--- a/solution.py
+++ b/solution.py
@@ -51,7 +51,7 @@
     return (lane == (row % BLOCK) * OWN + row // BLOCK).astype(f32)
 
 
-def prepare_kernel(design, prior, beta, kept, removed, labels, own, held, edge_a, edge_b, prior_rows, tile):
+def prepare_kernel(design, beta, kept, removed, labels, own, edge_a, edge_b, tile):
     probs = []
     for j in range(K):
         logit = sum(design[j, k] * beta[k] for k in range(K))
@@ -61,20 +61,23 @@
     for k in range(K):
         tile[pl.ds((K + k) * BLOCK, BLOCK), :] = sum(design[j, k] * probs[j] for j in range(K))
     tile[...] = jnp.dot(tile[...], lane_order(), precision=highest, preferred_element_type=f32)
-    channel = lax.broadcasted_iota(jnp.int32, prior_rows.shape, 0)
-    prior_rows[...] = sum(jnp.where(channel == k, prior[k], 0.0) for k in range(K))
     even = lax.axis_index("gy") % 2 == 0
     low = lanes_of((K, 128)) % OWN < HALO
     for f in range(2):
         rows = [tile[pl.ds(f * K * BLOCK + t, K, stride=BLOCK), :] for t in range(BLOCK)]
         for t in range(BLOCK):
             own[f, t] = rows[t]
-            held[f, t] = rows[t]
         for i in range(BLOCK // 2):
             left = jnp.where(low, rows[2 * i], roll(rows[2 * i + 1], HALO))
             right = jnp.where(low, roll(rows[2 * i], -HALO), rows[2 * i + 1])
             edge_a[f, i] = jnp.where(even, right, left)
             edge_b[f, i] = jnp.where(even, left, right)
+
+
+def hold_kernel(prior, own, held, prior_rows):
+    held[...] = own[...]
+    channel = lax.broadcasted_iota(jnp.int32, prior_rows.shape, 0)
+    prior_rows[...] = sum(jnp.where(channel == k, prior[k], 0.0) for k in range(K))
 
 
 def symmetric_inverse(a, n):
@@ -253,7 +256,7 @@
             finish(i, cols, total)
         return carry
 
-    lax.fori_loop(0, count, one, 0, unroll=min(count, 16))
+    lax.fori_loop(0, count, one, 0, unroll=min(count, 32))
 
 
 def v_cycle(inverse, prior, b, v, d, w):
@@ -469,7 +472,7 @@
         out[k] = sum(factors[i] * packed[i][k] for i in range(ITERS))
 
 
-def gather(value):
+def gather(value, beside=None):
     rows = lax.axis_size("gx")
     held = {0: value}
     bit = rows // 2
@@ -477,8 +480,11 @@
         pairs = [(i, i ^ bit) for i in range(rows)]
         for o in list(held):
             held[o ^ bit] = lax.ppermute(held[o], "gx", pairs)
+        if beside is not None:
+            *beside, held[bit] = lax.optimization_barrier((*beside, held[bit]))
         bit //= 2
-    return [held[o] for o in range(rows)]
+    values = [held[o] for o in range(rows)]
+    return values if beside is None else (values, beside)
 
 
 def local(beta, design, prior, kept, removed, removed_labels):
@@ -491,17 +497,26 @@
     def shape(*dims, dtype=f32):
         return jax.ShapeDtypeStruct(dims, dtype)
 
-    own, held, edge_a, edge_b, prior_rows = pl.pallas_call(
+    own, edge_a, edge_b = pl.pallas_call(
         prepare_kernel,
-        out_shape=[shape(2, 8, K, 128)] * 2 + [shape(2, 4, K, 128)] * 2 + [shape(K, width)],
-        in_specs=[SMEM, SMEM] + [VMEM] * 4,
-        out_specs=[VMEM] * 5,
+        out_shape=[shape(2, 8, K, 128)] + [shape(2, 4, K, 128)] * 2,
+        in_specs=[SMEM] + [VMEM] * 4,
+        out_specs=[VMEM] * 3,
         scratch_shapes=[pltpu.VMEM((2 * K * BLOCK, 128), f32)],
         name="prepare",
-    )(design, prior, beta, kept, removed, removed_labels)
+    )(design, beta, kept, removed, removed_labels)
+    held, prior_rows = pl.pallas_call(
+        hold_kernel,
+        out_shape=[shape(*own.shape), shape(K, width)],
+        in_specs=[SMEM, VMEM],
+        out_specs=[VMEM] * 2,
+        compiler_params=params(24),
+        name="hold",
+    )(prior, own)
     edge_a = lax.ppermute(edge_a, "gy", pairs)
     edge_b = lax.ppermute(edge_b, "gy", others)
-    gathered = [held] + gather(own)[1:] + gather(edge_a) + gather(edge_b)
+    last, (held, prior_rows) = gather(edge_b, (held, prior_rows))
+    gathered = [held] + gather(own)[1:] + gather(edge_a) + last
 
     products = (design[:, :, None] * design[:, None, :]).reshape(K, K * K).T
     parts, rest = [], products
@@ -584,6 +599,7 @@
         out_shape=own_tile,
         in_specs=[VMEM] * (1 + ITERS),
         out_specs=VMEM,
+        compiler_params=params(8),
         name="finish",
     )(total(parts), *packed, last_tile)
 

time: 102 us -> 97.9 us (0.960)
  blocking collectives: 17 us -> 15.8 us
  waiting for transfers between devices: 11.2 us -> 10.1 us
    ppermute x3, starting transfers between devices: 13.7 us -> 10.4 us  [exchange(): lax.ppermute(edge_a, 'gy', pairs)]
    ppermute x1, starting transfers between devices: 2.94 us -> 5.8 us  [local(): edge_a = lax.ppermute(edge_a, 'gy', pairs)]
    ppermute x9, waiting for transfers between devices: 4.47 us -> 1.92 us  [gather(): held[o ^ bit] = lax.ppermute(held[o], 'gx', pairs)]
    ppermute x3, waiting for transfers between devices: 6.69 us -> 8.13 us  [exchange(): lax.ppermute(edge_a, 'gy', pairs)]
    all_to_all x1, blocking collectives: 17 us -> 15.8 us  [total(): return lax.all_to_all(parts, 'gy', 0, 0, tiled=True)]
    pallas_call x1 -> x2, Pallas kernels: 2.19 us -> 2.74 us  [the longest x1 2.18 us: local(): pl.pallas_call(prepare_kernel, out_shape=[shape(2, 8, K, 128)] + [shape(2...]
    unnamed x13 -> x5, local copies, waits for them, and re-layouts: 2.38 us -> 2.32 us
  transfers between devices with their start and end apart: 17 -> 17, of which waited for: 7 -> 7; matrix products, arithmetic and copies ran while one was open for 1% -> 1% of each run, Pallas kernels for 1% -> 2%
where the time goes in v5:
time: 97.9 us; the launch traced here: 97.6 us
  Pallas kernels  45.5 us (46%)
  starting transfers between devices  23.6 us (24%)
  blocking collectives  15.8 us (16%)
  waiting for transfers between devices  10.1 us (10%)
  local copies, waits for them, and re-layouts  2.5 us (3%)
    pallas_call x4, Pallas kernels, iterate(): pl.pallas_call(functools.partial(iterate_kernel, step), out_shape=shapes,...  27.5 us
    all_to_all x1, blocking collectives, total(): return lax.all_to_all(parts, 'gy', 0, 0, tiled=True)  15.8 us
    pallas_call x1, Pallas kernels, local(): pl.pallas_call(setup_kernel, out_shape=[shape(width // 128, n, ROWS, 128)...  13.2 us
    ppermute x3, starting transfers between devices, exchange(): lax.ppermute(edge_a, 'gy', pairs)  10.4 us
    ppermute x3, waiting for transfers between devices, exchange(): lax.ppermute(edge_a, 'gy', pairs)  8.13 us
    ppermute x1, starting transfers between devices, local(): edge_a = lax.ppermute(edge_a, 'gy', pairs)  5.8 us
    ppermute x9, starting transfers between devices, gather(): held[o ^ bit] = lax.ppermute(held[o], 'gx', pairs)  4.37 us
    ppermute x3, starting transfers between devices, exchange(): lax.ppermute(edge_b, 'gy', others)  2.37 us
  transfers between devices with their start and end apart: 17, of which 7 were waited for; matrix products, arithmetic and copies ran while one was open for 1% of the time, Pallas kernels for 2%

profile of v5, /device:TPU:0, one launch (start us, length us, event | category | flops | bytes accessed | tf_op | source)
XLA Modules:
  0.0 97.6 jit_solution(7712229311083082949)
XLA Ops:
  0.0 2.2 %prepare.1 = (f32[2,8,16,128]{3,2,1,0:T(8,128)}, f32[2,4,16,128]{3,2,1,0:T(8,128)}, f32[2,4,16,128]{3,2,1,0:T(8,128)}) custom-call(f32[16,16]{1,0:T(8,128)} %design.1, f32[16,8,128]{2,1,0:T(8,128)} %beta.1, s32[16,8,128]{2,1,0:T(8,128)} %kept.1, s32[16,8,128]{2,1,0:T(8,128)} %removed.1, s32[16,8,128]{2,1,0:T(8,128)} %labels.1), custom_call_target="tpu_custom_call" | custom-call | tf_op jit(solution)/shard_map/prepare/pallas_call | solution.py:500
  2.8 5.8 %collective-permute-start.6 = (f32[2,4,16,128]{3,2,1,0:T(8,128)}, f32[2,4,16,128]{3,2,1,0:T(8,128)S(1)}, u32[]{:S(2)}, u32[]{:S(2)}) collective-permute-start(f32[2,4,16,128]{3,2,1,0:T(8,128)} %get-tuple-element.48), channel_id=1, source_target_pairs={{0,1},{1,0},{2,3},{3,2},{4,5},{5,4},{6,7},{7,6},{8,9},{9,8},{10,11... | collective-permute-start | bytes 196616 | tf_op jit(solution)/shard_map/ppermute | solution.py:516
  8.6 1.5 %collective-permute-start.4 = (f32[2,8,16,128]{3,2,1,0:T(8,128)}, f32[2,8,16,128]{3,2,1,0:T(8,128)S(1)}, u32[]{:S(2)}, u32[]{:S(2)}) collective-permute-start(f32[2,8,16,128]{3,2,1,0:T(8,128)} %get-tuple-element.40.own), channel_id=1, source_target_pairs={{0,16},{8,24},{16,0},{24,8},{1,17},{9,25},{17,1},{25,9},{2,18},{10... | collective-permute-start | bytes 393224 | tf_op jit(solution)/shard_map/ppermute | solution.py:482
  10.2 0.8 copy.9
  11.7 1.5 %collective-permute-start.8 = (f32[2,4,16,128]{3,2,1,0:T(8,128)S(1)}, f32[2,4,16,128]{3,2,1,0:T(8,128)S(1)}, u32[]{:S(2)}, u32[]{:S(2)}) collective-permute-start(f32[2,4,16,128]{3,2,1,0:T(8,128)S(1)} %collective-permute-done.6.refs_4_), channel_id=1, source_target_pairs={{0,16},{8,24},{16,0},{24,8},{1,17},{9,25},{17,1},{25,9},{2,18},{10... | collective-permute-start | bytes 196616 | tf_op jit(solution)/shard_map/ppermute | solution.py:482
  13.2 0.9 copy-done
  17.2 0.9 collective-permute-done.9.refs_7_
  18.1 13.2 %setup.1 = (f32[1,64,264,128]{3,2,1,0:T(8,128)S(1)}, f32[1,88,264,128]{3,2,1,0:T(8,128)S(1)}, f32[64,16,128]{2,1,0:T(8,128)S(1)}) custom-call(bf16[256,96]{1,0:T(8,128)(2,1)S(1)} %concatenate.4.outer, f32[16,128]{1,0:T(8,128)S(1)} %get-tuple-element.46.prior_rows.refs_0_, f32[2,8,16,128]{3,2,1,0:T(8,128)S(1)} %get-tuple-element.47.refs_0_, ...), custom_call_target="tpu_custom_call" | custom-call | tf_op jit(solution)/shard_map/setup/pallas_call | solution.py:530
  31.3 6.7 %iterate_0.1 = (f32[64,16,128]{2,1,0:T(8,128)S(1)}, f32[64,16,128]{2,1,0:T(8,128)S(1)}, f32[16,16,128]{2,1,0:T(8,128)S(1)}, f32[16,16,128]{2,1,0:T(8,128)S(1)}) custom-call(f32[16,128]{1,0:T(8,128)S(1)} %get-tuple-element.46.prior_rows.refs_0_, f32[1,64,264,128]{3,2,1,0:T(8,128)S(1)} %get-tuple-element.51.refs_1_, ...), custom_call_target="tpu_custom_call" | custom-call | tf_op jit(solution)/shard_map/iterate_0/pallas_call | solution.py:552
  38.0 1.7 %collective-permute-start.11 = (f32[16,16,128]{2,1,0:T(8,128)S(1)}, f32[16,16,128]{2,1,0:T(8,128)S(1)}, u32[]{:S(2)}, u32[]{:S(2)}) collective-permute-start(f32[16,16,128]{2,1,0:T(8,128)S(1)} %get-tuple-element.54), channel_id=1, source_target_pairs={{0,1},{1,0},{2,3},{3,2},{4,5},{5,4},{6,7},{7,6},{8,9},{9,8},{10,11... | collective-permute-start | bytes 393224 | tf_op jit(solution)/shard_map/ppermute | solution.py:563
  39.6 0.8 collective-permute-start.12
  40.5 3.1 %collective-permute-done.11.refs_4_ = f32[16,16,128]{2,1,0:T(8,128)S(1)} collective-permute-done((f32[16,16,128]{2,1,0:T(8,128)S(1)}, f32[16,16,128]{2,1,0:T(8,128)S(1)}, u32[]{:S(2)}, u32[]{:S(2)}) %collective-permute-start.11) | collective-permute-done | bytes 131104 | tf_op jit(solution)/shard_map/ppermute | solution.py:563
  43.6 6.7 %iterate_1.1 = (f32[64,16,128]{2,1,0:T(8,128)S(1)}, f32[64,16,128]{2,1,0:T(8,128)S(1)}, f32[16,16,128]{2,1,0:T(8,128)S(1)}, f32[16,16,128]{2,1,0:T(8,128)S(1)}, f32[64,16,128]{2,1,0:T(8,128)S(1)}) custom-call(f32[16,128]{1,0:T(8,128)S(1)} %get-tuple-element.46.prior_rows.refs_0_, f32[1,64,264,128]{3,2,1,0:T(8,128)S(1)} %get-tuple-element.51.refs_1_, ...), custom_call_target="tpu_custom_call" | custom-call | tf_op jit(solution)/shard_map/iterate_1/pallas_call | solution.py:552
  50.3 4.6 %collective-permute-start.13 = (f32[16,16,128]{2,1,0:T(8,128)S(1)}, f32[16,16,128]{2,1,0:T(8,128)S(1)}, u32[]{:S(2)}, u32[]{:S(2)}) collective-permute-start(f32[16,16,128]{2,1,0:T(8,128)S(1)} %get-tuple-element.58), channel_id=1, source_target_pairs={{0,1},{1,0},{2,3},{3,2},{4,5},{5,4},{6,7},{7,6},{8,9},{9,8},{10,11... | collective-permute-start | bytes 393224 | tf_op jit(solution)/shard_map/ppermute | solution.py:563
  54.9 0.7 collective-permute-start.14
  55.5 3.3 %collective-permute-done.13.refs_4_ = f32[16,16,128]{2,1,0:T(8,128)S(1)} collective-permute-done((f32[16,16,128]{2,1,0:T(8,128)S(1)}, f32[16,16,128]{2,1,0:T(8,128)S(1)}, u32[]{:S(2)}, u32[]{:S(2)}) %collective-permute-start.13) | collective-permute-done | bytes 131104 | tf_op jit(solution)/shard_map/ppermute | solution.py:563
  58.8 7.0 %iterate_2.1 = (f32[64,16,128]{2,1,0:T(8,128)S(1)}, f32[64,16,128]{2,1,0:T(8,128)S(1)}, f32[16,16,128]{2,1,0:T(8,128)S(1)}, f32[16,16,128]{2,1,0:T(8,128)S(1)}, f32[64,16,128]{2,1,0:T(8,128)S(1)}) custom-call(f32[16,128]{1,0:T(8,128)S(1)} %get-tuple-element.46.prior_rows.refs_0_, f32[1,64,264,128]{3,2,1,0:T(8,128)S(1)} %get-tuple-element.51.refs_1_, ...), custom_call_target="tpu_custom_call" | custom-call | tf_op jit(solution)/shard_map/iterate_2/pallas_call | solution.py:552
  65.8 4.1 %collective-permute-start.15 = (f32[16,16,128]{2,1,0:T(8,128)S(1)}, f32[16,16,128]{2,1,0:T(8,128)S(1)}, u32[]{:S(2)}, u32[]{:S(2)}) collective-permute-start(f32[16,16,128]{2,1,0:T(8,128)S(1)} %get-tuple-element.62), channel_id=1, source_target_pairs={{0,1},{1,0},{2,3},{3,2},{4,5},{5,4},{6,7},{7,6},{8,9},{9,8},{10,11... | collective-permute-start | bytes 393224 | tf_op jit(solution)/shard_map/ppermute | solution.py:563
  69.9 0.9 collective-permute-start.16
  70.8 0.7 side_1.1
  72.0 1.8 %collective-permute-done.15.refs_4_ = f32[16,16,128]{2,1,0:T(8,128)S(1)} collective-permute-done((f32[16,16,128]{2,1,0:T(8,128)S(1)}, f32[16,16,128]{2,1,0:T(8,128)S(1)}, u32[]{:S(2)}, u32[]{:S(2)}) %collective-permute-start.15) | collective-permute-done | bytes 131104 | tf_op jit(solution)/shard_map/ppermute | solution.py:563
  73.8 7.2 %iterate_3.1 = (f32[8,16,128]{2,1,0:T(8,128)S(1)}, f32[16,8,128]{2,1,0:T(8,128)S(1)}) custom-call(f32[16,128]{1,0:T(8,128)S(1)} %get-tuple-element.46.prior_rows.refs_0_, f32[1,64,264,128]{3,2,1,0:T(8,128)S(1)} %get-tuple-element.51.refs_1_, f32[1,88,264,128]{3,2,1,0:T(8,128)S(1)} %get-tuple-element.52.refs_2_, ...), custom_call_target="tpu_custom_call" | custom-call | tf_op jit(solution)/shard_map/iterate_3/pallas_call | solution.py:552
  81.0 15.8 %all_to_all.5.sums = f32[8,16,128]{2,1,0:T(8,128)S(1)} all-to-all(f32[8,16,128]{2,1,0:T(8,128)S(1)} %get-tuple-element.70), channel_id=1, replica_groups=mesh['gx'=4,'gy'=8] {'gy'}, dimensions={0} | all-to-all | bytes 131072 | tf_op jit(solution)/shard_map/all_to_all | solution.py:566
  96.8 0.8 finish.1
  (29 shorter events, 5.0 us)
Async XLA Ops:
  2.2 8.7 %collective-permute-start = (f32[2,4,16,128]{3,2,1,0:T(8,128)}, f32[2,4,16,128]{3,2,1,0:T(8,128)S(1)}, u32[]{:S(2)}, u32[]{:S(2)}) collective-permute-start(f32[2,4,16,128]{3,2,1,0:T(8,128)} %get-tuple-element.43), channel_id=1, source_target_pairs={{1,2},{2,1},{3,4},{4,3},{5,6},{6,5},{9,10},{10,9},{11,12},{12,11},... | collective-permute-start | bytes 196616 | tf_op jit(solution)/shard_map/ppermute | solution.py:517
  2.8 8.8 %collective-permute-start.6 = (f32[2,4,16,128]{3,2,1,0:T(8,128)}, f32[2,4,16,128]{3,2,1,0:T(8,128)S(1)}, u32[]{:S(2)}, u32[]{:S(2)}) collective-permute-start(f32[2,4,16,128]{3,2,1,0:T(8,128)} %get-tuple-element.48), channel_id=1, source_target_pairs={{0,1},{1,0},{2,3},{3,2},{4,5},{5,4},{6,7},{7,6},{8,9},{9,8},{10,11... | collective-permute-start | bytes 196616 | tf_op jit(solution)/shard_map/ppermute | solution.py:516
  8.6 7.7 %collective-permute-start.4 = (f32[2,8,16,128]{3,2,1,0:T(8,128)}, f32[2,8,16,128]{3,2,1,0:T(8,128)S(1)}, u32[]{:S(2)}, u32[]{:S(2)}) collective-permute-start(f32[2,8,16,128]{3,2,1,0:T(8,128)} %get-tuple-element.40.own), channel_id=1, source_target_pairs={{0,16},{8,24},{16,0},{24,8},{1,17},{9,25},{17,1},{25,9},{2,18},{10... | collective-permute-start | bytes 393224 | tf_op jit(solution)/shard_map/ppermute | solution.py:482
  10.2 6.9 %collective-permute-start.3 = (f32[2,8,16,128]{3,2,1,0:T(8,128)}, f32[2,8,16,128]{3,2,1,0:T(8,128)S(1)}, u32[]{:S(2)}, u32[]{:S(2)}) collective-permute-start(f32[2,8,16,128]{3,2,1,0:T(8,128)} %get-tuple-element.40.own), channel_id=1, source_target_pairs={{0,8},{8,0},{16,24},{24,16},{1,9},{9,1},{17,25},{25,17},{2,10},{10... | collective-permute-start | bytes 393224 | tf_op jit(solution)/shard_map/ppermute | solution.py:482
  10.9 4.9 %collective-permute-start.1 = (f32[2,4,16,128]{3,2,1,0:T(8,128)S(1)}, f32[2,4,16,128]{3,2,1,0:T(8,128)S(1)}, u32[]{:S(2)}, u32[]{:S(2)}) collective-permute-start(f32[2,4,16,128]{3,2,1,0:T(8,128)S(1)} %collective-permute-done.refs_8_), channel_id=1, source_target_pairs={{0,16},{8,24},{16,0},{24,8},{1,17},{9,25},{17,1},{25,9},{2,18},{10... | collective-permute-start | bytes 196616 | tf_op jit(solution)/shard_map/ppermute | solution.py:482
  11.4 4.4 %collective-permute-start.2 = (f32[2,4,16,128]{3,2,1,0:T(8,128)S(1)}, f32[2,4,16,128]{3,2,1,0:T(8,128)S(1)}, u32[]{:S(2)}, u32[]{:S(2)}) collective-permute-start(f32[2,4,16,128]{3,2,1,0:T(8,128)S(1)} %collective-permute-done.refs_8_), channel_id=1, source_target_pairs={{0,8},{8,0},{16,24},{24,16},{1,9},{9,1},{17,25},{25,17},{2,10},{10... | collective-permute-start | bytes 196616 | tf_op jit(solution)/shard_map/ppermute | solution.py:482
  11.7 5.2 %collective-permute-start.8 = (f32[2,4,16,128]{3,2,1,0:T(8,128)S(1)}, f32[2,4,16,128]{3,2,1,0:T(8,128)S(1)}, u32[]{:S(2)}, u32[]{:S(2)}) collective-permute-start(f32[2,4,16,128]{3,2,1,0:T(8,128)S(1)} %collective-permute-done.6.refs_4_), channel_id=1, source_target_pairs={{0,16},{8,24},{16,0},{24,8},{1,17},{9,25},{17,1},{25,9},{2,18},{10... | collective-permute-start | bytes 196616 | tf_op jit(solution)/shard_map/ppermute | solution.py:482
  13.2 0.9 copy-start
  14.1 0.7 copy-start.1
  15.8 1.3 %collective-permute-start.7 = (f32[2,4,16,128]{3,2,1,0:T(8,128)S(1)}, f32[2,4,16,128]{3,2,1,0:T(8,128)S(1)}, u32[]{:S(2)}, u32[]{:S(2)}) collective-permute-start(f32[2,4,16,128]{3,2,1,0:T(8,128)S(1)} %collective-permute-done.6.refs_4_), channel_id=1, source_target_pairs={{0,8},{8,0},{16,24},{24,16},{1,9},{9,1},{17,25},{25,17},{2,10},{10... | collective-permute-start | bytes 196616 | tf_op jit(solution)/shard_map/ppermute | solution.py:482
  15.8 1.4 %collective-permute-start.10 = (f32[2,4,16,128]{3,2,1,0:T(8,128)S(1)}, f32[2,4,16,128]{3,2,1,0:T(8,128)S(1)}, u32[]{:S(2)}, u32[]{:S(2)}) collective-permute-start(f32[2,4,16,128]{3,2,1,0:T(8,128)S(1)} %collective-permute-done.1.refs_10_), channel_id=1, source_target_pairs={{0,8},{8,0},{16,24},{24,16},{1,9},{9,1},{17,25},{25,17},{2,10},{10... | collective-permute-start | bytes 196616 | tf_op jit(solution)/shard_map/ppermute | solution.py:482
  16.3 1.8 %collective-permute-start.5 = (f32[2,8,16,128]{3,2,1,0:T(8,128)S(1)}, f32[2,8,16,128]{3,2,1,0:T(8,128)S(1)}, u32[]{:S(2)}, u32[]{:S(2)}) collective-permute-start(f32[2,8,16,128]{3,2,1,0:T(8,128)S(1)} %collective-permute-done.4.refs_2_), channel_id=1, source_target_pairs={{0,8},{8,0},{16,24},{24,16},{1,9},{9,1},{17,25},{25,17},{2,10},{10... | collective-permute-start | bytes 393224 | tf_op jit(solution)/shard_map/ppermute | solution.py:482
  16.8 1.3 %collective-permute-start.9 = (f32[2,4,16,128]{3,2,1,0:T(8,128)S(1)}, f32[2,4,16,128]{3,2,1,0:T(8,128)S(1)}, u32[]{:S(2)}, u32[]{:S(2)}) collective-permute-start(f32[2,4,16,128]{3,2,1,0:T(8,128)S(1)} %collective-permute-done.8.refs_6_), channel_id=1, source_target_pairs={{0,8},{8,0},{16,24},{24,16},{1,9},{9,1},{17,25},{25,17},{2,10},{10... | collective-permute-start | bytes 196616 | tf_op jit(solution)/shard_map/ppermute | solution.py:482
  38.0 5.6 %collective-permute-start.11 = (f32[16,16,128]{2,1,0:T(8,128)S(1)}, f32[16,16,128]{2,1,0:T(8,128)S(1)}, u32[]{:S(2)}, u32[]{:S(2)}) collective-permute-start(f32[16,16,128]{2,1,0:T(8,128)S(1)} %get-tuple-element.54), channel_id=1, source_target_pairs={{0,1},{1,0},{2,3},{3,2},{4,5},{5,4},{6,7},{7,6},{8,9},{9,8},{10,11... | collective-permute-start | bytes 393224 | tf_op jit(solution)/shard_map/ppermute | solution.py:563
  39.6 3.9 %collective-permute-start.12 = (f32[16,16,128]{2,1,0:T(8,128)S(1)}, f32[16,16,128]{2,1,0:T(8,128)S(1)}, u32[]{:S(2)}, u32[]{:S(2)}) collective-permute-start(f32[16,16,128]{2,1,0:T(8,128)S(1)} %get-tuple-element.55), channel_id=1, source_target_pairs={{1,2},{2,1},{3,4},{4,3},{5,6},{6,5},{9,10},{10,9},{11,12},{12,11},... | collective-permute-start | bytes 393224 | tf_op jit(solution)/shard_map/ppermute | solution.py:563
  50.3 8.5 %collective-permute-start.13 = (f32[16,16,128]{2,1,0:T(8,128)S(1)}, f32[16,16,128]{2,1,0:T(8,128)S(1)}, u32[]{:S(2)}, u32[]{:S(2)}) collective-permute-start(f32[16,16,128]{2,1,0:T(8,128)S(1)} %get-tuple-element.58), channel_id=1, source_target_pairs={{0,1},{1,0},{2,3},{3,2},{4,5},{5,4},{6,7},{7,6},{8,9},{9,8},{10,11... | collective-permute-start | bytes 393224 | tf_op jit(solution)/shard_map/ppermute | solution.py:563
  54.9 3.9 %collective-permute-start.14 = (f32[16,16,128]{2,1,0:T(8,128)S(1)}, f32[16,16,128]{2,1,0:T(8,128)S(1)}, u32[]{:S(2)}, u32[]{:S(2)}) collective-permute-start(f32[16,16,128]{2,1,0:T(8,128)S(1)} %get-tuple-element.59), channel_id=1, source_target_pairs={{1,2},{2,1},{3,4},{4,3},{5,6},{6,5},{9,10},{10,9},{11,12},{12,11},... | collective-permute-start | bytes 393224 | tf_op jit(solution)/shard_map/ppermute | solution.py:563
  65.8 8.1 %collective-permute-start.15 = (f32[16,16,128]{2,1,0:T(8,128)S(1)}, f32[16,16,128]{2,1,0:T(8,128)S(1)}, u32[]{:S(2)}, u32[]{:S(2)}) collective-permute-start(f32[16,16,128]{2,1,0:T(8,128)S(1)} %get-tuple-element.62), channel_id=1, source_target_pairs={{0,1},{1,0},{2,3},{3,2},{4,5},{5,4},{6,7},{7,6},{8,9},{9,8},{10,11... | collective-permute-start | bytes 393224 | tf_op jit(solution)/shard_map/ppermute | solution.py:563
  69.9 3.9 %collective-permute-start.16 = (f32[16,16,128]{2,1,0:T(8,128)S(1)}, f32[16,16,128]{2,1,0:T(8,128)S(1)}, u32[]{:S(2)}, u32[]{:S(2)}) collective-permute-start(f32[16,16,128]{2,1,0:T(8,128)S(1)} %get-tuple-element.63), channel_id=1, source_target_pairs={{1,2},{2,1},{3,4},{4,3},{5,6},{6,5},{9,10},{10,9},{11,12},{12,11},... | collective-permute-start | bytes 393224 | tf_op jit(solution)/shard_map/ppermute | solution.py:563

commit v6 on v5

--- a/solution.py
+++ b/solution.py
@@ -560,7 +560,7 @@
         )(prior_rows, blocks, inverse, *operands)
 
     def exchange(edge_a, edge_b):
-        return lax.ppermute(edge_a, "gy", pairs), lax.ppermute(edge_b, "gy", others)
+        return lax.ppermute(edge_a, "gy", pairs), lax.ppermute(edge_b, "gy", others + [(0, cols - 1), (cols - 1, 0)])
 
     def total(parts):
         return lax.all_to_all(parts, "gy", 0, 0, tiled=True)

time: 97.9 us -> 97.5 us (level)
  blocking collectives: 15.8 us -> 11.5 us
  waiting for transfers between devices: 10.1 us -> 13.3 us
    ppermute x3, starting transfers between devices: 2.37 us -> 10.7 us  [exchange(): lax.ppermute(edge_b, 'gy', others + [(0, cols - 1), (cols - 1, 0)])]
    ppermute x3, starting transfers between devices: 10.4 us -> 2.33 us  [exchange(): lax.ppermute(edge_a, 'gy', pairs)]
    ppermute x3, waiting for transfers between devices: 0.01 us -> 5.37 us  [exchange(): lax.ppermute(edge_b, 'gy', others + [(0, cols - 1), (cols - 1, 0)])]
    all_to_all x1, blocking collectives: 15.8 us -> 11.5 us  [total(): return lax.all_to_all(parts, 'gy', 0, 0, tiled=True)]
    ppermute x3, waiting for transfers between devices: 8.13 us -> 5.98 us  [exchange(): lax.ppermute(edge_a, 'gy', pairs)]
  transfers between devices with their start and end apart: 17 -> 17, of which waited for: 7 -> 10; matrix products, arithmetic and copies ran while one was open for 1% -> 1% of each run, Pallas kernels for 2% -> 2%
where the time goes in v6:
time: 97.5 us; the launch traced here: 97.2 us
  Pallas kernels  45.9 us (47%)
  starting transfers between devices  23.9 us (25%)
  waiting for transfers between devices  13.3 us (14%)
  blocking collectives  11.5 us (12%)
  local copies, waits for them, and re-layouts  2.5 us (3%)
    pallas_call x4, Pallas kernels, iterate(): pl.pallas_call(functools.partial(iterate_kernel, step), out_shape=shapes,...  27.7 us
    pallas_call x1, Pallas kernels, local(): pl.pallas_call(setup_kernel, out_shape=[shape(width // 128, n, ROWS, 128)...  13.3 us
    all_to_all x1, blocking collectives, total(): return lax.all_to_all(parts, 'gy', 0, 0, tiled=True)  11.5 us
    ppermute x3, starting transfers between devices, exchange(): lax.ppermute(edge_b, 'gy', others + [(0, cols - 1), (cols - 1, 0)])  10.7 us
    ppermute x3, waiting for transfers between devices, exchange(): lax.ppermute(edge_a, 'gy', pairs)  5.98 us
    ppermute x1, starting transfers between devices, local(): edge_a = lax.ppermute(edge_a, 'gy', pairs)  5.8 us
    ppermute x3, waiting for transfers between devices, exchange(): lax.ppermute(edge_b, 'gy', others + [(0, cols - 1), (cols - 1, 0)])  5.37 us
    ppermute x9, starting transfers between devices, gather(): held[o ^ bit] = lax.ppermute(held[o], 'gx', pairs)  4.37 us
  transfers between devices with their start and end apart: 17, of which 10 were waited for; matrix products, arithmetic and copies ran while one was open for 1% of the time, Pallas kernels for 2%

profile of v6, /device:TPU:0, one launch (start us, length us, event | category | flops | bytes accessed | tf_op | source)
XLA Modules:
  0.0 97.2 jit_solution(10488739782060145677)
XLA Ops:
  0.0 2.2 %prepare.1 = (f32[2,8,16,128]{3,2,1,0:T(8,128)}, f32[2,4,16,128]{3,2,1,0:T(8,128)}, f32[2,4,16,128]{3,2,1,0:T(8,128)}) custom-call(f32[16,16]{1,0:T(8,128)} %design.1, f32[16,8,128]{2,1,0:T(8,128)} %beta.1, s32[16,8,128]{2,1,0:T(8,128)} %kept.1, s32[16,8,128]{2,1,0:T(8,128)} %removed.1, s32[16,8,128]{2,1,0:T(8,128)} %labels.1), custom_call_target="tpu_custom_call" | custom-call | tf_op jit(solution)/shard_map/prepare/pallas_call | solution.py:500
  2.8 5.8 %collective-permute-start.6 = (f32[2,4,16,128]{3,2,1,0:T(8,128)}, f32[2,4,16,128]{3,2,1,0:T(8,128)S(1)}, u32[]{:S(2)}, u32[]{:S(2)}) collective-permute-start(f32[2,4,16,128]{3,2,1,0:T(8,128)} %get-tuple-element.48), channel_id=1, source_target_pairs={{0,1},{1,0},{2,3},{3,2},{4,5},{5,4},{6,7},{7,6},{8,9},{9,8},{10,11... | collective-permute-start | bytes 196616 | tf_op jit(solution)/shard_map/ppermute | solution.py:516
  8.6 1.5 %collective-permute-start.4 = (f32[2,8,16,128]{3,2,1,0:T(8,128)}, f32[2,8,16,128]{3,2,1,0:T(8,128)S(1)}, u32[]{:S(2)}, u32[]{:S(2)}) collective-permute-start(f32[2,8,16,128]{3,2,1,0:T(8,128)} %get-tuple-element.40.own), channel_id=1, source_target_pairs={{0,16},{8,24},{16,0},{24,8},{1,17},{9,25},{17,1},{25,9},{2,18},{10... | collective-permute-start | bytes 393224 | tf_op jit(solution)/shard_map/ppermute | solution.py:482
  10.2 0.8 copy.9
  11.7 1.5 %collective-permute-start.8 = (f32[2,4,16,128]{3,2,1,0:T(8,128)S(1)}, f32[2,4,16,128]{3,2,1,0:T(8,128)S(1)}, u32[]{:S(2)}, u32[]{:S(2)}) collective-permute-start(f32[2,4,16,128]{3,2,1,0:T(8,128)S(1)} %collective-permute-done.6.refs_4_), channel_id=1, source_target_pairs={{0,16},{8,24},{16,0},{24,8},{1,17},{9,25},{17,1},{25,9},{2,18},{10... | collective-permute-start | bytes 196616 | tf_op jit(solution)/shard_map/ppermute | solution.py:482
  13.2 0.9 copy-done
  17.2 0.9 collective-permute-done.9.refs_7_
  18.1 13.3 %setup.1 = (f32[1,64,264,128]{3,2,1,0:T(8,128)S(1)}, f32[1,88,264,128]{3,2,1,0:T(8,128)S(1)}, f32[64,16,128]{2,1,0:T(8,128)S(1)}) custom-call(bf16[256,96]{1,0:T(8,128)(2,1)S(1)} %concatenate.4.outer, f32[16,128]{1,0:T(8,128)S(1)} %get-tuple-element.46.prior_rows.refs_0_, f32[2,8,16,128]{3,2,1,0:T(8,128)S(1)} %get-tuple-element.47.refs_0_, ...), custom_call_target="tpu_custom_call" | custom-call | tf_op jit(solution)/shard_map/setup/pallas_call | solution.py:530
  31.4 6.7 %iterate_0.1 = (f32[64,16,128]{2,1,0:T(8,128)S(1)}, f32[64,16,128]{2,1,0:T(8,128)S(1)}, f32[16,16,128]{2,1,0:T(8,128)S(1)}, f32[16,16,128]{2,1,0:T(8,128)S(1)}) custom-call(f32[16,128]{1,0:T(8,128)S(1)} %get-tuple-element.46.prior_rows.refs_0_, f32[1,64,264,128]{3,2,1,0:T(8,128)S(1)} %get-tuple-element.51.refs_1_, ...), custom_call_target="tpu_custom_call" | custom-call | tf_op jit(solution)/shard_map/iterate_0/pallas_call | solution.py:552
  38.1 1.7 %collective-permute-start.11 = (f32[16,16,128]{2,1,0:T(8,128)S(1)}, f32[16,16,128]{2,1,0:T(8,128)S(1)}, u32[]{:S(2)}, u32[]{:S(2)}) collective-permute-start(f32[16,16,128]{2,1,0:T(8,128)S(1)} %get-tuple-element.54), channel_id=1, source_target_pairs={{0,1},{1,0},{2,3},{3,2},{4,5},{5,4},{6,7},{7,6},{8,9},{9,8},{10,11... | collective-permute-start | bytes 393224 | tf_op jit(solution)/shard_map/ppermute | solution.py:563
  39.8 3.6 %collective-permute-start.12 = (f32[16,16,128]{2,1,0:T(8,128)S(1)}, f32[16,16,128]{2,1,0:T(8,128)S(1)}, u32[]{:S(2)}, u32[]{:S(2)}) collective-permute-start(f32[16,16,128]{2,1,0:T(8,128)S(1)} %get-tuple-element.55), channel_id=1, source_target_pairs={{1,2},{2,1},{3,4},{4,3},{5,6},{6,5},{0,7},{7,0},{9,10},{10,9},{11,... | collective-permute-start | bytes 393224 | tf_op jit(solution)/shard_map/ppermute | solution.py:563
  43.4 2.3 %collective-permute-done.11.refs_4_ = f32[16,16,128]{2,1,0:T(8,128)S(1)} collective-permute-done((f32[16,16,128]{2,1,0:T(8,128)S(1)}, f32[16,16,128]{2,1,0:T(8,128)S(1)}, u32[]{:S(2)}, u32[]{:S(2)}) %collective-permute-start.11) | collective-permute-done | bytes 131104 | tf_op jit(solution)/shard_map/ppermute | solution.py:563
  45.7 2.1 %collective-permute-done.12.refs_5_ = f32[16,16,128]{2,1,0:T(8,128)S(1)} collective-permute-done((f32[16,16,128]{2,1,0:T(8,128)S(1)}, f32[16,16,128]{2,1,0:T(8,128)S(1)}, u32[]{:S(2)}, u32[]{:S(2)}) %collective-permute-start.12) | collective-permute-done | bytes 131104 | tf_op jit(solution)/shard_map/ppermute | solution.py:563
  47.8 6.7 %iterate_1.1 = (f32[64,16,128]{2,1,0:T(8,128)S(1)}, f32[64,16,128]{2,1,0:T(8,128)S(1)}, f32[16,16,128]{2,1,0:T(8,128)S(1)}, f32[16,16,128]{2,1,0:T(8,128)S(1)}, f32[64,16,128]{2,1,0:T(8,128)S(1)}) custom-call(f32[16,128]{1,0:T(8,128)S(1)} %get-tuple-element.46.prior_rows.refs_0_, f32[1,64,264,128]{3,2,1,0:T(8,128)S(1)} %get-tuple-element.51.refs_1_, ...), custom_call_target="tpu_custom_call" | custom-call | tf_op jit(solution)/shard_map/iterate_1/pallas_call | solution.py:552
  54.9 3.6 %collective-permute-start.14 = (f32[16,16,128]{2,1,0:T(8,128)S(1)}, f32[16,16,128]{2,1,0:T(8,128)S(1)}, u32[]{:S(2)}, u32[]{:S(2)}) collective-permute-start(f32[16,16,128]{2,1,0:T(8,128)S(1)} %get-tuple-element.59), channel_id=1, source_target_pairs={{1,2},{2,1},{3,4},{4,3},{5,6},{6,5},{0,7},{7,0},{9,10},{10,9},{11,... | collective-permute-start | bytes 393224 | tf_op jit(solution)/shard_map/ppermute | solution.py:563
  58.5 2.4 %collective-permute-done.13.refs_4_ = f32[16,16,128]{2,1,0:T(8,128)S(1)} collective-permute-done((f32[16,16,128]{2,1,0:T(8,128)S(1)}, f32[16,16,128]{2,1,0:T(8,128)S(1)}, u32[]{:S(2)}, u32[]{:S(2)}) %collective-permute-start.13) | collective-permute-done | bytes 131104 | tf_op jit(solution)/shard_map/ppermute | solution.py:563
  60.9 1.7 %collective-permute-done.14.refs_5_ = f32[16,16,128]{2,1,0:T(8,128)S(1)} collective-permute-done((f32[16,16,128]{2,1,0:T(8,128)S(1)}, f32[16,16,128]{2,1,0:T(8,128)S(1)}, u32[]{:S(2)}, u32[]{:S(2)}) %collective-permute-start.14) | collective-permute-done | bytes 131104 | tf_op jit(solution)/shard_map/ppermute | solution.py:563
  62.6 7.2 %iterate_2.1 = (f32[64,16,128]{2,1,0:T(8,128)S(1)}, f32[64,16,128]{2,1,0:T(8,128)S(1)}, f32[16,16,128]{2,1,0:T(8,128)S(1)}, f32[16,16,128]{2,1,0:T(8,128)S(1)}, f32[64,16,128]{2,1,0:T(8,128)S(1)}) custom-call(f32[16,128]{1,0:T(8,128)S(1)} %get-tuple-element.46.prior_rows.refs_0_, f32[1,64,264,128]{3,2,1,0:T(8,128)S(1)} %get-tuple-element.51.refs_1_, ...), custom_call_target="tpu_custom_call" | custom-call | tf_op jit(solution)/shard_map/iterate_2/pallas_call | solution.py:552
  70.0 3.6 %collective-permute-start.16 = (f32[16,16,128]{2,1,0:T(8,128)S(1)}, f32[16,16,128]{2,1,0:T(8,128)S(1)}, u32[]{:S(2)}, u32[]{:S(2)}) collective-permute-start(f32[16,16,128]{2,1,0:T(8,128)S(1)} %get-tuple-element.63), channel_id=1, source_target_pairs={{1,2},{2,1},{3,4},{4,3},{5,6},{6,5},{0,7},{7,0},{9,10},{10,9},{11,... | collective-permute-start | bytes 393224 | tf_op jit(solution)/shard_map/ppermute | solution.py:563
  74.8 1.3 %collective-permute-done.15.refs_4_ = f32[16,16,128]{2,1,0:T(8,128)S(1)} collective-permute-done((f32[16,16,128]{2,1,0:T(8,128)S(1)}, f32[16,16,128]{2,1,0:T(8,128)S(1)}, u32[]{:S(2)}, u32[]{:S(2)}) %collective-permute-start.15) | collective-permute-done | bytes 131104 | tf_op jit(solution)/shard_map/ppermute | solution.py:563
  76.0 1.6 %collective-permute-done.16.refs_5_ = f32[16,16,128]{2,1,0:T(8,128)S(1)} collective-permute-done((f32[16,16,128]{2,1,0:T(8,128)S(1)}, f32[16,16,128]{2,1,0:T(8,128)S(1)}, u32[]{:S(2)}, u32[]{:S(2)}) %collective-permute-start.16) | collective-permute-done | bytes 131104 | tf_op jit(solution)/shard_map/ppermute | solution.py:563
  77.6 7.2 %iterate_3.1 = (f32[8,16,128]{2,1,0:T(8,128)S(1)}, f32[16,8,128]{2,1,0:T(8,128)S(1)}) custom-call(f32[16,128]{1,0:T(8,128)S(1)} %get-tuple-element.46.prior_rows.refs_0_, f32[1,64,264,128]{3,2,1,0:T(8,128)S(1)} %get-tuple-element.51.refs_1_, f32[1,88,264,128]{3,2,1,0:T(8,128)S(1)} %get-tuple-element.52.refs_2_, ...), custom_call_target="tpu_custom_call" | custom-call | tf_op jit(solution)/shard_map/iterate_3/pallas_call | solution.py:552
  84.9 11.5 %all_to_all.5.sums = f32[8,16,128]{2,1,0:T(8,128)S(1)} all-to-all(f32[8,16,128]{2,1,0:T(8,128)S(1)} %get-tuple-element.70), channel_id=1, replica_groups=mesh['gx'=4,'gy'=8] {'gy'}, dimensions={0} | all-to-all | bytes 131072 | tf_op jit(solution)/shard_map/all_to_all | solution.py:566
  96.4 0.8 finish.1
  (29 shorter events, 6.4 us)
Async XLA Ops:
  2.2 8.7 %collective-permute-start = (f32[2,4,16,128]{3,2,1,0:T(8,128)}, f32[2,4,16,128]{3,2,1,0:T(8,128)S(1)}, u32[]{:S(2)}, u32[]{:S(2)}) collective-permute-start(f32[2,4,16,128]{3,2,1,0:T(8,128)} %get-tuple-element.43), channel_id=1, source_target_pairs={{1,2},{2,1},{3,4},{4,3},{5,6},{6,5},{9,10},{10,9},{11,12},{12,11},... | collective-permute-start | bytes 196616 | tf_op jit(solution)/shard_map/ppermute | solution.py:517
  2.8 8.8 %collective-permute-start.6 = (f32[2,4,16,128]{3,2,1,0:T(8,128)}, f32[2,4,16,128]{3,2,1,0:T(8,128)S(1)}, u32[]{:S(2)}, u32[]{:S(2)}) collective-permute-start(f32[2,4,16,128]{3,2,1,0:T(8,128)} %get-tuple-element.48), channel_id=1, source_target_pairs={{0,1},{1,0},{2,3},{3,2},{4,5},{5,4},{6,7},{7,6},{8,9},{9,8},{10,11... | collective-permute-start | bytes 196616 | tf_op jit(solution)/shard_map/ppermute | solution.py:516
  8.6 7.7 %collective-permute-start.4 = (f32[2,8,16,128]{3,2,1,0:T(8,128)}, f32[2,8,16,128]{3,2,1,0:T(8,128)S(1)}, u32[]{:S(2)}, u32[]{:S(2)}) collective-permute-start(f32[2,8,16,128]{3,2,1,0:T(8,128)} %get-tuple-element.40.own), channel_id=1, source_target_pairs={{0,16},{8,24},{16,0},{24,8},{1,17},{9,25},{17,1},{25,9},{2,18},{10... | collective-permute-start | bytes 393224 | tf_op jit(solution)/shard_map/ppermute | solution.py:482
  10.2 6.9 %collective-permute-start.3 = (f32[2,8,16,128]{3,2,1,0:T(8,128)}, f32[2,8,16,128]{3,2,1,0:T(8,128)S(1)}, u32[]{:S(2)}, u32[]{:S(2)}) collective-permute-start(f32[2,8,16,128]{3,2,1,0:T(8,128)} %get-tuple-element.40.own), channel_id=1, source_target_pairs={{0,8},{8,0},{16,24},{24,16},{1,9},{9,1},{17,25},{25,17},{2,10},{10... | collective-permute-start | bytes 393224 | tf_op jit(solution)/shard_map/ppermute | solution.py:482
  10.9 4.9 %collective-permute-start.1 = (f32[2,4,16,128]{3,2,1,0:T(8,128)S(1)}, f32[2,4,16,128]{3,2,1,0:T(8,128)S(1)}, u32[]{:S(2)}, u32[]{:S(2)}) collective-permute-start(f32[2,4,16,128]{3,2,1,0:T(8,128)S(1)} %collective-permute-done.refs_8_), channel_id=1, source_target_pairs={{0,16},{8,24},{16,0},{24,8},{1,17},{9,25},{17,1},{25,9},{2,18},{10... | collective-permute-start | bytes 196616 | tf_op jit(solution)/shard_map/ppermute | solution.py:482
  11.4 4.4 %collective-permute-start.2 = (f32[2,4,16,128]{3,2,1,0:T(8,128)S(1)}, f32[2,4,16,128]{3,2,1,0:T(8,128)S(1)}, u32[]{:S(2)}, u32[]{:S(2)}) collective-permute-start(f32[2,4,16,128]{3,2,1,0:T(8,128)S(1)} %collective-permute-done.refs_8_), channel_id=1, source_target_pairs={{0,8},{8,0},{16,24},{24,16},{1,9},{9,1},{17,25},{25,17},{2,10},{10... | collective-permute-start | bytes 196616 | tf_op jit(solution)/shard_map/ppermute | solution.py:482
  11.7 5.2 %collective-permute-start.8 = (f32[2,4,16,128]{3,2,1,0:T(8,128)S(1)}, f32[2,4,16,128]{3,2,1,0:T(8,128)S(1)}, u32[]{:S(2)}, u32[]{:S(2)}) collective-permute-start(f32[2,4,16,128]{3,2,1,0:T(8,128)S(1)} %collective-permute-done.6.refs_4_), channel_id=1, source_target_pairs={{0,16},{8,24},{16,0},{24,8},{1,17},{9,25},{17,1},{25,9},{2,18},{10... | collective-permute-start | bytes 196616 | tf_op jit(solution)/shard_map/ppermute | solution.py:482
  13.2 0.9 copy-start
  14.1 0.7 copy-start.1
  15.8 1.3 %collective-permute-start.7 = (f32[2,4,16,128]{3,2,1,0:T(8,128)S(1)}, f32[2,4,16,128]{3,2,1,0:T(8,128)S(1)}, u32[]{:S(2)}, u32[]{:S(2)}) collective-permute-start(f32[2,4,16,128]{3,2,1,0:T(8,128)S(1)} %collective-permute-done.6.refs_4_), channel_id=1, source_target_pairs={{0,8},{8,0},{16,24},{24,16},{1,9},{9,1},{17,25},{25,17},{2,10},{10... | collective-permute-start | bytes 196616 | tf_op jit(solution)/shard_map/ppermute | solution.py:482
  15.8 1.4 %collective-permute-start.10 = (f32[2,4,16,128]{3,2,1,0:T(8,128)S(1)}, f32[2,4,16,128]{3,2,1,0:T(8,128)S(1)}, u32[]{:S(2)}, u32[]{:S(2)}) collective-permute-start(f32[2,4,16,128]{3,2,1,0:T(8,128)S(1)} %collective-permute-done.1.refs_10_), channel_id=1, source_target_pairs={{0,8},{8,0},{16,24},{24,16},{1,9},{9,1},{17,25},{25,17},{2,10},{10... | collective-permute-start | bytes 196616 | tf_op jit(solution)/shard_map/ppermute | solution.py:482
  16.3 1.8 %collective-permute-start.5 = (f32[2,8,16,128]{3,2,1,0:T(8,128)S(1)}, f32[2,8,16,128]{3,2,1,0:T(8,128)S(1)}, u32[]{:S(2)}, u32[]{:S(2)}) collective-permute-start(f32[2,8,16,128]{3,2,1,0:T(8,128)S(1)} %collective-permute-done.4.refs_2_), channel_id=1, source_target_pairs={{0,8},{8,0},{16,24},{24,16},{1,9},{9,1},{17,25},{25,17},{2,10},{10... | collective-permute-start | bytes 393224 | tf_op jit(solution)/shard_map/ppermute | solution.py:482
  16.8 1.3 %collective-permute-start.9 = (f32[2,4,16,128]{3,2,1,0:T(8,128)S(1)}, f32[2,4,16,128]{3,2,1,0:T(8,128)S(1)}, u32[]{:S(2)}, u32[]{:S(2)}) collective-permute-start(f32[2,4,16,128]{3,2,1,0:T(8,128)S(1)} %collective-permute-done.8.refs_6_), channel_id=1, source_target_pairs={{0,8},{8,0},{16,24},{24,16},{1,9},{9,1},{17,25},{25,17},{2,10},{10... | collective-permute-start | bytes 196616 | tf_op jit(solution)/shard_map/ppermute | solution.py:482
  38.1 7.6 %collective-permute-start.11 = (f32[16,16,128]{2,1,0:T(8,128)S(1)}, f32[16,16,128]{2,1,0:T(8,128)S(1)}, u32[]{:S(2)}, u32[]{:S(2)}) collective-permute-start(f32[16,16,128]{2,1,0:T(8,128)S(1)} %get-tuple-element.54), channel_id=1, source_target_pairs={{0,1},{1,0},{2,3},{3,2},{4,5},{5,4},{6,7},{7,6},{8,9},{9,8},{10,11... | collective-permute-start | bytes 393224 | tf_op jit(solution)/shard_map/ppermute | solution.py:563
  39.8 8.0 %collective-permute-start.12 = (f32[16,16,128]{2,1,0:T(8,128)S(1)}, f32[16,16,128]{2,1,0:T(8,128)S(1)}, u32[]{:S(2)}, u32[]{:S(2)}) collective-permute-start(f32[16,16,128]{2,1,0:T(8,128)S(1)} %get-tuple-element.55), channel_id=1, source_target_pairs={{1,2},{2,1},{3,4},{4,3},{5,6},{6,5},{0,7},{7,0},{9,10},{10,9},{11,... | collective-permute-start | bytes 393224 | tf_op jit(solution)/shard_map/ppermute | solution.py:563
  54.5 6.4 %collective-permute-start.13 = (f32[16,16,128]{2,1,0:T(8,128)S(1)}, f32[16,16,128]{2,1,0:T(8,128)S(1)}, u32[]{:S(2)}, u32[]{:S(2)}) collective-permute-start(f32[16,16,128]{2,1,0:T(8,128)S(1)} %get-tuple-element.58), channel_id=1, source_target_pairs={{0,1},{1,0},{2,3},{3,2},{4,5},{5,4},{6,7},{7,6},{8,9},{9,8},{10,11... | collective-permute-start | bytes 393224 | tf_op jit(solution)/shard_map/ppermute | solution.py:563
  54.9 7.7 %collective-permute-start.14 = (f32[16,16,128]{2,1,0:T(8,128)S(1)}, f32[16,16,128]{2,1,0:T(8,128)S(1)}, u32[]{:S(2)}, u32[]{:S(2)}) collective-permute-start(f32[16,16,128]{2,1,0:T(8,128)S(1)} %get-tuple-element.59), channel_id=1, source_target_pairs={{1,2},{2,1},{3,4},{4,3},{5,6},{6,5},{0,7},{7,0},{9,10},{10,9},{11,... | collective-permute-start | bytes 393224 | tf_op jit(solution)/shard_map/ppermute | solution.py:563
  69.8 6.3 %collective-permute-start.15 = (f32[16,16,128]{2,1,0:T(8,128)S(1)}, f32[16,16,128]{2,1,0:T(8,128)S(1)}, u32[]{:S(2)}, u32[]{:S(2)}) collective-permute-start(f32[16,16,128]{2,1,0:T(8,128)S(1)} %get-tuple-element.62), channel_id=1, source_target_pairs={{0,1},{1,0},{2,3},{3,2},{4,5},{5,4},{6,7},{7,6},{8,9},{9,8},{10,11... | collective-permute-start | bytes 393224 | tf_op jit(solution)/shard_map/ppermute | solution.py:563
  70.0 7.7 %collective-permute-start.16 = (f32[16,16,128]{2,1,0:T(8,128)S(1)}, f32[16,16,128]{2,1,0:T(8,128)S(1)}, u32[]{:S(2)}, u32[]{:S(2)}) collective-permute-start(f32[16,16,128]{2,1,0:T(8,128)S(1)} %get-tuple-element.63), channel_id=1, source_target_pairs={{1,2},{2,1},{3,4},{4,3},{5,6},{6,5},{0,7},{7,0},{9,10},{10,9},{11,... | collective-permute-start | bytes 393224 | tf_op jit(solution)/shard_map/ppermute | solution.py:563
